TPU v7x, 32 devices: a whole 2x2x4 slice. The times are simulated.
32 devices in a mesh: rep: 8 (over y, x, core), grp: 4 (over z).
Axes of the slice: x: 2, y: 2, z: 4, core: 2. Of those that a mesh axis runs over, the one named last changes fastest.
Arguments:
- tokens: bfloat16 [8192, 576], P(('rep', 'grp')), may hold values from -40 to 40
- segments: int32 [8192], P(('rep', 'grp')), may hold values from 0 to 31, as said below
- out_grad: bfloat16 [8192, 576], P(('rep', 'grp')), may hold values from -6 to 6
- norm_gain: bfloat16 [576], P('grp'), may hold values from 0.25 to 1.75
- query_gain: bfloat16 [64], P('grp'), may hold values from 0.25 to 1.75
- key_gain: bfloat16 [64], P('grp'), may hold values from 0.25 to 1.75
- query_weight: bfloat16 [576, 576], P('grp'), may hold values from -0.25 to 0.25
- key_weight: bfloat16 [576, 192], P('grp'), may hold values from -0.25 to 0.25
- value_weight: bfloat16 [576, 192], P('grp'), may hold values from -0.25 to 0.25
- output_weight: bfloat16 [576, 576], P('grp'), may hold values from -2 to 2
- second_gain: bfloat16 [576], P('grp'), may hold values from 0.25 to 1.75
- gate_weight: bfloat16 [576, 1536], P('grp'), may hold values from -0.25 to 0.25
- up_weight: bfloat16 [576, 1536], P('grp'), may hold values from -0.25 to 0.25
- down_weight: bfloat16 [1536, 576], P('grp'), may hold values from -0.15625 to 0.15625
Outputs:
- layer_out: bfloat16 [8192, 576], P(('rep', 'grp'))
- token_grad: float32 [8192, 576], P(('rep', 'grp'))
- grad_norm_gain: float32 [576], P('grp')
- grad_query_gain: float32 [64], P('grp')
- grad_key_gain: float32 [64], P('grp')
- grad_query_weight: float32 [576, 576], P('grp')
- grad_key_weight: float32 [576, 192], P('grp')
- grad_value_weight: float32 [576, 192], P('grp')
- grad_output_weight: float32 [576, 576], P('grp')
- grad_second_gain: float32 [576], P('grp')
- grad_gate_weight: float32 [576, 1536], P('grp')
- grad_up_weight: float32 [576, 1536], P('grp')
- grad_down_weight: float32 [1536, 576], P('grp')
Inputs may be any that keep to these rules, and one draw needn't show every extreme that they name: `segments`: segment numbers never fall along the tokens. Each sequence s holds three or four documents of 60 to 800 tokens; its first document is numbered 4 * s and its last 4 * s + 3, those between take numbers between these. One of its documents begins within the sequence's first 256 tokens and ends within its last 256.
All inputs are finite; a program needn't handle non-finite values.
Results may differ from a plain program's by a relative error of at most 0.012.
The roundings to bfloat16 on the way count: a program that leaves them out, or rounds other values in their place, can miss the bound.
Values may be sent and summed in bfloat16 or wider, within the bound.
No kernel may reach another device: no remote copies, remote signals or barrier semaphores. Data moves between devices by JAX's collectives and lax.ppermute only.
A program may use at most 128 MiB of HBM per device.

v0:
```python
import functools

import jax
import jax.numpy as jnp
from jax import lax
from jax.experimental import pallas as pl
from jax.experimental.pallas import tpu as pltpu
from jax.sharding import PartitionSpec as P

NORM_EPS = 1e-05
ROPE_BASE = 100000.0
LANES = 128
SMALL = 16
MIB = 1024 * 1024
BIG = 58


def vmem():
    return pl.BlockSpec(memory_space=pltpu.VMEM)


def smem():
    return pl.BlockSpec(memory_space=pltpu.SMEM)


def hbm():
    return pl.BlockSpec(memory_space=pl.ANY)


def shape(dims, kind):
    return jax.ShapeDtypeStruct(dims, kind)


def options(mebibytes):
    return pltpu.CompilerParams(vmem_limit_bytes=mebibytes * MIB)


def cost():
    return pl.CostEstimate(flops=1, bytes_accessed=1024, transcendentals=0)


class Staged:
    def __init__(self, source, target, sem):
        self.copy = pltpu.make_async_copy(source, target, sem)
        self.copy.start()
        self.target, self.waiting = target, True
        self.shape, self.dtype = target.shape, target.dtype

    def wait(self):
        if self.waiting:
            self.copy.wait()
            self.waiting = False

    def __getitem__(self, index):
        self.wait()
        return self.target[index]


def staged_call(kernel, name, where, operands, held, out_shape, out_specs, scratch, mebibytes):
    count = len(operands)

    def whole(where_ref, *refs):
        sources, refs = refs[:count], refs[count:]
        targets, sems = refs[len(refs) - count - 1 : -1], refs[-1]
        rest = refs[: len(refs) - count - 1]
        staged = [
            Staged(source, target, sems.at[at])
            for at, (source, target) in enumerate(zip(sources, targets))
        ]
        kernel(where_ref, *staged, *rest)
        for operand in staged:
            operand.wait()

    return pl.pallas_call(
        whole,
        out_shape=out_shape,
        in_specs=[smem()] + [hbm()] * (count + len(held)),
        out_specs=out_specs,
        scratch_shapes=list(scratch)
        + [pltpu.VMEM(operand.shape, operand.dtype) for operand in operands]
        + [pltpu.SemaphoreType.DMA((count,))],
        compiler_params=options(mebibytes),
        cost_estimate=cost(),
        name=name,
    )(where, *operands, *held)


def hop(value, bit):
    count = lax.axis_size("rep")
    return lax.ppermute(value, "rep", [(i, i ^ bit) for i in range(count)])


def shift(value, step):
    count = lax.axis_size("grp")
    return lax.ppermute(value, "grp", [(i, (i + step) % count) for i in range(count)])


def rep_bits():
    index = lax.axis_index("rep")
    return index & 1, (index >> 1) & 1, (index >> 2) & 1


def hop_split(value, even, odd):
    count = lax.axis_size("rep")
    return lax.ppermute(value, "rep", [(i, i ^ (odd if i % 2 else even)) for i in range(count)])


def add_low(one, two):
    return (one.astype(jnp.float32) + two.astype(jnp.float32)).astype(one.dtype)


def fold_grp(parts):
    f32 = jnp.float32
    total = parts[0].astype(f32)
    for step in range(1, len(parts)):
        total = total + shift(parts[step], step).astype(f32)
    total = total.astype(parts[0].dtype)
    bit = 8
    while bit < lax.axis_size("rep"):
        total = add_low(total, hop(total, bit))
        bit *= 2
    return total


def fold_blocks(keep, send):
    f32 = jnp.float32
    got = hop(send, 1)
    sums = [add_low(keep[j], got[j]) for j in range(4)]
    across, along, both = hop(sums[2], 2), hop(sums[1], 4), hop(sums[3], 6)
    return [
        (
            sums[0][d].astype(f32)
            + across[d].astype(f32)
            + along[d].astype(f32)
            + both[d].astype(f32)
        ).astype(keep.dtype)
        for d in range(lax.axis_size("grp"))
    ]


def spread_blocks(own):
    near = jnp.stack([own, hop(own, 4), hop(own, 2), hop(own, 6)])
    return near, hop(near, 1)


def rows_of(vector, count):
    short = count * LANES - vector.shape[0]
    return jnp.pad(vector, (0, short)).reshape(count, LANES)


def lined(rows, length):
    return rows.reshape(rows.shape[0], -1)[:, :length].reshape(1, -1)


def place_scalars():
    bit_c, bit_x, bit_y = rep_bits()
    return jnp.stack([lax.axis_index("grp"), bit_c, bit_x, bit_y]).astype(jnp.int32)


def piece_row(where, core, high, low, rows):
    owner = where[1] ^ core
    first = jnp.where(owner == 0, where[2], where[3])
    second = jnp.where(owner == 0, where[3], where[2])
    index = owner * 4 + (first ^ high) * 2 + (second ^ low)
    return pl.multiple_of(index * (rows // 8), 16)


def piece_list():
    return [(c, h, l) for c in range(2) for h in range(2) for l in range(2)]


def dot(one, two, contract=(1, 0)):
    return lax.dot_general(
        one, two, (((contract[0],), (contract[1],)), ((), ())), preferred_element_type=jnp.float32
    )


def turned(value):
    return value.astype(jnp.float32).T.astype(value.dtype)


class Chunk:
    def __init__(self, dims, shares, has_out):
        self.shard, self.width, self.own, self.groups = dims
        self.shares, self.has_out = tuple(shares), has_out
        self.out_blocks = -(-self.width // LANES)
        self.rows_at, at = {}, 0
        if has_out:
            for j in range(self.out_blocks):
                self.rows_at["out", j] = at
                at += self.shard
        for share in self.shares:
            for kind in ("gate", "up"):
                for f in self.blocks(share):
                    self.rows_at[kind, f] = at
                    at += self.shard
            self.rows_at["down", share] = at
            at += self.width
        self.used = at
        self.rows = -(-at // 128) * 128
        self.part = self.rows // 8

    def blocks(self, share):
        return [owner * self.own + share for owner in range(self.groups)]


def chunks_of(shard, width, own_hidden, groups):
    own = own_hidden // LANES
    whole = (Chunk((shard, width, own, groups), range(own), True),)
    return whole, whole


def pack_first_kernel(where, query, key, value, small, out, blocks):
    shard = query.shape[0]
    whole = jnp.concatenate([query[...], key[...], value[...]], 1)
    for j in range(blocks.shape[0]):
        stop = min((j + 1) * LANES, whole.shape[1])
        blocks[j, :, : stop - j * LANES] = whole[:, j * LANES : stop]
        if stop < (j + 1) * LANES:
            blocks[j, :, stop - j * LANES :] = jnp.zeros(
                (shard, (j + 1) * LANES - stop), whole.dtype
            )
    out[:shard, :] = blocks[where[1] * 4 + where[2] * 2 + where[3]]
    out[shard:, :] = small[...]


def pack_second_kernel(chunks, where, gate, up, down_t, output, *refs):
    outs, packs = refs[: len(chunks)], refs[len(chunks) :]
    for chunk, out, pack in zip(chunks, outs, packs):
        shard, width = chunk.shard, chunk.width
        for (kind, j), at in chunk.rows_at.items():
            if kind == "down":
                pack[at : at + width, :] = down_t[:, j * LANES : (j + 1) * LANES]
                continue
            source = {"gate": gate, "up": up, "out": output}[kind]
            stop = min((j + 1) * LANES, source.shape[1])
            pack[at : at + shard, : stop - j * LANES] = source[:, j * LANES : stop]
            if stop < (j + 1) * LANES:
                pack[at : at + shard, stop - j * LANES :] = jnp.zeros(
                    (shard, (j + 1) * LANES - stop), pack.dtype
                )
        if chunk.used < chunk.rows:
            pack[chunk.used :, :] = jnp.zeros((chunk.rows - chunk.used, LANES), pack.dtype)
        row = piece_row(where, 0, 0, 0, chunk.rows)
        out[...] = pack[pl.ds(row, chunk.part), :]


def run_pack_first(where, query, key, value, small):
    shard = query.shape[0]
    return staged_call(
        pack_first_kernel,
        "pack_first",
        where,
        (query, key, value, small),
        (),
        shape((shard + SMALL, LANES), query.dtype),
        vmem(),
        [pltpu.VMEM((8, shard, LANES), query.dtype)],
        BIG,
    )


def run_pack_second(where, chunks, gate, up, down_t, output):
    kind = gate.dtype
    return staged_call(
        functools.partial(pack_second_kernel, chunks),
        "pack_second",
        where,
        (gate, up, down_t, output),
        (),
        tuple(shape((chunk.part, LANES), kind) for chunk in chunks),
        (vmem(),) * len(chunks),
        [pltpu.VMEM((chunk.rows, LANES), kind) for chunk in chunks],
        BIG,
    )


def block_at(where, core, across, along):
    return (where[1] ^ core) * 4 + (where[2] ^ across) * 2 + (where[3] ^ along)


def unit_heads(raw, head_size):
    pairs = []
    for at in range(0, raw.shape[1], head_size):
        head = raw[:, at : at + head_size]
        factor = lax.rsqrt(jnp.mean(head * head, axis=1, keepdims=True) + NORM_EPS)
        pairs.append((head * factor, factor))
    return pairs


def proj_kernel(sizes, where, near, far, tokens_t, gain, head_gains, cosine, sine, *refs):
    f32, bf16 = jnp.float32, jnp.bfloat16
    q_width, kv_width, head_size = sizes
    normed_out, raw_out, query_out, kv_out, weights_out = refs
    groups = near.shape[1]
    inputs = tokens_t[...].astype(f32).T
    scale = lax.rsqrt(jnp.mean(inputs * inputs, axis=1, keepdims=True) + NORM_EPS)
    normed = (inputs * scale * gain[...]).astype(bf16)
    normed_out[...] = normed
    for j in range(8):
        core, across, along = j // 4, j // 2 % 2, j % 2
        place = (where[2] ^ across) * 2 + (where[3] ^ along)
        pieces = []
        for owner in range(groups):
            behind = lax.rem(where[0] + groups - owner, groups)
            pieces.append(
                jnp.where(where[1] == core, near[place, behind], far[place, behind])
            )
        weights_out[:, j * LANES : (j + 1) * LANES] = jnp.concatenate(pieces, 0)
    flat = weights_out[...]
    raw = dot(normed, flat)
    raw_out[...] = raw[:, : q_width + kv_width]
    half = head_size // 2
    cos, sin = cosine[...], sine[...]

    def turn(head):
        one, two = head[:, :half], head[:, half:]
        return jnp.concatenate([one * cos - two * sin, two * cos + one * sin], 1)

    heads = []
    for at, (unit, _) in enumerate(unit_heads(raw[:, : q_width + kv_width], head_size)):
        row = 0 if at * head_size < q_width else 1
        heads.append(turn(unit * head_gains[row : row + 1, :]).astype(bf16))
    queries = jnp.concatenate(heads[: q_width // head_size], 1)
    query_out[...] = (queries.astype(f32) * head_size ** (-0.5)).astype(bf16)
    values = raw[:, q_width + kv_width : q_width + 2 * kv_width].astype(bf16)
    kv_out[...] = jnp.concatenate(heads[q_width // head_size :] + [values], 1)


def run_proj(where, near, far, tokens_t, gain, head_gains, cosine, sine, sizes):
    f32, bf16 = jnp.float32, jnp.bfloat16
    q_width, kv_width, _ = sizes
    width, toks = tokens_t.shape
    return pl.pallas_call(
        functools.partial(proj_kernel, sizes),
        out_shape=(
            shape((toks, width), bf16),
            shape((toks, q_width + kv_width), f32),
            shape((toks, q_width), bf16),
            shape((toks, 2 * kv_width), bf16),
            shape((width, 8 * LANES), bf16),
        ),
        in_specs=[smem()] + [vmem()] * 7,
        out_specs=(vmem(),) * 5,
        compiler_params=options(24),
        cost_estimate=cost(),
        name="proj",
    )(where, near, far, tokens_t, gain, head_gains, cosine, sine)


def attend_kernel(sizes, where, query, own_seg, key_seg, *refs):
    f32, bf16 = jnp.float32, jnp.bfloat16
    q_width, kv_width, head_size = sizes
    held = refs[: len(refs) - 5]
    attended, probs_out, bias, probs, sems = refs[len(refs) - 5 :]
    toks = query.shape[0]
    same = own_seg[...] == key_seg[...]
    order = lax.broadcasted_iota(jnp.int32, same.shape, 0) - lax.broadcasted_iota(
        jnp.int32, same.shape, 1
    )
    later = lax.broadcasted_iota(jnp.int32, same.shape, 1) >= toks
    bias[...] = jnp.where(same & ((order >= 0) | later), 0.0, -1e30)
    outs = []
    per = q_width // kv_width
    for g in range(kv_width // head_size):
        cols = slice(g * head_size, (g + 1) * head_size)
        keys = jnp.concatenate([kv[:, cols] for kv in held], 0)
        cols = slice(kv_width + g * head_size, kv_width + (g + 1) * head_size)
        values = jnp.concatenate([kv[:, cols] for kv in held], 0)
        for head in range(g * per, (g + 1) * per):
            scores = dot(query[:, head * head_size : (head + 1) * head_size], keys, (1, 1))
            scores = scores + bias[...]
            powers = jnp.exp(scores - jnp.max(scores, axis=1, keepdims=True))
            share = 1.0 / jnp.sum(powers, axis=1, keepdims=True)
            low = (powers * share).astype(bf16)
            probs[head] = low
            pltpu.make_async_copy(probs.at[head], probs_out.at[head], sems.at[head]).start()
            outs.append(dot(low, values))
    attended[...] = jnp.concatenate(outs, 1).astype(bf16)
    for head in range(probs.shape[0]):
        pltpu.make_async_copy(probs.at[head], probs_out.at[head], sems.at[head]).wait()


def run_attend(where, query, own_seg, key_seg, held, sizes):
    bf16 = jnp.bfloat16
    q_width, kv_width, head_size = sizes
    toks = query.shape[0]
    keys = toks * len(held)
    heads = q_width // head_size
    return staged_call(
        functools.partial(attend_kernel, sizes),
        "attend",
        where,
        (query, own_seg, key_seg, *held),
        (),
        (shape((toks, q_width), bf16), shape((heads, toks, keys), bf16)),
        (vmem(), hbm()),
        [
            pltpu.VMEM((toks, keys), jnp.float32),
            pltpu.VMEM((heads, toks, keys), bf16),
            pltpu.SemaphoreType.DMA((heads,)),
        ],
        BIG,
    )


def attend_back_kernel(sizes, where, query, grad, *refs):
    f32, bf16 = jnp.float32, jnp.bfloat16
    q_width, kv_width, head_size = sizes
    probs, sems = refs[-2:]
    refs = refs[:-2]
    groups = (len(refs) - 2) // 2
    probs_in = refs[groups]
    refs = refs[:groups] + refs[groups + 1 :]
    copies = [
        pltpu.make_async_copy(probs_in.at[head], probs.at[head], sems.at[head])
        for head in range(probs.shape[0])
    ]
    for copy in copies:
        copy.start()
    held = refs[:groups]
    query_grad = refs[groups]
    kv_grads = refs[groups + 1 :]
    toks = query.shape[0]
    per = q_width // kv_width
    query_t = query[...].astype(f32).T.astype(bf16)
    grad_t = grad[...].astype(f32).T.astype(bf16)
    outs, key_parts, value_parts = [], [], []
    for g in range(kv_width // head_size):
        cols = slice(g * head_size, (g + 1) * head_size)
        keys = jnp.concatenate([kv[:, cols] for kv in held], 0)
        cols = slice(kv_width + g * head_size, kv_width + (g + 1) * head_size)
        values = jnp.concatenate([kv[:, cols] for kv in held], 0)
        key_t = value_t = None
        for head in range(g * per, (g + 1) * per):
            cols = slice(head * head_size, (head + 1) * head_size)
            copies[head].wait()
            low = probs[head]
            share = low.astype(f32)
            weighed = share * dot(grad[:, cols], values, (1, 1))
            scores = (weighed - share * jnp.sum(weighed, axis=1, keepdims=True)).astype(bf16)
            outs.append(dot(scores, keys))
            key_one = dot(query_t[cols, :], scores)
            value_one = dot(grad_t[cols, :], low)
            key_t = key_one if key_t is None else key_t + key_one
            value_t = value_one if value_t is None else value_t + value_one
        key_parts.append(key_t)
        value_parts.append(value_t)
    query_grad[...] = jnp.concatenate(outs, 1) * head_size ** (-0.5)
    both = jnp.concatenate(key_parts + value_parts, 0)
    for at, out in enumerate(kv_grads):
        out[...] = both[:, at * toks : (at + 1) * toks].T.astype(out.dtype)


def run_attend_back(where, query, grad, probs, held, sizes):
    f32, bf16 = jnp.float32, jnp.bfloat16
    q_width, kv_width, head_size = sizes
    toks = query.shape[0]
    keys = toks * len(held)
    return staged_call(
        functools.partial(attend_back_kernel, sizes),
        "attend_back",
        where,
        (query, grad, *held),
        (probs,),
        (shape((toks, q_width), f32),) + tuple(shape((toks, 2 * kv_width), bf16) for _ in held),
        (vmem(),) * (1 + len(held)),
        [pltpu.VMEM(probs.shape, bf16), pltpu.SemaphoreType.DMA((probs.shape[0],))],
        BIG,
    )


def mlp_kernel(w_chunks, g_chunks, where, *refs):
    f32, bf16 = jnp.float32, jnp.bfloat16
    count = 4 * len(w_chunks)
    attended, tokens_t, out_grad_t, gain = refs[:4]
    pieces = refs[4 : count + 4]
    refs = refs[count + 4 :]
    layer_out_t, mixed_grad, attended_grad, gain_grad = refs[:4]
    packed, refs = refs[4 : 4 + 2 * len(g_chunks)], refs[4 + 2 * len(g_chunks) :]
    weights, refs = refs[: len(w_chunks)], refs[len(w_chunks) :]
    grads, (sem_in, sem_out) = refs[: len(g_chunks)], refs[len(g_chunks) :]
    width, toks = tokens_t.shape
    shard, groups, out_blocks = w_chunks[0].shard, w_chunks[0].groups, w_chunks[0].out_blocks
    for number, chunk in enumerate(w_chunks):
        for core, high, low in piece_list():
            row = piece_row(where, core, high, low, chunk.rows)
            for behind in range(groups):
                pltpu.make_async_copy(
                    pieces[number * 4 + core * 2 + high].at[low, behind],
                    weights[number].at[
                        lax.rem(where[0] + groups - behind, groups), pl.ds(row, chunk.part)
                    ],
                    sem_in.at[number],
                ).start()

    def leave(number):
        chunk = g_chunks[number]
        keep, send = packed[2 * number : 2 * number + 2]
        for core, high, low in piece_list():
            row = piece_row(where, core, high, low, chunk.rows)
            for step in range(groups):
                pltpu.make_async_copy(
                    grads[number].at[lax.rem(where[0] + step, groups), pl.ds(row, chunk.part)],
                    (send if core else keep).at[high, low, step],
                    sem_out.at[number, core],
                ).start()

    def column(number, kind, f):
        at = w_chunks[number].rows_at[kind, f]
        return weights[number][:, at : at + shard, :].reshape(groups * shard, LANES)

    def store(number, kind, f, block):
        at = g_chunks[number].rows_at[kind, f]
        for owner in range(groups):
            grads[number][owner, at : at + shard, :] = block[owner * shard : (owner + 1) * shard]

    out_t = out_grad_t[...]
    upstream = turned(out_t)
    inputs = tokens_t[...].astype(f32).T
    att_t = turned(attended[...])
    for number, chunk in enumerate(g_chunks):
        if chunk.used < chunk.rows:
            grads[number][:, chunk.used :, :] = jnp.zeros(
                (groups, chunk.rows - chunk.used, LANES), bf16
            )
    waited = 0

    def need(number):
        nonlocal waited
        while waited <= number:
            pltpu.make_async_copy(weights[waited], weights[waited], sem_in.at[waited]).wait()
            waited += 1

    need(0)
    output_w = jnp.concatenate([column(0, "out", j) for j in range(out_blocks)], 1)[:, :width]
    mixed = inputs + dot(attended[...], output_w)
    scale = lax.rsqrt(jnp.mean(mixed * mixed, axis=1, keepdims=True) + NORM_EPS)
    unit = mixed * scale
    gained = gain[...]
    normed = (unit * gained).astype(bf16)
    normed_t = turned(normed)
    back = jnp.zeros(mixed.shape, f32)
    ahead = mixed
    w_home = {share: number for number, chunk in enumerate(w_chunks) for share in chunk.shares}
    g_home = {share: number for number, chunk in enumerate(g_chunks) for share in chunk.shares}
    for share in range(w_chunks[0].own):
        source, sink = w_home[share], g_home[share]
        need(source)
        w_chunk, g_chunk = w_chunks[source], g_chunks[sink]
        blocks = w_chunk.blocks(share)
        down_at = w_chunk.rows_at["down", share]
        down_to = g_chunk.rows_at["down", share]
        for pair in range(0, len(blocks), 2):
            some = blocks[pair : pair + 2]
            gate_w = jnp.concatenate([column(source, "gate", f) for f in some], 1)
            up_w = jnp.concatenate([column(source, "up", f) for f in some], 1)
            down_w = jnp.concatenate(
                [weights[source][f // w_chunk.own, down_at : down_at + width, :] for f in some], 1
            )
            gate = dot(normed, gate_w)
            up = dot(normed, up_w)
            hidden_grad = dot(upstream, down_w)
            sigmoid = 1.0 / (1.0 + jnp.exp(-gate))
            silu = gate * sigmoid
            hidden = (silu * up).astype(bf16)
            gate_low = (hidden_grad * up * (sigmoid * (1.0 + gate * (1.0 - sigmoid)))).astype(bf16)
            up_low = (hidden_grad * silu).astype(bf16)
            ahead = ahead + dot(hidden, down_w, (1, 1))
            back = back + dot(gate_low, gate_w, (1, 1)) + dot(up_low, up_w, (1, 1))
            gate_wg = dot(normed_t, gate_low).astype(bf16)
            up_wg = dot(normed_t, up_low).astype(bf16)
            down_wg = dot(out_t, hidden).astype(bf16)
            for at, f in enumerate(some):
                cols = slice(at * LANES, (at + 1) * LANES)
                store(sink, "gate", f, gate_wg[:, cols])
                store(sink, "up", f, up_wg[:, cols])
                grads[sink][f // g_chunk.own, down_to : down_to + width, :] = down_wg[:, cols]
        if share == g_chunk.shares[-1] and not g_chunk.has_out:
            leave(sink)
    layer_out_t[...] = ahead.T.astype(bf16)
    gain_grad[...] = jnp.sum(back * unit, axis=0, keepdims=True)
    inner = back * gained
    through = scale * (inner - unit * jnp.mean(inner * unit, axis=1, keepdims=True))
    mixed_back = upstream.astype(f32) + through
    mixed_grad[...] = mixed_back
    branch = mixed_back.astype(bf16)
    attended_grad[...] = dot(branch, output_w, (1, 1)).astype(bf16)
    output_wg = dot(att_t, branch)
    last = len(g_chunks) - 1
    for j in range(out_blocks):
        block = output_wg[:, j * LANES : min((j + 1) * LANES, width)]
        if block.shape[1] < LANES:
            block = jnp.concatenate(
                [block, jnp.zeros((block.shape[0], LANES - block.shape[1]), f32)], 1
            )
        store(last, "out", j, block.astype(bf16))
    leave(last)
    for number in range(len(g_chunks)):
        for core in range(2):
            out = packed[2 * number + core]
            pltpu.make_async_copy(out, out, sem_out.at[number, core]).wait()


def run_mlp(where, w_chunks, g_chunks, pieces, attended, tokens_t, out_grad_t, gain):
    f32, bf16 = jnp.float32, jnp.bfloat16
    groups = w_chunks[0].groups
    width, toks = tokens_t.shape
    packed = []
    for chunk in g_chunks:
        packed += [shape((2, 2, groups, chunk.part, LANES), bf16)] * 2
    return staged_call(
        functools.partial(mlp_kernel, w_chunks, g_chunks),
        "mlp",
        where,
        (attended, tokens_t, out_grad_t, gain),
        pieces,
        (
            shape((width, toks), bf16),
            shape((toks, width), f32),
            shape((toks, width), bf16),
            shape((1, width), f32),
        )
        + tuple(packed),
        (vmem(),) * 4 + (hbm(),) * len(packed),
        [pltpu.VMEM((groups, chunk.rows, LANES), bf16) for chunk in w_chunks + g_chunks]
        + [
            pltpu.SemaphoreType.DMA((len(w_chunks),)),
            pltpu.SemaphoreType.DMA((len(g_chunks), 2)),
        ],
        BIG,
    )


def last_kernel(sizes, where, query_grad, raw, normed, tokens_t, mixed_grad, gain, head_gains, cosine, sine, weights, second, *refs):
    f32, bf16 = jnp.float32, jnp.bfloat16
    q_width, kv_width, head_size = sizes
    kv_parts = refs[: len(refs) - 4]
    token_grad_t, keep, send, grads = refs[len(refs) - 4 :]
    count, groups, rows, _ = grads.shape
    width, toks = tokens_t.shape
    shard = width // groups
    half = head_size // 2
    cos, sin = cosine[...], sine[...]
    kv_grad = kv_parts[0][...].astype(f32)
    for part in kv_parts[1:]:
        kv_grad = kv_grad + part[...].astype(f32)
    lows, head_sums = [], [jnp.zeros((1, head_size), f32)] * 2
    for at, (unit, factor) in enumerate(unit_heads(raw[...], head_size)):
        kind = 0 if at * head_size < q_width else 1
        source, place = (query_grad, at * head_size) if kind == 0 else (kv_grad, at * head_size - q_width)
        one = source[:, place : place + half]
        two = source[:, place + half : place + head_size]
        back = jnp.concatenate([one * cos + two * sin, two * cos - one * sin], 1)
        head_sums[kind] = head_sums[kind] + jnp.sum(back * unit, axis=0, keepdims=True)
        inner = back * head_gains[kind : kind + 1, :]
        lows.append(factor * (inner - unit * jnp.mean(inner * unit, axis=1, keepdims=True)))
    lows.append(kv_grad[:, kv_width:])
    short = count * LANES - q_width - 2 * kv_width
    if short:
        lows.append(jnp.zeros((toks, short), f32))
    low = jnp.concatenate(lows, 1).astype(bf16)
    back = dot(low, weights[...], (1, 1))
    inputs = tokens_t[...].astype(f32).T
    scale = lax.rsqrt(jnp.mean(inputs * inputs, axis=1, keepdims=True) + NORM_EPS)
    unit = inputs * scale
    first = jnp.sum(back * unit, axis=0, keepdims=True)
    inner = back * gain[...]
    whole = mixed_grad[...] + scale * (inner - unit * jnp.mean(inner * unit, axis=1, keepdims=True))
    token_grad_t[...] = whole.T
    normed_t = turned(normed[...])
    products = dot(normed_t, low).astype(bf16)
    for j in range(count):
        for owner in range(groups):
            grads[j, owner, :shard, :] = products[
                owner * shard : (owner + 1) * shard, j * LANES : (j + 1) * LANES
            ]
            grads[j, owner, shard:, :] = jnp.zeros((rows - shard, LANES), bf16)

    def line(vector):
        short = LANES - vector.shape[1]
        return jnp.concatenate([vector, jnp.zeros((1, short), f32)], 1) if short else vector

    head_part = head_size // groups
    for owner in range(groups):
        lines = []
        for vector in (first, second[...]):
            mine = vector[:, owner * shard : (owner + 1) * shard]
            lines += [line(mine[:, at : at + LANES]) for at in range(0, shard, LANES)]
        for vector in head_sums:
            lines.append(line(vector[:, owner * head_part : (owner + 1) * head_part]))
        lines.append(jnp.zeros((rows - shard - len(lines), LANES), f32))
        grads[0, owner, shard:, :] = jnp.concatenate(lines, 0).astype(bf16)
    for core in range(2):
        for across in range(2):
            for along in range(2):
                block = block_at(where, core, across, along)
                for step in range(groups):
                    owner = lax.rem(where[0] + step, groups)
                    (send if core else keep)[across * 2 + along, step] = grads[block, owner]


def run_last(where, query_grad, raw, normed, tokens_t, mixed_grad, gain, head_gains, cosine, sine, weights, second, kv_parts, sizes):
    f32, bf16 = jnp.float32, jnp.bfloat16
    width, toks = tokens_t.shape
    groups = lax.axis_size("grp")
    rows = width // groups + SMALL
    packed = shape((4, groups, rows, LANES), bf16)
    return pl.pallas_call(
        functools.partial(last_kernel, sizes),
        out_shape=(shape((width, toks), f32), packed, packed),
        in_specs=[smem()] + [vmem()] * (11 + len(kv_parts)),
        out_specs=(vmem(),) * 3,
        scratch_shapes=[pltpu.VMEM((8, groups, rows, LANES), bf16)],
        compiler_params=options(24),
        cost_estimate=cost(),
        name="last",
    )(where, query_grad, raw, normed, tokens_t, mixed_grad, gain, head_gains, cosine, sine, weights, second, *kv_parts)


def unpack_kernel(sizes, chunks, where, near, far, *refs):
    f32 = jnp.float32
    q_width, kv_width, _ = sizes
    gate, up, down_t, output, query, key, value = refs[:7]
    lines_out = refs[7:11]
    packs = refs[11 : 11 + len(chunks)]
    shard, width = chunks[0].shard, chunks[0].width
    projections = []
    small = None
    for core in range(2):
        for across in range(2):
            for along in range(2):
                place = (where[2] ^ across) * 2 + (where[3] ^ along)
                piece = jnp.where(where[1] == core, near[place], far[place])
                at = 0
                for chunk, pack in zip(chunks, packs):
                    high, low = (across, along) if core == 0 else (along, across)
                    row = (core * 4 + high * 2 + low) * chunk.part
                    pack[row : row + chunk.part, :] = piece[at : at + chunk.part]
                    at += chunk.part
                projections.append(piece[at : at + shard])
                if small is None:
                    small = piece[at + shard :].astype(f32)
    for chunk, pack in zip(chunks, packs):
        for (kind, j), at in chunk.rows_at.items():
            if kind == "down":
                down_t[:, j * LANES : (j + 1) * LANES] = pack[at : at + width].astype(f32)
                continue
            out = {"gate": gate, "up": up, "out": output}[kind]
            stop = min((j + 1) * LANES, out.shape[1])
            out[:, j * LANES : stop] = pack[at : at + shard].astype(f32)[:, : stop - j * LANES]
    whole = jnp.concatenate(projections, 1).astype(f32)
    query[...] = whole[:, :q_width]
    key[...] = whole[:, q_width : q_width + kv_width]
    value[...] = whole[:, q_width + kv_width : q_width + 2 * kv_width]
    row = 0
    for out in lines_out:
        for at in range(0, out.shape[1], LANES):
            stop = min(at + LANES, out.shape[1])
            out[:, at:stop] = small[row : row + 1, : stop - at]
            row += 1


def run_unpack(where, chunks, sizes, near, far, hidden_width, own_hidden, head_part):
    f32 = jnp.float32
    q_width, kv_width, _ = sizes
    shard, width = chunks[0].shard, chunks[0].width
    return staged_call(
        functools.partial(unpack_kernel, sizes, chunks),
        "unpack",
        where,
        (near, far),
        (),
        (
            shape((shard, hidden_width), f32),
            shape((shard, hidden_width), f32),
            shape((width, own_hidden), f32),
            shape((shard, width), f32),
            shape((shard, q_width), f32),
            shape((shard, kv_width), f32),
            shape((shard, kv_width), f32),
            shape((1, shard), f32),
            shape((1, shard), f32),
            shape((1, head_part), f32),
            shape((1, head_part), f32),
        ),
        (vmem(),) * 11,
        [pltpu.VMEM((chunk.rows, LANES), near.dtype) for chunk in chunks],
        BIG,
    )


def body(
    tokens,
    segments,
    out_grad,
    norm_gain,
    query_gain,
    key_gain,
    query_weight,
    key_weight,
    value_weight,
    output_weight,
    second_gain,
    gate_weight,
    up_weight,
    down_weight,
):
    f32, bf16 = jnp.float32, jnp.bfloat16
    groups = lax.axis_size("grp")
    place_z = lax.axis_index("grp")
    where = place_scalars()
    toks, width = tokens.shape
    shard = norm_gain.shape[0]
    head_part = query_gain.shape[0]
    head_size = head_part * groups
    hidden_width, own_hidden = gate_weight.shape[1], down_weight.shape[0]
    sizes = (query_weight.shape[1], key_weight.shape[1], head_size)
    w_chunks, g_chunks = chunks_of(shard, width, own_hidden, groups)
    tokens_t, out_grad_t = tokens.T, out_grad.T

    gain_rows = -(-shard // LANES)
    seg_rows = -(-toks // LANES)
    small = jnp.zeros((SMALL * LANES,), bf16)
    at = 0
    for line, count in (
        (norm_gain, gain_rows),
        (second_gain, gain_rows),
        (query_gain, 1),
        (key_gain, 1),
        (segments.astype(bf16), seg_rows),
    ):
        small = small + jnp.pad(line, (at, SMALL * LANES - at - line.shape[0]))
        at += count * LANES
    fence = lax.optimization_barrier
    (own_second,) = run_pack_second(
        where, w_chunks, gate_weight, up_weight, down_weight.T, output_weight
    )
    second_z = [own_second] + [shift(own_second, step) for step in range(1, groups)]
    _, small = fence((own_second, small))
    own_first = run_pack_first(
        where, query_weight, key_weight, value_weight, small.reshape(SMALL, LANES)
    )
    first_z = [own_first] + [shift(own_first, step) for step in range(1, groups)]
    near, far = spread_blocks(jnp.stack([held[:shard] for held in first_z]))

    small_behind = jnp.stack([held[shard:] for held in first_z]).astype(f32)
    small_all = small_behind[lax.rem(place_z + groups - jnp.arange(groups), groups)]
    at = 0
    gains = []
    for count, length in ((gain_rows, shard), (gain_rows, shard), (1, head_part), (1, head_part)):
        gains.append(lined(small_all[:, at : at + count], length))
        at += count
    gain_first, gain_second, gain_query, gain_key = gains
    head_gains = jnp.concatenate([gain_query, gain_key])
    segs = small_behind[:, at : at + seg_rows].reshape(groups, -1)[:, :toks]
    there = (place_z >= jnp.arange(groups))[:, None]
    key_seg = jnp.where(there, segs, -1.0).reshape(1, -1)
    own_seg = segs[0][:, None]
    earlier = ((key_seg < own_seg) & (key_seg >= 0.0)).astype(jnp.int32)
    positions = place_z * toks + jnp.arange(toks, dtype=jnp.int32) - jnp.sum(earlier, axis=1)
    half = head_size // 2
    inverse = ROPE_BASE ** (-(jnp.arange(half, dtype=f32) * 2.0 / head_size))
    angles = positions.astype(f32)[:, None] * inverse[None, :]
    cosine, sine = jnp.cos(angles), jnp.sin(angles)

    normed, raw, query, key_value, proj_weights = run_proj(
        where, near, far, tokens_t, gain_first, head_gains, cosine, sine, sizes
    )
    held = [key_value]
    for step in range(1, groups):
        ahead = [(i, i + step) for i in range(groups - step)]
        held.append(lax.ppermute(key_value, "grp", ahead))
    whole = jnp.stack(second_z)
    whole = jnp.stack([whole, hop_split(whole, 4, 2)])
    far_whole = hop_split(whole, 2, 4)
    whole, held = fence((whole, held))
    other = hop(whole, 1)
    attended, probs = run_attend(where, query, own_seg, key_seg, held, sizes)
    got, attended, other = fence((far_whole, attended, other))
    pieces = [whole, got, other, hop(got, 1)]
    layer_out_t, mixed_grad, attended_grad, second_sum, keep, send = run_mlp(
        where, w_chunks, g_chunks, pieces, attended, tokens_t, out_grad_t, gain_second
    )
    got = hop(send, 1)
    query_grad, *kv_parts = run_attend_back(where, query, attended_grad, probs, held, sizes)
    got, query_grad, kv_parts = fence((got, query_grad, kv_parts))
    kv_back = [kv_parts[0]]
    for step in range(1, groups):
        behind = [(i + step, i) for i in range(groups - step)]
        kv_back.append(lax.ppermute(kv_parts[step], "grp", behind))
    near, away = add_low(keep[0], got[0]), add_low(keep[1], got[1])
    got, kv_back = fence((hop_split(away, 2, 4), kv_back))
    near, away = add_low(near[0], got[0]), add_low(near[1], got[1])
    got = hop_split(away, 4, 2)
    token_grad_t, late_keep, late_send = run_last(
        where, query_grad, raw, normed, tokens_t, mixed_grad, gain_first, head_gains, cosine, sine,
        proj_weights, second_sum, kv_back, sizes,
    )
    got, late_keep, late_send = fence((got, late_keep, late_send))
    early = fold_grp([add_low(near[d], got[d]) for d in range(groups)])
    late = fold_blocks(late_keep, late_send)
    early, late = fence((early, late))
    near, far = spread_blocks(jnp.concatenate([early, fold_grp(late)]))
    (
        gate_sum, up_sum, down_sum_t, output_sum, query_sum, key_sum, value_sum,
        first_sum, second_sum, query_gsum, key_gsum,
    ) = run_unpack(where, g_chunks, sizes, near, far, hidden_width, own_hidden, head_part)
    return (
        layer_out_t.T,
        token_grad_t.T,
        first_sum.reshape(-1),
        query_gsum.reshape(-1),
        key_gsum.reshape(-1),
        query_sum,
        key_sum,
        value_sum,
        output_sum,
        second_sum.reshape(-1),
        gate_sum,
        up_sum,
        down_sum_t.T,
    )


def solution(mesh):
    placed = (
        P(("rep", "grp"), None),
        P(("rep", "grp")),
        P(("rep", "grp"), None),
        P("grp"),
        P("grp"),
        P("grp"),
        P("grp", None),
        P("grp", None),
        P("grp", None),
        P("grp", None),
        P("grp"),
        P("grp", None),
        P("grp", None),
        P("grp", None),
    )
    return jax.shard_map(
        body,
        mesh=mesh,
        in_specs=placed,
        out_specs=(
            P(("rep", "grp"), None),
            P(("rep", "grp"), None),
            P("grp"),
            P("grp"),
            P("grp"),
            P("grp", None),
            P("grp", None),
            P("grp", None),
            P("grp", None),
            P("grp"),
            P("grp", None),
            P("grp", None),
            P("grp", None),
        ),
        check_vma=False,
    )
```

profile of v0, /device:TPU:0, one launch (start us, length us, event | category | flops | bytes accessed | tf_op | source)
XLA Modules:
  0.0 195.1 jit_solution(1333171740511912352)
XLA Ops:
  0.7 0.7 convert_element_type.317
  1.3 0.6 pad_add_fusion.1.where_ref.where
  2.0 1.3 pad_add_fusion
  3.3 3.0 %pack_second.1 = bf16[752,128]{1,0:T(8,128)(2,1)} custom-call(s32[4]{0:T(128)} %pad_add_fusion.1.where_ref.where, bf16[144,1536]{1,0:T(8,128)(2,1)} %refs_0_.2, bf16[144,1536]{1,0:T(8,128)(2,1)} %refs_1_.2, bf16[576,384]{1,0:T(8,128)(2,1)} %bitcast.156, bf16[144,576]{1,0:T(8,128)(2,1)} %refs_3_.1), custom_call_target="tpu_custom_call" | custom-call | flops 1 | bytes 1024 | tf_op jit(solution)/shard_map/pack_second/pallas_call | solution.py:74
  6.3 2.4 %pack_first.1 = bf16[160,128]{1,0:T(8,128)(2,1)} custom-call(s32[4]{0:T(128)} %pad_add_fusion.1.where_ref.where, bf16[144,576]{1,0:T(8,128)(2,1)} %refs_0_.3, bf16[144,192]{1,0:T(8,128)(2,1)} %refs_1_.3, bf16[144,192]{1,0:T(8,128)(2,1)} %refs_2_.1, bf16[16,128]{1,0:T(8,128)(2,1)} %bitcast.169), custom_call_target="tpu_custom_call" | custom-call | flops 1 | bytes 1024 | tf_op jit(solution)/shard_map/pack_first/pallas_call | solution.py:74
  8.7 5.1 %collective-permute-start.7 = (bf16[160,128]{1,0:T(8,128)(2,1)}, bf16[160,128]{1,0:T(8,128)(2,1)S(1)}, u32[]{:S(2)}, u32[]{:S(2)}) collective-permute-start(bf16[160,128]{1,0:T(8,128)(2,1)} %pack_first.1), channel_id=1, source_target_pairs={{0,3},{1,0},{2,1},{3,2},{4,7},{5,4},{6,5},{7,6},{8,11},{9,8},{10,9... | collective-permute-start | bytes 122888 | tf_op jit(solution)/shard_map/ppermute | solution.py:95
  13.8 1.0 collective-permute-start.5
  14.8 2.8 %collective-permute-start.2 = (bf16[752,128]{1,0:T(8,128)(2,1)}, bf16[752,128]{1,0:T(8,128)(2,1)S(1)}, u32[]{:S(2)}, u32[]{:S(2)}) collective-permute-start(bf16[752,128]{1,0:T(8,128)(2,1)} %pack_second.1), channel_id=1, source_target_pairs={{0,3},{1,0},{2,1},{3,2},{4,7},{5,4},{6,5},{7,6},{8,11},{9,8},{10,9... | collective-permute-start | bytes 577544 | tf_op jit(solution)/shard_map/ppermute | solution.py:95
  17.6 1.1 collective-permute-start.1
  18.8 0.7 slice_bitcast_fusion.19
  19.5 0.8 slice_bitcast_fusion.13
  21.2 1.6 collective-permute-start.9
  22.7 1.5 collective-permute-start.8
  24.3 1.4 collective-permute-start.10
  25.8 10.0 %collective-permute-done.1 = bf16[752,128]{1,0:T(8,128)(2,1)S(1)} collective-permute-done((bf16[752,128]{1,0:T(8,128)(2,1)}, bf16[752,128]{1,0:T(8,128)(2,1)S(1)}, u32[]{:S(2)}, u32[]{:S(2)}) %collective-permute-start.1) | collective-permute-done | bytes 192544 | tf_op jit(solution)/shard_map/ppermute | solution.py:95
  35.9 2.2 %fusion.38 = (bf16[1,4,752,128]{3,2,1,0:T(8,128)(2,1)}, bf16[4,752,128]{2,1,0:T(8,128)(2,1)}) fusion(bf16[1,752,128]{2,1,0:T(8,128)(2,1)S(1)} %bitcast.161, bf16[1,752,128]{2,1,0:T(8,128)(2,1)S(1)} %bitcast.162, bf16[1,752,128]{2,1,0:T(8,128)(2,1)S(1)} %bitcast.163, bf16[1,752,128]{2,1,0:T(8,128)(2,1)} %bitcast.155), kind=kLoop, calls=%fused_computation.104 | loop fusion | flops 1155072 | bytes 2310144 | tf_op jit(solution)/shard_map/stack | solution.py:875
  38.1 1.5 collective-permute-start.3
  40.7 1.0 collective-permute-done.11.far
  41.8 0.8 copy-done.6
  42.6 1.1 copy-done.7
  43.7 5.0 %proj.1 = (bf16[256,576]{1,0:T(8,128)(2,1)S(1)}, f32[256,768]{1,0:T(8,128)S(1)}, bf16[256,576]{1,0:T(8,128)(2,1)S(1)}, bf16[256,384]{1,0:T(8,128)(2,1)S(1)}, bf16[576,1024]{1,0:T(8,128)(2,1)S(1)}) custom-call(s32[4]{0:T(128)S(1)} %copy-done.11, bf16[4,4,144,128]{3,2,1,0:T(8,128)(2,1)S(1)} %pad_maximum_fusion.3.near, bf16[4,4,144,128]{3,2,1,0:T(8,128)(2,1)S(1)} %copy-done.7, ...), custom_call_target="tpu_custom_call" | custom-call | flops 1 | bytes 1024 | tf_op jit(solution)/shard_map/proj/pallas_call | solution.py:334
  48.7 1.3 collective-permute-start.14
  50.0 2.4 %collective-permute-start.13 = (bf16[256,384]{1,0:T(8,128)(2,1)S(1)}, bf16[256,384]{1,0:T(8,128)(2,1)S(1)}, u32[]{:S(2)}, u32[]{:S(2)}) collective-permute-start(bf16[256,384]{1,0:T(8,128)(2,1)S(1)} %get-tuple-element.76.refs_3_.refs_2_), channel_id=1, source_target_pairs={{0,2},{1,3},{4,6},{5,7},{8,10},{9,11},{12,14},{13,15},{16,18},{17,... | collective-permute-start | bytes 589832 | tf_op jit(solution)/shard_map/ppermute | solution.py:873
  52.4 1.5 collective-permute-start.12
  53.9 2.7 %pad_maximum_fusion.refs_4_ = bf16[2,4,752,128]{3,2,1,0:T(8,128)(2,1)} fusion(bf16[1,4,752,128]{3,2,1,0:T(8,128)(2,1)} %bitcast.10, bf16[1,4,752,128]{3,2,1,0:T(8,128)(2,1)} %get-tuple-element.146), kind=kLoop, calls=%fused_computation.4 | loop fusion | flops 770048 | bytes 3080192 | tf_op jit(solution)/shard_map/stack | solution.py:875
  56.6 1.5 collective-permute-start.4
  58.2 1.3 collective-permute-done.13.refs_5_.refs_4_
  59.5 3.7 %collective-permute-done.12.refs_4_.refs_3_ = bf16[256,384]{1,0:T(8,128)(2,1)S(1)} collective-permute-done((bf16[256,384]{1,0:T(8,128)(2,1)S(1)}, bf16[256,384]{1,0:T(8,128)(2,1)S(1)}, u32[]{:S(2)}, u32[]{:S(2)}) %collective-permute-start.12) | collective-permute-done | bytes 196640 | tf_op jit(solution)/shard_map/ppermute | solution.py:873
  63.3 0.8 copy.28.refs_1_
  64.1 0.6 broadcast_select_fusion.refs_2_
  64.7 9.2 %attend.1 = (bf16[256,576]{1,0:T(8,128)(2,1)}, bf16[9,256,1024]{2,1,0:T(8,128)(2,1)}) custom-call(s32[4]{0:T(128)} %pad_add_fusion.1.where_ref.where, bf16[256,576]{1,0:T(8,128)(2,1)} %copy-done.2, f32[256,1]{1,0:T(8,128)} %copy.28.refs_1_, f32[1,1024]{1,0:T(1,128)} %broadcast_select_fusion.refs_2_, bf16[256,384]{1,0:T(8,128)(2,1)} %copy-done.3, ...), custom_call_target="tpu_custom_call" | custom-call | flops 1 | bytes 1024 | tf_op jit(solution)/shard_map/attend/pallas_call | solution.py:74
  73.9 3.1 %collective-permute-done.4.refs_5_ = bf16[2,4,752,128]{3,2,1,0:T(8,128)(2,1)} collective-permute-done((bf16[2,4,752,128]{3,2,1,0:T(8,128)(2,1)}, bf16[2,4,752,128]{3,2,1,0:T(8,128)(2,1)}, u32[]{:S(2)}, u32[]{:S(2)}) %collective-permute-start.4) | collective-permute-done | bytes 1540128 | tf_op jit(solution)/shard_map/ppermute | solution.py:105
  77.1 0.7 reshape.280.refs_3_
  77.7 3.0 %collective-permute-done.16.refs_7_ = bf16[2,4,752,128]{3,2,1,0:T(8,128)(2,1)} collective-permute-done((bf16[2,4,752,128]{3,2,1,0:T(8,128)(2,1)}, bf16[2,4,752,128]{3,2,1,0:T(8,128)(2,1)}, u32[]{:S(2)}, u32[]{:S(2)}) %collective-permute-start.16) | collective-permute-done | bytes 1540128 | tf_op jit(solution)/shard_map/ppermute | solution.py:90
  80.8 15.0 %mlp.1 = (bf16[576,256]{1,0:T(8,128)(2,1)}, f32[256,576]{1,0:T(8,128)}, bf16[256,576]{1,0:T(8,128)(2,1)}, f32[1,576]{1,0:T(1,128)}, bf16[2,2,4,752,128]{4,3,2,1,...) custom-call(s32[4]{0:T(128)} %pad_add_fusion.1.where_ref.where, bf16[256,576]{1,0:T(8,128)(2,1)} %get-tuple-element.82.refs_0_, ...), custom_call_target="tpu_custom_call" | custom-call | flops 1 | bytes 1024 | tf_op jit(solution)/shard_map/mlp/pallas_call | solution.py:74
  96.0 11.8 %attend_back.1 = (f32[256,576]{1,0:T(8,128)}, bf16[256,384]{1,0:T(8,128)(2,1)}, bf16[256,384]{1,0:T(8,128)(2,1)}, bf16[256,384]{1,0:T(8,128)(2,1)}, bf16[256,384]{1,0:T(8,128)(2,1)}) custom-call(s32[4]{0:T(128)} %pad_add_fusion.1.where_ref.where, bf16[256,576]{1,0:T(8,128)(2,1)} %copy-done.2, bf16[256,576]{1,0:T(8,128)(2,1)} %get-tuple-element.87.refs_1_, ...), custom_call_target="tpu_custom_call" | custom-call | flops 1 | bytes 1024 | tf_op jit(solution)/shard_map/attend_back/pallas_call | solution.py:74
  107.8 3.6 %add_convert_fusion = (bf16[1,2,4,752,128]{4,3,2,1,0:T(8,128)(2,1)S(1)}, bf16[2,4,752,128]{3,2,1,0:T(8,128)(2,1)S(1)}) fusion(bf16[2,2,4,752,128]{4,3,2,1,0:T(8,128)(2,1)} %collective-permute-done.17, bf16[2,2,4,752,128]{4,3,2,1,0:T(8,128)(2,1)} %get-tuple-element.100), kind=kLoop, calls=%fused_computation.1 | loop fusion | flops 6160384 | bytes 9240576 | tf_op jit(solution)/shard_map/convert_element_type | solution.py:109
  111.5 1.6 collective-permute-start.18
  113.0 1.3 collective-permute-start.19
  114.3 1.3 collective-permute-start.20
  115.6 1.6 collective-permute-start.21
  117.2 4.6 %collective-permute-done.19.refs_1_ = bf16[256,384]{1,0:T(8,128)(2,1)S(1)} collective-permute-done((bf16[256,384]{1,0:T(8,128)(2,1)S(1)}, bf16[256,384]{1,0:T(8,128)(2,1)S(1)}, u32[]{:S(2)}, u32[]{:S(2)}) %collective-permute-start.19) | collective-permute-done | bytes 196640 | tf_op jit(solution)/shard_map/ppermute | solution.py:891
  121.8 14.6 %collective-permute-done.20.refs_2_ = bf16[256,384]{1,0:T(8,128)(2,1)S(1)} collective-permute-done((bf16[256,384]{1,0:T(8,128)(2,1)S(1)}, bf16[256,384]{1,0:T(8,128)(2,1)S(1)}, u32[]{:S(2)}, u32[]{:S(2)}) %collective-permute-start.20) | collective-permute-done | bytes 196640 | tf_op jit(solution)/shard_map/ppermute | solution.py:891
  136.9 1.0 collective-permute-start.22
  137.9 6.8 %last.1 = (f32[576,256]{1,0:T(8,128)}, bf16[4,4,160,128]{3,2,1,0:T(8,128)(2,1)S(1)}, bf16[4,4,160,128]{3,2,1,0:T(8,128)(2,1)S(1)}) custom-call(s32[4]{0:T(128)S(1)} %copy-done.12, f32[256,576]{1,0:T(8,128)S(1)} %copy-done.5, f32[256,768]{1,0:T(8,128)S(1)} %get-tuple-element.95.raw, bf16[256,576]{1,0:T(8,128)(2,1)S(1)} %copy-done.9, ...), custom_call_target="tpu_custom_call" | custom-call | flops 1 | bytes 1024 | tf_op jit(solution)/shard_map/last/pallas_call | solution.py:709
  144.8 4.0 %collective-permute-done.22 = bf16[4,752,128]{2,1,0:T(8,128)(2,1)S(1)} collective-permute-done((bf16[4,752,128]{2,1,0:T(8,128)(2,1)S(1)}, bf16[4,752,128]{2,1,0:T(8,128)(2,1)S(1)}, u32[]{:S(2)}, u32[]{:S(2)}) %collective-permute-start.22) | collective-permute-done | bytes 770080 | tf_op jit(solution)/shard_map/ppermute | solution.py:105
  149.0 3.8 %collective-permute-start.25 = (bf16[752,128]{1,0:T(8,128)(2,1)S(1)}, bf16[752,128]{1,0:T(8,128)(2,1)S(1)}, u32[]{:S(2)}, u32[]{:S(2)}) collective-permute-start(bf16[752,128]{1,0:T(8,128)(2,1)S(1)} %get-tuple-element.140), channel_id=1, source_target_pairs={{0,3},{1,0},{2,1},{3,2},{4,7},{5,4},{6,5},{7,6},{8,11},{9,8},{10,9... | collective-permute-start | bytes 577544 | tf_op jit(solution)/shard_map/ppermute | solution.py:95
  153.0 1.9 collective-permute-start.29
  154.9 1.1 collective-permute-start.28
  156.0 2.4 %collective-permute-done.23 = bf16[752,128]{1,0:T(8,128)(2,1)S(1)} collective-permute-done((bf16[752,128]{1,0:T(8,128)(2,1)S(1)}, bf16[752,128]{1,0:T(8,128)(2,1)S(1)}, u32[]{:S(2)}, u32[]{:S(2)}) %collective-permute-start.23) | collective-permute-done | bytes 192544 | tf_op jit(solution)/shard_map/ppermute | solution.py:95
  158.5 1.5 collective-permute-start.27
  159.9 3.1 %collective-permute-done.25 = bf16[752,128]{1,0:T(8,128)(2,1)S(1)} collective-permute-done((bf16[752,128]{1,0:T(8,128)(2,1)S(1)}, bf16[752,128]{1,0:T(8,128)(2,1)S(1)}, u32[]{:S(2)}, u32[]{:S(2)}) %collective-permute-start.25) | collective-permute-done | bytes 192544 | tf_op jit(solution)/shard_map/ppermute | solution.py:95
  163.1 4.8 %collective-permute-done.24 = bf16[752,128]{1,0:T(8,128)(2,1)S(1)} collective-permute-done((bf16[752,128]{1,0:T(8,128)(2,1)S(1)}, bf16[752,128]{1,0:T(8,128)(2,1)S(1)}, u32[]{:S(2)}, u32[]{:S(2)}) %collective-permute-start.24) | collective-permute-done | bytes 192544 | tf_op jit(solution)/shard_map/ppermute | solution.py:95
  168.2 1.7 collective-permute-start.31
  169.9 2.1 %collective-permute-start.32 = (bf16[160,128]{1,0:T(8,128)(2,1)S(1)}, bf16[160,128]{1,0:T(8,128)(2,1)S(1)}, u32[]{:S(2)}, u32[]{:S(2)}) collective-permute-start(bf16[160,128]{1,0:T(8,128)(2,1)S(1)} %get-tuple-element.121), channel_id=1, source_target_pairs={{0,3},{1,0},{2,1},{3,2},{4,7},{5,4},{6,5},{7,6},{8,11},{9,8},{10,9... | collective-permute-start | bytes 122888 | tf_op jit(solution)/shard_map/ppermute | solution.py:95
  172.1 2.1 %collective-permute-done.30 = bf16[160,128]{1,0:T(8,128)(2,1)S(1)} collective-permute-done((bf16[160,128]{1,0:T(8,128)(2,1)S(1)}, bf16[160,128]{1,0:T(8,128)(2,1)S(1)}, u32[]{:S(2)}, u32[]{:S(2)}) %collective-permute-start.30) | collective-permute-done | bytes 40992 | tf_op jit(solution)/shard_map/ppermute | solution.py:95
  174.7 1.6 collective-permute-start.34
  176.2 1.0 collective-permute-start.33
  177.2 1.0 collective-permute-start.35
  178.2 5.0 %collective-permute-done.34 = bf16[912,128]{1,0:T(8,128)(2,1)S(1)} collective-permute-done((bf16[912,128]{1,0:T(8,128)(2,1)S(1)}, bf16[912,128]{1,0:T(8,128)(2,1)S(1)}, u32[]{:S(2)}, u32[]{:S(2)}) %collective-permute-start.34) | collective-permute-done | bytes 233504 | tf_op jit(solution)/shard_map/ppermute | solution.py:90
  183.3 3.7 %collective-permute-done.33 = bf16[912,128]{1,0:T(8,128)(2,1)S(1)} collective-permute-done((bf16[912,128]{1,0:T(8,128)(2,1)S(1)}, bf16[912,128]{1,0:T(8,128)(2,1)S(1)}, u32[]{:S(2)}, u32[]{:S(2)}) %collective-permute-start.33) | collective-permute-done | bytes 233504 | tf_op jit(solution)/shard_map/ppermute | solution.py:90
  187.2 2.5 %collective-permute-done.36.refs_1_ = bf16[4,912,128]{2,1,0:T(8,128)(2,1)S(1)} collective-permute-done((bf16[4,912,128]{2,1,0:T(8,128)(2,1)S(1)}, bf16[4,912,128]{2,1,0:T(8,128)(2,1)S(1)}, u32[]{:S(2)}, u32[]{:S(2)}) %collective-permute-start.36) | collective-permute-done | bytes 933920 | tf_op jit(solution)/shard_map/ppermute | solution.py:90
  189.7 0.9 copy-done.15
  190.6 4.2 %unpack.1 = (f32[144,1536]{1,0:T(8,128)}, f32[144,1536]{1,0:T(8,128)}, f32[576,384]{1,0:T(8,128)}, f32[144,576]{1,0:T(8,128)}, f32[144,576]{1,0:T(8,128)}, /*ind...) custom-call(s32[4]{0:T(128)} %pad_add_fusion.1.where_ref.where, ...), custom_call_target="tpu_custom_call" | custom-call | flops 1 | bytes 1024 | tf_op jit(solution)/shard_map/unpack/pallas_call | solution.py:74
  (112 shorter events, 4.3 us)
Async XLA Ops:
  8.7 11.6 %collective-permute-start.7 = (bf16[160,128]{1,0:T(8,128)(2,1)}, bf16[160,128]{1,0:T(8,128)(2,1)S(1)}, u32[]{:S(2)}, u32[]{:S(2)}) collective-permute-start(bf16[160,128]{1,0:T(8,128)(2,1)} %pack_first.1), channel_id=1, source_target_pairs={{0,3},{1,0},{2,1},{3,2},{4,7},{5,4},{6,5},{7,6},{8,11},{9,8},{10,9... | collective-permute-start | bytes 122888 | tf_op jit(solution)/shard_map/ppermute | solution.py:95
  13.8 6.6 %collective-permute-start.6 = (bf16[160,128]{1,0:T(8,128)(2,1)}, bf16[160,128]{1,0:T(8,128)(2,1)S(1)}, u32[]{:S(2)}, u32[]{:S(2)}) collective-permute-start(bf16[160,128]{1,0:T(8,128)(2,1)} %pack_first.1), channel_id=1, source_target_pairs={{0,2},{1,3},{2,0},{3,1},{4,6},{5,7},{6,4},{7,5},{8,10},{9,11},{10,... | collective-permute-start | bytes 122888 | tf_op jit(solution)/shard_map/ppermute | solution.py:95
  13.8 6.6 %collective-permute-start.5 = (bf16[160,128]{1,0:T(8,128)(2,1)}, bf16[160,128]{1,0:T(8,128)(2,1)S(1)}, u32[]{:S(2)}, u32[]{:S(2)}) collective-permute-start(bf16[160,128]{1,0:T(8,128)(2,1)} %pack_first.1), channel_id=1, source_target_pairs={{0,1},{1,2},{2,3},{3,0},{4,5},{5,6},{6,7},{7,4},{8,9},{9,10},{10,1... | collective-permute-start | bytes 122888 | tf_op jit(solution)/shard_map/ppermute | solution.py:95
  14.8 9.4 %collective-permute-start.2 = (bf16[752,128]{1,0:T(8,128)(2,1)}, bf16[752,128]{1,0:T(8,128)(2,1)S(1)}, u32[]{:S(2)}, u32[]{:S(2)}) collective-permute-start(bf16[752,128]{1,0:T(8,128)(2,1)} %pack_second.1), channel_id=1, source_target_pairs={{0,3},{1,0},{2,1},{3,2},{4,7},{5,4},{6,5},{7,6},{8,11},{9,8},{10,9... | collective-permute-start | bytes 577544 | tf_op jit(solution)/shard_map/ppermute | solution.py:95
  17.6 18.2 %collective-permute-start.1 = (bf16[752,128]{1,0:T(8,128)(2,1)}, bf16[752,128]{1,0:T(8,128)(2,1)S(1)}, u32[]{:S(2)}, u32[]{:S(2)}) collective-permute-start(bf16[752,128]{1,0:T(8,128)(2,1)} %pack_second.1), channel_id=1, source_target_pairs={{0,2},{1,3},{2,0},{3,1},{4,6},{5,7},{6,4},{7,5},{8,10},{9,11},{10,... | collective-permute-start | bytes 577544 | tf_op jit(solution)/shard_map/ppermute | solution.py:95
  20.4 15.5 %collective-permute-start = (bf16[752,128]{1,0:T(8,128)(2,1)}, bf16[752,128]{1,0:T(8,128)(2,1)S(1)}, u32[]{:S(2)}, u32[]{:S(2)}) collective-permute-start(bf16[752,128]{1,0:T(8,128)(2,1)} %pack_second.1), channel_id=1, source_target_pairs={{0,1},{1,2},{2,3},{3,0},{4,5},{5,6},{6,7},{7,4},{8,9},{9,10},{10,1... | collective-permute-start | bytes 577544 | tf_op jit(solution)/shard_map/ppermute | solution.py:95
  21.2 18.5 %collective-permute-start.9 = (bf16[4,144,128]{2,1,0:T(8,128)(2,1)S(1)}, bf16[4,144,128]{2,1,0:T(8,128)(2,1)S(1)}, u32[]{:S(2)}, u32[]{:S(2)}) collective-permute-start(bf16[4,144,128]{2,1,0:T(8,128)(2,1)S(1)} %get-tuple-element.155), channel_id=1, source_target_pairs={{0,8},{4,12},{8,0},{12,4},{16,24},{20,28},{24,16},{28,20},{1,9},{5... | collective-permute-start | bytes 442376 | tf_op jit(solution)/shard_map/ppermute | solution.py:90
  22.7 16.9 %collective-permute-start.8 = (bf16[4,144,128]{2,1,0:T(8,128)(2,1)S(1)}, bf16[4,144,128]{2,1,0:T(8,128)(2,1)S(1)}, u32[]{:S(2)}, u32[]{:S(2)}) collective-permute-start(bf16[4,144,128]{2,1,0:T(8,128)(2,1)S(1)} %get-tuple-element.155), channel_id=1, source_target_pairs={{0,16},{4,20},{8,24},{12,28},{16,0},{20,4},{24,8},{28,12},{1,17},{... | collective-permute-start | bytes 442376 | tf_op jit(solution)/shard_map/ppermute | solution.py:90
  24.3 15.4 %collective-permute-start.10 = (bf16[4,144,128]{2,1,0:T(8,128)(2,1)S(1)}, bf16[4,144,128]{2,1,0:T(8,128)(2,1)S(1)}, u32[]{:S(2)}, u32[]{:S(2)}) collective-permute-start(bf16[4,144,128]{2,1,0:T(8,128)(2,1)S(1)} %get-tuple-element.155), channel_id=1, source_target_pairs={{0,24},{4,28},{8,16},{12,20},{16,8},{20,12},{24,0},{28,4},{1,25},{... | collective-permute-start | bytes 442376 | tf_op jit(solution)/shard_map/ppermute | solution.py:90
  35.9 6.7 %copy-start = (bf16[256,576]{0,1:T(8,128)(2,1)S(1)}, bf16[256,576]{0,1:T(8,128)(2,1)}, u32[]{:S(2)}) copy-start(bf16[256,576]{0,1:T(8,128)(2,1)} %param.14) | copy-start | bytes 884740
  35.9 6.7 %copy-start.11 = (s32[4]{0:T(128)S(1)}, s32[4]{0:T(128)}, u32[]{:S(2)}) copy-start(s32[4]{0:T(128)} %pad_add_fusion.1.where_ref.where) | copy-start | bytes 52
  38.1 15.8 %collective-permute-start.3 = (bf16[4,752,128]{2,1,0:T(8,128)(2,1)}, bf16[4,752,128]{2,1,0:T(8,128)(2,1)}, u32[]{:S(2)}, u32[]{:S(2)}) collective-permute-start(bf16[4,752,128]{2,1,0:T(8,128)(2,1)} %get-tuple-element.147), channel_id=1, source_target_pairs={{0,16},{4,12},{8,24},{12,4},{16,0},{20,28},{24,8},{28,20},{1,17},{... | collective-permute-start | bytes 2310152 | tf_op jit(solution)/shard_map/ppermute | solution.py:105
  39.7 2.1 %collective-permute-start.11 = (bf16[4,4,144,128]{3,2,1,0:T(8,128)(2,1)S(1)}, bf16[4,4,144,128]{3,2,1,0:T(8,128)(2,1)S(1)}, u32[]{:S(2)}, u32[]{:S(2)}) collective-permute-start(bf16[4,4,144,128]{3,2,1,0:T(8,128)(2,1)S(1)} %pad_maximum_fusion.3.near), channel_id=1, source_target_pairs={{0,4},{4,0},{8,12},{12,8},{16,20},{20,16},{24,28},{28,24},{1,5},{5... | collective-permute-start | bytes 1769480 | tf_op jit(solution)/shard_map/ppermute | solution.py:90
  41.8 0.8 copy-start.6
  42.6 1.1 copy-start.7
  48.6 7.9 %copy-start.2 = (bf16[256,576]{1,0:T(8,128)(2,1)}, bf16[256,576]{1,0:T(8,128)(2,1)S(1)}, u32[]{:S(2)}) copy-start(bf16[256,576]{1,0:T(8,128)(2,1)S(1)} %get-tuple-element.74.refs_0_) | copy-start | bytes 884740
  48.7 7.9 %copy-start.3 = (bf16[256,384]{1,0:T(8,128)(2,1)}, bf16[256,384]{1,0:T(8,128)(2,1)S(1)}, u32[]{:S(2)}) copy-start(bf16[256,384]{1,0:T(8,128)(2,1)S(1)} %get-tuple-element.76.refs_3_.refs_2_) | copy-start | bytes 589828
  48.7 7.9 %copy-start.8 = (bf16[256,576]{1,0:T(8,128)(2,1)}, bf16[256,576]{1,0:T(8,128)(2,1)S(1)}, u32[]{:S(2)}) copy-start(bf16[256,576]{1,0:T(8,128)(2,1)S(1)} %get-tuple-element.96.normed) | copy-start | bytes 884740
  48.7 9.5 %collective-permute-start.14 = (bf16[256,384]{1,0:T(8,128)(2,1)S(1)}, bf16[256,384]{1,0:T(8,128)(2,1)S(1)}, u32[]{:S(2)}, u32[]{:S(2)}) collective-permute-start(bf16[256,384]{1,0:T(8,128)(2,1)S(1)} %get-tuple-element.76.refs_3_.refs_2_), channel_id=1, source_target_pairs={{0,3},{4,7},{8,11},{12,15},{16,19},{20,23},{24,27},{28,31}} | collective-permute-start | bytes 589832 | tf_op jit(solution)/shard_map/ppermute | solution.py:873
  50.0 9.5 %collective-permute-start.13 = (bf16[256,384]{1,0:T(8,128)(2,1)S(1)}, bf16[256,384]{1,0:T(8,128)(2,1)S(1)}, u32[]{:S(2)}, u32[]{:S(2)}) collective-permute-start(bf16[256,384]{1,0:T(8,128)(2,1)S(1)} %get-tuple-element.76.refs_3_.refs_2_), channel_id=1, source_target_pairs={{0,2},{1,3},{4,6},{5,7},{8,10},{9,11},{12,14},{13,15},{16,18},{17,... | collective-permute-start | bytes 589832 | tf_op jit(solution)/shard_map/ppermute | solution.py:873
  52.4 10.8 %collective-permute-start.12 = (bf16[256,384]{1,0:T(8,128)(2,1)S(1)}, bf16[256,384]{1,0:T(8,128)(2,1)S(1)}, u32[]{:S(2)}, u32[]{:S(2)}) collective-permute-start(bf16[256,384]{1,0:T(8,128)(2,1)S(1)} %get-tuple-element.76.refs_3_.refs_2_), channel_id=1, source_target_pairs={{0,1},{1,2},{2,3},{4,5},{5,6},{6,7},{8,9},{9,10},{10,11},{12,13},{... | collective-permute-start | bytes 589832 | tf_op jit(solution)/shard_map/ppermute | solution.py:873
  56.6 20.4 %collective-permute-start.4 = (bf16[2,4,752,128]{3,2,1,0:T(8,128)(2,1)}, bf16[2,4,752,128]{3,2,1,0:T(8,128)(2,1)}, u32[]{:S(2)}, u32[]{:S(2)}) collective-permute-start(bf16[2,4,752,128]{3,2,1,0:T(8,128)(2,1)} %pad_maximum_fusion.refs_4_), channel_id=1, source_target_pairs={{0,8},{4,20},{8,0},{12,28},{16,24},{20,4},{24,16},{28,12},{1,9},{5... | collective-permute-start | bytes 4620296 | tf_op jit(solution)/shard_map/ppermute | solution.py:105
  58.2 6.5 %copy-start.16 = (bf16[256,384]{1,0:T(8,128)(2,1)}, bf16[256,384]{1,0:T(8,128)(2,1)S(1)}, u32[]{:S(2)}) copy-start(bf16[256,384]{1,0:T(8,128)(2,1)S(1)} %collective-permute-done.14.refs_6_.refs_5_) | copy-start | bytes 589828
  59.5 5.2 %copy-start.17 = (bf16[256,384]{1,0:T(8,128)(2,1)}, bf16[256,384]{1,0:T(8,128)(2,1)S(1)}, u32[]{:S(2)}) copy-start(bf16[256,384]{1,0:T(8,128)(2,1)S(1)} %collective-permute-done.13.refs_5_.refs_4_) | copy-start | bytes 589828
  63.2 1.5 copy-start.18
  63.2 13.8 %collective-permute-start.15 = (bf16[2,4,752,128]{3,2,1,0:T(8,128)(2,1)}, bf16[2,4,752,128]{3,2,1,0:T(8,128)(2,1)}, u32[]{:S(2)}, u32[]{:S(2)}) collective-permute-start(bf16[2,4,752,128]{3,2,1,0:T(8,128)(2,1)} %pad_maximum_fusion.refs_4_), channel_id=1, source_target_pairs={{0,4},{4,0},{8,12},{12,8},{16,20},{20,16},{24,28},{28,24},{1,5},{5... | collective-permute-start | bytes 4620296 | tf_op jit(solution)/shard_map/ppermute | solution.py:90
  77.1 3.7 %collective-permute-start.16 = (bf16[2,4,752,128]{3,2,1,0:T(8,128)(2,1)}, bf16[2,4,752,128]{3,2,1,0:T(8,128)(2,1)}, u32[]{:S(2)}, u32[]{:S(2)}) collective-permute-start(bf16[2,4,752,128]{3,2,1,0:T(8,128)(2,1)} %collective-permute-done.4.refs_5_), channel_id=1, source_target_pairs={{0,4},{4,0},{8,12},{12,8},{16,20},{20,16},{24,28},{28,24},{1,5},{5... | collective-permute-start | bytes 4620296 | tf_op jit(solution)/shard_map/ppermute | solution.py:90
  95.8 12.0 %collective-permute-start.17 = (bf16[2,2,4,752,128]{4,3,2,1,0:T(8,128)(2,1)}, bf16[2,2,4,752,128]{4,3,2,1,0:T(8,128)(2,1)}, u32[]{:S(2)}, u32[]{:S(2)}) collective-permute-start(bf16[2,2,4,752,128]{4,3,2,1,0:T(8,128)(2,1)} %get-tuple-element.86), channel_id=1, source_target_pairs={{0,4},{4,0},{8,12},{12,8},{16,20},{20,16},{24,28},{28,24},{1,5},{5... | collective-permute-start | bytes 9240584 | tf_op jit(solution)/shard_map/ppermute | solution.py:90
  107.8 5.2 %copy-start.21 = (bf16[256,384]{1,0:T(8,128)(2,1)S(1)}, bf16[256,384]{1,0:T(8,128)(2,1)}, u32[]{:S(2)}) copy-start(bf16[256,384]{1,0:T(8,128)(2,1)} %get-tuple-element.103) | copy-start | bytes 589828
  107.8 6.5 %copy-start.20 = (bf16[256,384]{1,0:T(8,128)(2,1)S(1)}, bf16[256,384]{1,0:T(8,128)(2,1)}, u32[]{:S(2)}) copy-start(bf16[256,384]{1,0:T(8,128)(2,1)} %get-tuple-element.104) | copy-start | bytes 589828
  107.8 7.8 %copy-start.19 = (bf16[256,384]{1,0:T(8,128)(2,1)S(1)}, bf16[256,384]{1,0:T(8,128)(2,1)}, u32[]{:S(2)}) copy-start(bf16[256,384]{1,0:T(8,128)(2,1)} %get-tuple-element.105) | copy-start | bytes 589828
  111.5 24.9 %collective-permute-start.18 = (bf16[2,4,752,128]{3,2,1,0:T(8,128)(2,1)S(1)}, bf16[2,4,752,128]{3,2,1,0:T(8,128)(2,1)S(1)}, u32[]{:S(2)}, u32[]{:S(2)}) collective-permute-start(bf16[2,4,752,128]{3,2,1,0:T(8,128)(2,1)S(1)} %get-tuple-element.136), channel_id=1, source_target_pairs={{0,8},{4,20},{8,0},{12,28},{16,24},{20,4},{24,16},{28,12},{1,9},{5... | collective-permute-start | bytes 4620296 | tf_op jit(solution)/shard_map/ppermute | solution.py:105
  113.0 8.8 %collective-permute-start.19 = (bf16[256,384]{1,0:T(8,128)(2,1)S(1)}, bf16[256,384]{1,0:T(8,128)(2,1)S(1)}, u32[]{:S(2)}, u32[]{:S(2)}) collective-permute-start(bf16[256,384]{1,0:T(8,128)(2,1)S(1)} %copy-done.21), channel_id=1, source_target_pairs={{1,0},{2,1},{3,2},{5,4},{6,5},{7,6},{9,8},{10,9},{11,10},{13,12},{... | collective-permute-start | bytes 589832 | tf_op jit(solution)/shard_map/ppermute | solution.py:891
  114.3 22.1 %collective-permute-start.20 = (bf16[256,384]{1,0:T(8,128)(2,1)S(1)}, bf16[256,384]{1,0:T(8,128)(2,1)S(1)}, u32[]{:S(2)}, u32[]{:S(2)}) collective-permute-start(bf16[256,384]{1,0:T(8,128)(2,1)S(1)} %copy-done.20), channel_id=1, source_target_pairs={{2,0},{3,1},{6,4},{7,5},{10,8},{11,9},{14,12},{15,13},{18,16},{19,... | collective-permute-start | bytes 589832 | tf_op jit(solution)/shard_map/ppermute | solution.py:891
  115.6 20.8 %collective-permute-start.21 = (bf16[256,384]{1,0:T(8,128)(2,1)S(1)}, bf16[256,384]{1,0:T(8,128)(2,1)S(1)}, u32[]{:S(2)}, u32[]{:S(2)}) collective-permute-start(bf16[256,384]{1,0:T(8,128)(2,1)S(1)} %copy-done.19), channel_id=1, source_target_pairs={{3,0},{7,4},{11,8},{15,12},{19,16},{23,20},{27,24},{31,28}} | collective-permute-start | bytes 589832 | tf_op jit(solution)/shard_map/ppermute | solution.py:891
  136.4 1.5 copy-start.1
  136.4 1.5 copy-start.4
  136.4 1.5 copy-start.5
  136.4 1.5 copy-start.9
  136.4 1.5 copy-start.10
  136.5 1.5 copy-start.12
  136.5 1.5 copy-start.13
  136.9 11.9 %collective-permute-start.22 = (bf16[4,752,128]{2,1,0:T(8,128)(2,1)S(1)}, bf16[4,752,128]{2,1,0:T(8,128)(2,1)S(1)}, u32[]{:S(2)}, u32[]{:S(2)}) collective-permute-start(bf16[4,752,128]{2,1,0:T(8,128)(2,1)S(1)} %get-tuple-element.137), channel_id=1, source_target_pairs={{0,16},{4,12},{8,24},{12,4},{16,0},{20,28},{24,8},{28,20},{1,17},{... | collective-permute-start | bytes 2310152 | tf_op jit(solution)/shard_map/ppermute | solution.py:105
  148.8 4.0 %collective-permute-start.26 = (bf16[4,4,160,128]{3,2,1,0:T(8,128)(2,1)S(1)}, bf16[4,4,160,128]{3,2,1,0:T(8,128)(2,1)S(1)}, u32[]{:S(2)}, u32[]{:S(2)}) collective-permute-start(bf16[4,4,160,128]{3,2,1,0:T(8,128)(2,1)S(1)} %get-tuple-element.116), channel_id=1, source_target_pairs={{0,4},{4,0},{8,12},{12,8},{16,20},{20,16},{24,28},{28,24},{1,5},{5... | collective-permute-start | bytes 1966088 | tf_op jit(solution)/shard_map/ppermute | solution.py:90
  148.9 9.5 %collective-permute-start.23 = (bf16[752,128]{1,0:T(8,128)(2,1)S(1)}, bf16[752,128]{1,0:T(8,128)(2,1)S(1)}, u32[]{:S(2)}, u32[]{:S(2)}) collective-permute-start(bf16[752,128]{1,0:T(8,128)(2,1)S(1)} %get-tuple-element.139), channel_id=1, source_target_pairs={{0,1},{1,2},{2,3},{3,0},{4,5},{5,6},{6,7},{7,4},{8,9},{9,10},{10,1... | collective-permute-start | bytes 577544 | tf_op jit(solution)/shard_map/ppermute | solution.py:95
  149.0 14.0 %collective-permute-start.25 = (bf16[752,128]{1,0:T(8,128)(2,1)S(1)}, bf16[752,128]{1,0:T(8,128)(2,1)S(1)}, u32[]{:S(2)}, u32[]{:S(2)}) collective-permute-start(bf16[752,128]{1,0:T(8,128)(2,1)S(1)} %get-tuple-element.140), channel_id=1, source_target_pairs={{0,3},{1,0},{2,1},{3,2},{4,7},{5,4},{6,5},{7,6},{8,11},{9,8},{10,9... | collective-permute-start | bytes 577544 | tf_op jit(solution)/shard_map/ppermute | solution.py:95
  152.8 15.1 %collective-permute-start.24 = (bf16[752,128]{1,0:T(8,128)(2,1)S(1)}, bf16[752,128]{1,0:T(8,128)(2,1)S(1)}, u32[]{:S(2)}, u32[]{:S(2)}) collective-permute-start(bf16[752,128]{1,0:T(8,128)(2,1)S(1)} %get-tuple-element.141), channel_id=1, source_target_pairs={{0,2},{1,3},{2,0},{3,1},{4,6},{5,7},{6,4},{7,5},{8,10},{9,11},{10,... | collective-permute-start | bytes 577544 | tf_op jit(solution)/shard_map/ppermute | solution.py:95
  153.0 15.0 %collective-permute-start.29 = (bf16[4,160,128]{2,1,0:T(8,128)(2,1)S(1)}, bf16[4,160,128]{2,1,0:T(8,128)(2,1)S(1)}, u32[]{:S(2)}, u32[]{:S(2)}) collective-permute-start(bf16[4,160,128]{2,1,0:T(8,128)(2,1)S(1)} %get-tuple-element.143), channel_id=1, source_target_pairs={{0,24},{4,28},{8,16},{12,20},{16,8},{20,12},{24,0},{28,4},{1,25},{... | collective-permute-start | bytes 491528 | tf_op jit(solution)/shard_map/ppermute | solution.py:90
  154.9 13.1 %collective-permute-start.28 = (bf16[4,160,128]{2,1,0:T(8,128)(2,1)S(1)}, bf16[4,160,128]{2,1,0:T(8,128)(2,1)S(1)}, u32[]{:S(2)}, u32[]{:S(2)}) collective-permute-start(bf16[4,160,128]{2,1,0:T(8,128)(2,1)S(1)} %get-tuple-element.144), channel_id=1, source_target_pairs={{0,16},{4,20},{8,24},{12,28},{16,0},{20,4},{24,8},{28,12},{1,17},{... | collective-permute-start | bytes 491528 | tf_op jit(solution)/shard_map/ppermute | solution.py:90
  158.5 9.6 %collective-permute-start.27 = (bf16[4,160,128]{2,1,0:T(8,128)(2,1)S(1)}, bf16[4,160,128]{2,1,0:T(8,128)(2,1)S(1)}, u32[]{:S(2)}, u32[]{:S(2)}) collective-permute-start(bf16[4,160,128]{2,1,0:T(8,128)(2,1)S(1)} %get-tuple-element.145), channel_id=1, source_target_pairs={{0,8},{4,12},{8,0},{12,4},{16,24},{20,28},{24,16},{28,20},{1,9},{5... | collective-permute-start | bytes 491528 | tf_op jit(solution)/shard_map/ppermute | solution.py:90
  168.2 6.0 %collective-permute-start.30 = (bf16[160,128]{1,0:T(8,128)(2,1)S(1)}, bf16[160,128]{1,0:T(8,128)(2,1)S(1)}, u32[]{:S(2)}, u32[]{:S(2)}) collective-permute-start(bf16[160,128]{1,0:T(8,128)(2,1)S(1)} %get-tuple-element.119), channel_id=1, source_target_pairs={{0,1},{1,2},{2,3},{3,0},{4,5},{5,6},{6,7},{7,4},{8,9},{9,10},{10,1... | collective-permute-start | bytes 122888 | tf_op jit(solution)/shard_map/ppermute | solution.py:95
  168.2 5.9 %collective-permute-start.31 = (bf16[160,128]{1,0:T(8,128)(2,1)S(1)}, bf16[160,128]{1,0:T(8,128)(2,1)S(1)}, u32[]{:S(2)}, u32[]{:S(2)}) collective-permute-start(bf16[160,128]{1,0:T(8,128)(2,1)S(1)} %get-tuple-element.120), channel_id=1, source_target_pairs={{0,2},{1,3},{2,0},{3,1},{4,6},{5,7},{6,4},{7,5},{8,10},{9,11},{10,... | collective-permute-start | bytes 122888 | tf_op jit(solution)/shard_map/ppermute | solution.py:95
  169.9 4.7 %collective-permute-start.32 = (bf16[160,128]{1,0:T(8,128)(2,1)S(1)}, bf16[160,128]{1,0:T(8,128)(2,1)S(1)}, u32[]{:S(2)}, u32[]{:S(2)}) collective-permute-start(bf16[160,128]{1,0:T(8,128)(2,1)S(1)} %get-tuple-element.121), channel_id=1, source_target_pairs={{0,3},{1,0},{2,1},{3,2},{4,7},{5,4},{6,5},{7,6},{8,11},{9,8},{10,9... | collective-permute-start | bytes 122888 | tf_op jit(solution)/shard_map/ppermute | solution.py:95
  174.7 8.6 %collective-permute-start.34 = (bf16[912,128]{1,0:T(8,128)(2,1)S(1)}, bf16[912,128]{1,0:T(8,128)(2,1)S(1)}, u32[]{:S(2)}, u32[]{:S(2)}) collective-permute-start(bf16[912,128]{1,0:T(8,128)(2,1)S(1)} %get-tuple-element.153), channel_id=1, source_target_pairs={{0,8},{4,12},{8,0},{12,4},{16,24},{20,28},{24,16},{28,20},{1,9},{5... | collective-permute-start | bytes 700424 | tf_op jit(solution)/shard_map/ppermute | solution.py:90
  176.2 10.8 %collective-permute-start.33 = (bf16[912,128]{1,0:T(8,128)(2,1)S(1)}, bf16[912,128]{1,0:T(8,128)(2,1)S(1)}, u32[]{:S(2)}, u32[]{:S(2)}) collective-permute-start(bf16[912,128]{1,0:T(8,128)(2,1)S(1)} %get-tuple-element.153), channel_id=1, source_target_pairs={{0,16},{4,20},{8,24},{12,28},{16,0},{20,4},{24,8},{28,12},{1,17},{... | collective-permute-start | bytes 700424 | tf_op jit(solution)/shard_map/ppermute | solution.py:90
  177.2 9.8 %collective-permute-start.35 = (bf16[912,128]{1,0:T(8,128)(2,1)S(1)}, bf16[912,128]{1,0:T(8,128)(2,1)S(1)}, u32[]{:S(2)}, u32[]{:S(2)}) collective-permute-start(bf16[912,128]{1,0:T(8,128)(2,1)S(1)} %get-tuple-element.153), channel_id=1, source_target_pairs={{0,24},{4,28},{8,16},{12,20},{16,8},{20,12},{24,0},{28,4},{1,25},{... | collective-permute-start | bytes 700424 | tf_op jit(solution)/shard_map/ppermute | solution.py:90
  187.1 2.6 %copy-start.14 = (bf16[4,912,128]{2,1,0:T(8,128)(2,1)}, bf16[4,912,128]{2,1,0:T(8,128)(2,1)S(1)}, u32[]{:S(2)}) copy-start(bf16[4,912,128]{2,1,0:T(8,128)(2,1)S(1)} %pad_maximum_fusion.1.refs_0_) | copy-start | bytes 2801668
  187.1 2.6 %collective-permute-start.36 = (bf16[4,912,128]{2,1,0:T(8,128)(2,1)S(1)}, bf16[4,912,128]{2,1,0:T(8,128)(2,1)S(1)}, u32[]{:S(2)}, u32[]{:S(2)}) collective-permute-start(bf16[4,912,128]{2,1,0:T(8,128)(2,1)S(1)} %pad_maximum_fusion.1.refs_0_), channel_id=1, source_target_pairs={{0,4},{4,0},{8,12},{12,8},{16,20},{20,16},{24,28},{28,24},{1,5},{5... | collective-permute-start | bytes 2801672 | tf_op jit(solution)/shard_map/ppermute | solution.py:90
  189.7 1.0 copy-start.15
where the time goes:
time: 196 us; the launch traced here: 195 us
  waiting for transfers between devices  69.7 us (36%)
  Pallas kernels  57.4 us (29%)
  starting transfers between devices  45.6 us (23%)
  other arithmetic  14 us (7%)
  local copies, waits for them, and re-layouts  6.87 us (4%)
    pallas_call x6, Pallas kernels, staged_call(): pl.pallas_call(whole, out_shape=out_shape, in_specs=[smem()] + [hbm()] *...  45.6 us
    ppermute x12, waiting for transfers between devices, shift(): lax.ppermute(value, 'grp', [(i, (i + step) % count) for i in range(count)])  23 us
    ppermute x3, waiting for transfers between devices, body(): kv_back.append(lax.ppermute(kv_parts[step], 'grp', behind))  19.2 us
    ppermute x12, starting transfers between devices, shift(): lax.ppermute(value, 'grp', [(i, (i + step) % count) for i in range(count)])  17.8 us
    ppermute x15, waiting for transfers between devices, hop(): return lax.ppermute(value, 'rep', [(i, i ^ bit) for i in range(count)])  15.3 us
    ppermute x15, starting transfers between devices, hop(): return lax.ppermute(value, 'rep', [(i, i ^ bit) for i in range(count)])  12.9 us
    ppermute x4, waiting for transfers between devices, hop_split(): lax.ppermute(value, 'rep', [(i, i ^ (odd if i % 2 else even)) for i in ra...  7.17 us
    pallas_call x1, Pallas kernels, run_last(): pl.pallas_call(functools.partial(last_kernel, sizes), out_shape=(shape((w...  6.82 us
  transfers between devices with their start and end apart: 37, of which 17 were waited for; matrix products, arithmetic and copies ran while one was open for 6% of the time, Pallas kernels for 17%

commit v1 on v0

v1 whole, which is shorter than its diff:
```python
import functools

import jax
import jax.numpy as jnp
from jax import lax
from jax.experimental import pallas as pl
from jax.experimental.pallas import tpu as pltpu
from jax.sharding import PartitionSpec as P

NORM_EPS = 1e-05
ROPE_BASE = 100000.0
LANES = 128
SMALL = 16
MIB = 1024 * 1024
BIG = 58


def vmem():
    return pl.BlockSpec(memory_space=pltpu.VMEM)


def smem():
    return pl.BlockSpec(memory_space=pltpu.SMEM)


def hbm():
    return pl.BlockSpec(memory_space=pl.ANY)


def shape(dims, kind):
    return jax.ShapeDtypeStruct(dims, kind)


def options(mebibytes):
    return pltpu.CompilerParams(vmem_limit_bytes=mebibytes * MIB)


def cost():
    return pl.CostEstimate(flops=1, bytes_accessed=1024, transcendentals=0)


class Staged:
    def __init__(self, source, target, sem):
        self.copy = pltpu.make_async_copy(source, target, sem)
        self.copy.start()
        self.target, self.waiting = target, True
        self.shape, self.dtype = target.shape, target.dtype

    def wait(self):
        if self.waiting:
            self.copy.wait()
            self.waiting = False

    def __getitem__(self, index):
        self.wait()
        return self.target[index]


def staged_call(kernel, name, operands, out_shape, out_specs, scratch, mebibytes):
    kinds = [kind for kind, _ in operands]
    staged = [array for kind, array in operands if kind == "staged"]
    count = len(operands)

    def whole(*refs):
        sources, refs = refs[:count], refs[count:]
        if staged:
            targets, sems = refs[len(refs) - len(staged) - 1 : -1], refs[-1]
            refs = refs[: len(refs) - len(staged) - 1]
        given, at = [], 0
        for kind, source in zip(kinds, sources):
            if kind == "staged":
                source = Staged(source, targets[at], sems.at[at])
                at += 1
            given.append(source)
        kernel(*given, *refs)
        for operand in given:
            if isinstance(operand, Staged):
                operand.wait()

    specs = {"smem": smem, "vmem": vmem, "hbm": hbm, "staged": hbm}
    more = [pltpu.VMEM(array.shape, array.dtype) for array in staged]
    if staged:
        more.append(pltpu.SemaphoreType.DMA((len(staged),)))
    return pl.pallas_call(
        whole,
        out_shape=out_shape,
        in_specs=[specs[kind]() for kind in kinds],
        out_specs=out_specs,
        scratch_shapes=list(scratch) + more,
        compiler_params=options(mebibytes),
        cost_estimate=cost(),
        name=name,
    )(*[array for _, array in operands])


def kept(kind, *arrays):
    return [(kind, array) for array in arrays]


def hop(value, bit):
    count = lax.axis_size("rep")
    return lax.ppermute(value, "rep", [(i, i ^ bit) for i in range(count)])


def shift(value, step):
    count = lax.axis_size("grp")
    return lax.ppermute(value, "grp", [(i, (i + step) % count) for i in range(count)])


def rep_bits():
    index = lax.axis_index("rep")
    return index & 1, (index >> 1) & 1, (index >> 2) & 1


def hop_split(value, even, odd):
    count = lax.axis_size("rep")
    return lax.ppermute(value, "rep", [(i, i ^ (odd if i % 2 else even)) for i in range(count)])


def add_low(*values):
    total = values[0].astype(jnp.float32)
    for value in values[1:]:
        total = total + value.astype(jnp.float32)
    return total.astype(values[0].dtype)


def fold_grp(parts):
    f32 = jnp.float32
    total = parts[0].astype(f32)
    for step in range(1, len(parts)):
        total = total + shift(parts[step], step).astype(f32)
    total = total.astype(parts[0].dtype)
    bit = 8
    while bit < lax.axis_size("rep"):
        total = add_low(total, hop(total, bit))
        bit *= 2
    return total


def fold_blocks(keep, got):
    f32 = jnp.float32
    sums = [add_low(keep[j], got[j]) for j in range(4)]
    across, along, both = hop(sums[2], 2), hop(sums[1], 4), hop(sums[3], 6)
    return [
        (
            sums[0][d].astype(f32)
            + across[d].astype(f32)
            + along[d].astype(f32)
            + both[d].astype(f32)
        ).astype(keep.dtype)
        for d in range(lax.axis_size("grp"))
    ]


def spread_chip(own):
    return jnp.stack([own, hop(own, 4), hop(own, 2), hop(own, 6)])


def rows_of(vector, count):
    short = count * LANES - vector.shape[0]
    return jnp.pad(vector, (0, short)).reshape(count, LANES)


def lined(rows, length):
    return rows.reshape(rows.shape[0], -1)[:, :length].reshape(1, -1)


def place_scalars():
    bit_c, bit_x, bit_y = rep_bits()
    return jnp.stack([lax.axis_index("grp"), bit_c, bit_x, bit_y]).astype(jnp.int32)


def piece_row(where, core, high, low, rows):
    owner = where[1] ^ core
    first = jnp.where(owner == 0, where[2], where[3])
    second = jnp.where(owner == 0, where[3], where[2])
    index = owner * 4 + (first ^ high) * 2 + (second ^ low)
    return pl.multiple_of(index * (rows // 8), 16)


def piece_list():
    return [(c, h, l) for c in range(2) for h in range(2) for l in range(2)]


def dot(one, two, contract=(1, 0)):
    return lax.dot_general(
        one, two, (((contract[0],), (contract[1],)), ((), ())), preferred_element_type=jnp.float32
    )


def turned(value):
    return value.astype(jnp.float32).T.astype(value.dtype)


class Chunk:
    def __init__(self, dims, out_first):
        self.shard, self.width, self.own, self.groups = dims
        self.out_blocks = -(-self.width // LANES)
        self.rows_at, self.share_end, at = {}, [], 0

        def out_rows(at):
            for j in range(self.out_blocks):
                self.rows_at["out", j] = at
                at += self.shard
            return at

        if out_first:
            at = out_rows(at)
        self.out_end = at
        for share in range(self.own):
            for kind in ("gate", "up"):
                for f in self.blocks(share):
                    self.rows_at[kind, f] = at
                    at += self.shard
            self.rows_at["down", share] = at
            at += self.width
            self.share_end.append(at)
        if not out_first:
            at = out_rows(at)
        self.used = at
        self.rows = -(-at // 128) * 128
        self.part = self.rows // 8

    def blocks(self, share):
        return [owner * self.own + share for owner in range(self.groups)]


def chunks_of(shard, width, own_hidden, groups):
    dims = (shard, width, own_hidden // LANES, groups)
    return Chunk(dims, True), Chunk(dims, False)


def pack_kernel(chunk, where, query, key, value, gate, up, down_t, output, first, second, blocks, pack):
    shard, width = chunk.shard, chunk.width
    whole = jnp.concatenate([query[...], key[...], value[...]], 1)
    for j in range(blocks.shape[0]):
        stop = min((j + 1) * LANES, whole.shape[1])
        blocks[j, :, : stop - j * LANES] = whole[:, j * LANES : stop]
        if stop < (j + 1) * LANES:
            blocks[j, :, stop - j * LANES :] = jnp.zeros(
                (shard, (j + 1) * LANES - stop), whole.dtype
            )
    first[...] = blocks[where[1] * 4 + where[2] * 2 + where[3]]
    for (kind, j), at in chunk.rows_at.items():
        if kind == "down":
            pack[at : at + width, :] = down_t[:, j * LANES : (j + 1) * LANES]
            continue
        source = {"gate": gate, "up": up, "out": output}[kind]
        stop = min((j + 1) * LANES, source.shape[1])
        pack[at : at + shard, : stop - j * LANES] = source[:, j * LANES : stop]
        if stop < (j + 1) * LANES:
            pack[at : at + shard, stop - j * LANES :] = jnp.zeros(
                (shard, (j + 1) * LANES - stop), pack.dtype
            )
    if chunk.used < chunk.rows:
        pack[chunk.used :, :] = jnp.zeros((chunk.rows - chunk.used, LANES), pack.dtype)
    row = piece_row(where, 0, 0, 0, chunk.rows)
    second[...] = pack[pl.ds(row, chunk.part), :]


def run_pack(where, chunk, query, key, value, gate, up, down_t, output):
    kind = gate.dtype
    return staged_call(
        functools.partial(pack_kernel, chunk),
        "pack",
        kept("smem", where) + kept("staged", query, key, value, gate, up, down_t, output),
        (shape((chunk.shard, LANES), kind), shape((chunk.part, LANES), kind)),
        (vmem(), vmem()),
        [pltpu.VMEM((8, chunk.shard, LANES), kind), pltpu.VMEM((chunk.rows, LANES), kind)],
        BIG,
    )


def block_at(where, core, across, along):
    return (where[1] ^ core) * 4 + (where[2] ^ across) * 2 + (where[3] ^ along)


def unit_heads(raw, head_size):
    pairs = []
    for at in range(0, raw.shape[1], head_size):
        head = raw[:, at : at + head_size]
        factor = lax.rsqrt(jnp.mean(head * head, axis=1, keepdims=True) + NORM_EPS)
        pairs.append((head * factor, factor))
    return pairs


def proj_kernel(sizes, where, near, far, tokens_t, gain, head_gains, cosine, sine, *refs):
    f32, bf16 = jnp.float32, jnp.bfloat16
    q_width, kv_width, head_size = sizes
    normed_out, raw_out, query_out, kv_out, weights_out = refs
    groups = near.shape[1]
    inputs = tokens_t[...].astype(f32).T
    scale = lax.rsqrt(jnp.mean(inputs * inputs, axis=1, keepdims=True) + NORM_EPS)
    normed = (inputs * scale * gain[...]).astype(bf16)
    normed_out[...] = normed
    for j in range(8):
        core, across, along = j // 4, j // 2 % 2, j % 2
        place = (where[2] ^ across) * 2 + (where[3] ^ along)
        pieces = []
        for owner in range(groups):
            behind = lax.rem(where[0] + groups - owner, groups)
            pieces.append(
                jnp.where(where[1] == core, near[place, behind], far[place, behind])
            )
        weights_out[:, j * LANES : (j + 1) * LANES] = jnp.concatenate(pieces, 0)
    flat = weights_out[...]
    raw = dot(normed, flat)
    raw_out[...] = raw[:, : q_width + kv_width]
    half = head_size // 2
    cos, sin = cosine[...], sine[...]

    def turn(head):
        one, two = head[:, :half], head[:, half:]
        return jnp.concatenate([one * cos - two * sin, two * cos + one * sin], 1)

    heads = []
    for at, (unit, _) in enumerate(unit_heads(raw[:, : q_width + kv_width], head_size)):
        row = 0 if at * head_size < q_width else 1
        heads.append(turn(unit * head_gains[row : row + 1, :]).astype(bf16))
    queries = jnp.concatenate(heads[: q_width // head_size], 1)
    query_out[...] = (queries.astype(f32) * head_size ** (-0.5)).astype(bf16)
    values = raw[:, q_width + kv_width : q_width + 2 * kv_width].astype(bf16)
    kv_out[...] = jnp.concatenate(heads[q_width // head_size :] + [values], 1)


def run_proj(where, near, far, tokens_t, gain, head_gains, cosine, sine, sizes):
    f32, bf16 = jnp.float32, jnp.bfloat16
    q_width, kv_width, _ = sizes
    width, toks = tokens_t.shape
    return staged_call(
        functools.partial(proj_kernel, sizes),
        "proj",
        kept("smem", where)
        + kept("vmem", near, far)
        + kept("staged", tokens_t)
        + kept("vmem", gain, head_gains, cosine, sine),
        (
            shape((toks, width), bf16),
            shape((toks, q_width + kv_width), f32),
            shape((toks, q_width), bf16),
            shape((toks, 2 * kv_width), bf16),
            shape((width, 8 * LANES), bf16),
        ),
        (vmem(),) * 5,
        (),
        24,
    )


def attend_kernel(sizes, query, own_seg, key_seg, *refs):
    f32, bf16 = jnp.float32, jnp.bfloat16
    q_width, kv_width, head_size = sizes
    held = refs[: len(refs) - 6]
    attended, exact, probs_out, bias, probs, sems = refs[len(refs) - 6 :]
    toks = query.shape[0]
    same = own_seg[...] == key_seg[...]
    order = lax.broadcasted_iota(jnp.int32, same.shape, 0) - lax.broadcasted_iota(
        jnp.int32, same.shape, 1
    )
    later = lax.broadcasted_iota(jnp.int32, same.shape, 1) >= toks
    bias[...] = jnp.where(same & ((order >= 0) | later), 0.0, -1e30)
    outs = []
    per = q_width // kv_width
    for g in range(kv_width // head_size):
        cols = slice(g * head_size, (g + 1) * head_size)
        keys = jnp.concatenate([kv[:, cols] for kv in held], 0)
        cols = slice(kv_width + g * head_size, kv_width + (g + 1) * head_size)
        values = jnp.concatenate([kv[:, cols] for kv in held], 0)
        for head in range(g * per, (g + 1) * per):
            scores = dot(query[:, head * head_size : (head + 1) * head_size], keys, (1, 1))
            scores = scores + bias[...]
            powers = jnp.exp(scores)
            share = 1.0 / jnp.sum(powers, axis=1, keepdims=True)
            low = (powers * share).astype(bf16)
            probs[head] = low
            pltpu.make_async_copy(probs.at[head], probs_out.at[head], sems.at[head]).start()
            outs.append(dot(low, values))
    whole = jnp.concatenate(outs, 1)
    exact[...] = whole
    attended[...] = whole.astype(bf16)
    for head in range(probs.shape[0]):
        pltpu.make_async_copy(probs.at[head], probs_out.at[head], sems.at[head]).wait()


def run_attend(query, own_seg, key_seg, held, sizes):
    bf16 = jnp.bfloat16
    q_width, kv_width, head_size = sizes
    toks = query.shape[0]
    keys = toks * len(held)
    heads = q_width // head_size
    return staged_call(
        functools.partial(attend_kernel, sizes),
        "attend",
        kept("staged", query, own_seg, key_seg, *held),
        (
            shape((toks, q_width), bf16),
            shape((toks, q_width), jnp.float32),
            shape((heads, toks, keys), bf16),
        ),
        (vmem(), vmem(), hbm()),
        [
            pltpu.VMEM((toks, keys), jnp.float32),
            pltpu.VMEM((heads, toks, keys), bf16),
            pltpu.SemaphoreType.DMA((heads,)),
        ],
        BIG,
    )


def attend_back_kernel(sizes, query, grad, exact, *refs):
    f32, bf16 = jnp.float32, jnp.bfloat16
    q_width, kv_width, head_size = sizes
    probs, sems = refs[-2:]
    refs = refs[:-2]
    groups = (len(refs) - 2) // 2
    probs_in = refs[groups]
    refs = refs[:groups] + refs[groups + 1 :]
    copies = [
        pltpu.make_async_copy(probs_in.at[head], probs.at[head], sems.at[head])
        for head in range(probs.shape[0])
    ]
    for copy in copies:
        copy.start()
    held = refs[:groups]
    query_grad = refs[groups]
    kv_grads = refs[groups + 1 :]
    toks = query.shape[0]
    per = q_width // kv_width
    query_t = query[...].astype(f32).T.astype(bf16)
    grad_t = grad[...].astype(f32).T.astype(bf16)
    outs, key_parts, value_parts = [], [], []
    for g in range(kv_width // head_size):
        cols = slice(g * head_size, (g + 1) * head_size)
        keys = jnp.concatenate([kv[:, cols] for kv in held], 0)
        cols = slice(kv_width + g * head_size, kv_width + (g + 1) * head_size)
        values = jnp.concatenate([kv[:, cols] for kv in held], 0)
        key_t = value_t = None
        for head in range(g * per, (g + 1) * per):
            cols = slice(head * head_size, (head + 1) * head_size)
            copies[head].wait()
            low = probs[head]
            inner = jnp.sum(grad[:, cols].astype(f32) * exact[:, cols], axis=1, keepdims=True)
            scores = dot(grad[:, cols], values, (1, 1)) - inner
            scores = (low.astype(f32) * scores).astype(bf16)
            outs.append(dot(scores, keys))
            key_one = dot(query_t[cols, :], scores)
            value_one = dot(grad_t[cols, :], low)
            key_t = key_one if key_t is None else key_t + key_one
            value_t = value_one if value_t is None else value_t + value_one
        key_parts.append(key_t)
        value_parts.append(value_t)
    query_grad[...] = jnp.concatenate(outs, 1) * head_size ** (-0.5)
    both = jnp.concatenate(key_parts + value_parts, 0)
    for at, out in enumerate(kv_grads):
        out[...] = both[:, at * toks : (at + 1) * toks].T.astype(out.dtype)


def run_attend_back(query, grad, exact, probs, held, sizes):
    f32, bf16 = jnp.float32, jnp.bfloat16
    q_width, kv_width, head_size = sizes
    toks = query.shape[0]
    keys = toks * len(held)
    return staged_call(
        functools.partial(attend_back_kernel, sizes),
        "attend_back",
        kept("staged", query, grad, exact, *held) + kept("hbm", probs),
        (shape((toks, q_width), f32),) + tuple(shape((toks, 2 * kv_width), bf16) for _ in held),
        (vmem(),) * (1 + len(held)),
        [pltpu.VMEM(probs.shape, bf16), pltpu.SemaphoreType.DMA((probs.shape[0],))],
        BIG,
    )


def mlp_kernel(w_chunk, g_chunk, where, attended, tokens_t, out_grad_t, gain, *refs):
    f32, bf16 = jnp.float32, jnp.bfloat16
    pieces, refs = refs[:4], refs[4:]
    layer_out_t, mixed_grad, attended_grad, gain_grad, keep, send = refs[:6]
    weights, grads, sem_in, sem_out = refs[6:]
    width, toks = tokens_t.shape
    shard, groups, out_blocks = w_chunk.shard, w_chunk.groups, w_chunk.out_blocks

    def piece_place(number):
        core = number // 4
        first, second = (where[2], where[3]) if core == 0 else (where[3], where[2])
        return where[1] ^ core, first ^ (number // 2 % 2), second ^ (number % 2)

    for number in range(8):
        core, high, low = piece_place(number)
        for place in range(4):

            @pl.when(core * 2 + high == place)
            def _(number=number, low=low, place=place):
                pltpu.make_async_copy(
                    pieces[place].at[low],
                    weights.at[:, pl.ds(number * w_chunk.part, w_chunk.part)],
                    sem_in.at[number],
                ).start()

    waited = 0

    def need(rows):
        nonlocal waited
        while waited < 8 and waited * w_chunk.part < rows:
            here = weights.at[:, pl.ds(waited * w_chunk.part, w_chunk.part)]
            pltpu.make_async_copy(here, here, sem_in.at[waited]).wait()
            waited += 1

    left = 0

    def leave(rows):
        nonlocal left
        while left < 8 and (left + 1) * g_chunk.part <= rows:
            core, high, low = piece_place(left)
            for away, out in ((0, keep), (1, send)):

                @pl.when(core == away)
                def _(number=left, high=high, low=low, away=away, out=out):
                    pltpu.make_async_copy(
                        grads.at[:, pl.ds(number * g_chunk.part, g_chunk.part)],
                        out.at[high, low],
                        sem_out.at[away],
                    ).start()

            left += 1

    behind = [lax.rem(where[0] + groups - owner, groups) for owner in range(groups)]
    ahead_of = [lax.rem(owner + groups - where[0], groups) for owner in range(groups)]

    def column(kind, f):
        at = w_chunk.rows_at[kind, f]
        return jnp.concatenate([weights[place, at : at + shard, :] for place in behind], 0)

    def store(kind, f, block):
        at = g_chunk.rows_at[kind, f]
        for owner in range(groups):
            grads[ahead_of[owner], at : at + shard, :] = block[owner * shard : (owner + 1) * shard]

    out_t = out_grad_t[...]
    upstream = turned(out_t)
    inputs = tokens_t[...].astype(f32).T
    att_t = turned(attended[...])
    if g_chunk.used < g_chunk.rows:
        grads[:, g_chunk.used :, :] = jnp.zeros(
            (groups, g_chunk.rows - g_chunk.used, LANES), bf16
        )
    need(w_chunk.out_end)
    output_w = jnp.concatenate([column("out", j) for j in range(out_blocks)], 1)[:, :width]
    mixed = inputs + dot(attended[...], output_w)
    scale = lax.rsqrt(jnp.mean(mixed * mixed, axis=1, keepdims=True) + NORM_EPS)
    unit = mixed * scale
    gained = gain[...]
    normed = (unit * gained).astype(bf16)
    normed_t = turned(normed)
    back = jnp.zeros(mixed.shape, f32)
    ahead = mixed
    for share in range(w_chunk.own):
        need(w_chunk.share_end[share])
        blocks = w_chunk.blocks(share)
        down_at = w_chunk.rows_at["down", share]
        down_to = g_chunk.rows_at["down", share]
        for pair in range(0, len(blocks), 2):
            some = blocks[pair : pair + 2]
            gate_w = jnp.concatenate([column("gate", f) for f in some], 1)
            up_w = jnp.concatenate([column("up", f) for f in some], 1)
            down_w = jnp.concatenate(
                [weights[behind[f // w_chunk.own], down_at : down_at + width, :] for f in some], 1
            )
            gate = dot(normed, gate_w)
            up = dot(normed, up_w)
            hidden_grad = dot(upstream, down_w)
            sigmoid = 1.0 / (1.0 + jnp.exp(-gate))
            silu = gate * sigmoid
            hidden = (silu * up).astype(bf16)
            gate_low = (hidden_grad * up * (sigmoid * (1.0 + gate * (1.0 - sigmoid)))).astype(bf16)
            up_low = (hidden_grad * silu).astype(bf16)
            ahead = ahead + dot(hidden, down_w, (1, 1))
            back = back + dot(gate_low, gate_w, (1, 1)) + dot(up_low, up_w, (1, 1))
            gate_wg = dot(normed_t, gate_low).astype(bf16)
            up_wg = dot(normed_t, up_low).astype(bf16)
            down_wg = dot(out_t, hidden).astype(bf16)
            for at, f in enumerate(some):
                cols = slice(at * LANES, (at + 1) * LANES)
                store("gate", f, gate_wg[:, cols])
                store("up", f, up_wg[:, cols])
                grads[ahead_of[f // g_chunk.own], down_to : down_to + width, :] = down_wg[:, cols]
        leave(g_chunk.share_end[share])
    layer_out_t[...] = ahead.T.astype(bf16)
    gain_grad[...] = jnp.sum(back * unit, axis=0, keepdims=True)
    inner = back * gained
    through = scale * (inner - unit * jnp.mean(inner * unit, axis=1, keepdims=True))
    mixed_back = upstream.astype(f32) + through
    mixed_grad[...] = mixed_back
    branch = mixed_back.astype(bf16)
    attended_grad[...] = dot(branch, output_w, (1, 1)).astype(bf16)
    output_wg = dot(att_t, branch)
    for j in range(out_blocks):
        block = output_wg[:, j * LANES : min((j + 1) * LANES, width)]
        if block.shape[1] < LANES:
            block = jnp.concatenate(
                [block, jnp.zeros((block.shape[0], LANES - block.shape[1]), f32)], 1
            )
        store("out", j, block.astype(bf16))
    leave(g_chunk.rows)
    pltpu.make_async_copy(keep, keep, sem_out.at[0]).wait()
    pltpu.make_async_copy(send, send, sem_out.at[1]).wait()


def run_mlp(where, w_chunk, g_chunk, pieces, attended, tokens_t, out_grad_t, gain):
    f32, bf16 = jnp.float32, jnp.bfloat16
    groups = w_chunk.groups
    width, toks = tokens_t.shape
    packed = shape((2, 2, groups, g_chunk.part, LANES), bf16)
    return staged_call(
        functools.partial(mlp_kernel, w_chunk, g_chunk),
        "mlp",
        kept("smem", where) + kept("staged", attended, tokens_t, out_grad_t, gain) + kept("hbm", *pieces),
        (
            shape((width, toks), bf16),
            shape((toks, width), f32),
            shape((toks, width), bf16),
            shape((1, width), f32),
            packed,
            packed,
        ),
        (vmem(),) * 4 + (hbm(),) * 2,
        [pltpu.VMEM((groups, chunk.rows, LANES), bf16) for chunk in (w_chunk, g_chunk)]
        + [pltpu.SemaphoreType.DMA((8,)), pltpu.SemaphoreType.DMA((2,))],
        BIG,
    )


def heads_back(grad, raw, cos, sin, gain, head_size):
    half = head_size // 2
    lows, total = [], jnp.zeros((1, head_size), jnp.float32)
    for at, (unit, factor) in enumerate(unit_heads(raw, head_size)):
        at *= head_size
        one, two = grad[:, at : at + half], grad[:, at + half : at + head_size]
        back = jnp.concatenate([one * cos + two * sin, two * cos - one * sin], 1)
        total = total + jnp.sum(back * unit, axis=0, keepdims=True)
        inner = back * gain
        lows.append(factor * (inner - unit * jnp.mean(inner * unit, axis=1, keepdims=True)))
    return lows, total


def query_back_kernel(sizes, query_grad, raw, normed, head_gains, cosine, sine, weights, products, back, total):
    q_width, _, head_size = sizes
    lows, total[...] = heads_back(
        query_grad[...], raw[:, :q_width], cosine[...], sine[...], head_gains[0:1, :], head_size
    )
    low = jnp.concatenate(lows, 1).astype(products.dtype)
    back[...] = dot(low, weights[:, :q_width], (1, 1))
    products[...] = dot(turned(normed[...]), low).astype(products.dtype)


def run_query_back(query_grad, raw, normed, head_gains, cosine, sine, weights, sizes):
    f32 = jnp.float32
    q_width, _, head_size = sizes
    toks, width = normed.shape
    return staged_call(
        functools.partial(query_back_kernel, sizes),
        "query_back",
        kept("vmem", query_grad, raw, normed, head_gains, cosine, sine, weights),
        (shape((width, q_width), normed.dtype), shape((toks, width), f32), shape((1, head_size), f32)),
        (vmem(),) * 3,
        (),
        24,
    )


def last_kernel(sizes, where, products, back, q_total, raw, normed, tokens_t, mixed_grad, gain, head_gains, cosine, sine, weights, second, *refs):
    f32, bf16 = jnp.float32, jnp.bfloat16
    q_width, kv_width, head_size = sizes
    kv_parts = refs[: len(refs) - 4]
    token_grad_t, keep, send, grads = refs[len(refs) - 4 :]
    count, groups, rows, _ = grads.shape
    width, toks = tokens_t.shape
    shard = width // groups
    kv_grad = kv_parts[0][...].astype(f32)
    for part in kv_parts[1:]:
        kv_grad = kv_grad + part[...].astype(f32)
    lows, k_total = heads_back(
        kv_grad, raw[:, q_width:], cosine[...], sine[...], head_gains[1:2, :], head_size
    )
    low = jnp.concatenate(lows + [kv_grad[:, kv_width:]], 1).astype(bf16)
    short = count * LANES - q_width - 2 * kv_width
    pieces = [products[...], dot(turned(normed[...]), low).astype(bf16)]
    if short:
        pieces.append(jnp.zeros((width, short), bf16))
    blocks = jnp.concatenate(pieces, 1)
    for j in range(count):
        for owner in range(groups):
            grads[j, owner, :shard, :] = blocks[
                owner * shard : (owner + 1) * shard, j * LANES : (j + 1) * LANES
            ]
            grads[j, owner, shard:, :] = jnp.zeros((rows - shard, LANES), bf16)
    whole = back[...] + dot(low, weights[:, q_width : q_width + 2 * kv_width], (1, 1))
    inputs = tokens_t[...].astype(f32).T
    scale = lax.rsqrt(jnp.mean(inputs * inputs, axis=1, keepdims=True) + NORM_EPS)
    unit = inputs * scale
    first = jnp.sum(whole * unit, axis=0, keepdims=True)
    inner = whole * gain[...]
    whole = mixed_grad[...] + scale * (inner - unit * jnp.mean(inner * unit, axis=1, keepdims=True))
    token_grad_t[...] = whole.T

    def line(vector):
        short = LANES - vector.shape[1]
        return jnp.concatenate([vector, jnp.zeros((1, short), f32)], 1) if short else vector

    head_part = head_size // groups
    for owner in range(groups):
        lines = []
        for vector in (first, second[...]):
            mine = vector[:, owner * shard : (owner + 1) * shard]
            lines += [line(mine[:, at : at + LANES]) for at in range(0, shard, LANES)]
        for vector in (q_total[...], k_total):
            lines.append(line(vector[:, owner * head_part : (owner + 1) * head_part]))
        lines.append(jnp.zeros((rows - shard - len(lines), LANES), f32))
        grads[0, owner, shard:, :] = jnp.concatenate(lines, 0).astype(bf16)
    for core in range(2):
        for across in range(2):
            for along in range(2):
                block = block_at(where, core, across, along)
                for step in range(groups):
                    owner = lax.rem(where[0] + step, groups)
                    (send if core else keep)[across * 2 + along, step] = grads[block, owner]


def run_last(where, products, back, q_total, raw, normed, tokens_t, mixed_grad, gain, head_gains, cosine, sine, weights, second, kv_parts, sizes):
    width = tokens_t.shape[0]
    groups = lax.axis_size("grp")
    rows = width // groups + SMALL
    packed = shape((4, groups, rows, LANES), jnp.bfloat16)
    return staged_call(
        functools.partial(last_kernel, sizes),
        "last",
        kept("smem", where)
        + kept("vmem", products, back, q_total, raw, normed)
        + kept("staged", tokens_t)
        + kept("vmem", mixed_grad, gain, head_gains, cosine, sine, weights, second, *kv_parts),
        (shape(tokens_t.shape, jnp.float32), packed, packed),
        (vmem(),) * 3,
        [pltpu.VMEM((8, groups, rows, LANES), jnp.bfloat16)],
        24,
    )


def unpack_kernel(sizes, chunk, where, near, far, *refs):
    f32 = jnp.float32
    q_width, kv_width, _ = sizes
    gate, up, down_t, output, query, key, value = refs[:7]
    lines_out = refs[7:11]
    pack = refs[11]
    shard, width = chunk.shard, chunk.width
    projections = []
    small = None
    for core in range(2):
        for across in range(2):
            for along in range(2):
                place = (where[2] ^ across) * 2 + (where[3] ^ along)
                piece = jnp.where(where[1] == core, near[place], far[place])
                at = chunk.part
                high, low = (across, along) if core == 0 else (along, across)
                row = (core * 4 + high * 2 + low) * chunk.part
                pack[row : row + chunk.part, :] = piece[:at]
                projections.append(piece[at : at + shard])
                if small is None:
                    small = piece[at + shard :].astype(f32)
    for (kind, j), at in chunk.rows_at.items():
        if kind == "down":
            down_t[:, j * LANES : (j + 1) * LANES] = pack[at : at + width].astype(f32)
            continue
        out = {"gate": gate, "up": up, "out": output}[kind]
        stop = min((j + 1) * LANES, out.shape[1])
        out[:, j * LANES : stop] = pack[at : at + shard].astype(f32)[:, : stop - j * LANES]
    whole = jnp.concatenate(projections, 1).astype(f32)
    query[...] = whole[:, :q_width]
    key[...] = whole[:, q_width : q_width + kv_width]
    value[...] = whole[:, q_width + kv_width : q_width + 2 * kv_width]
    row = 0
    for out in lines_out:
        for at in range(0, out.shape[1], LANES):
            stop = min(at + LANES, out.shape[1])
            out[:, at:stop] = small[row : row + 1, : stop - at]
            row += 1


def run_unpack(where, chunk, sizes, near, far, hidden_width, own_hidden, head_part):
    f32 = jnp.float32
    q_width, kv_width, _ = sizes
    shard, width = chunk.shard, chunk.width
    return staged_call(
        functools.partial(unpack_kernel, sizes, chunk),
        "unpack",
        kept("smem", where) + kept("vmem", near, far),
        (
            shape((shard, hidden_width), f32),
            shape((shard, hidden_width), f32),
            shape((width, own_hidden), f32),
            shape((shard, width), f32),
            shape((shard, q_width), f32),
            shape((shard, kv_width), f32),
            shape((shard, kv_width), f32),
            shape((1, shard), f32),
            shape((1, shard), f32),
            shape((1, head_part), f32),
            shape((1, head_part), f32),
        ),
        (vmem(),) * 11,
        [pltpu.VMEM((chunk.rows, LANES), near.dtype)],
        24,
    )


def body(
    tokens,
    segments,
    out_grad,
    norm_gain,
    query_gain,
    key_gain,
    query_weight,
    key_weight,
    value_weight,
    output_weight,
    second_gain,
    gate_weight,
    up_weight,
    down_weight,
):
    f32, bf16 = jnp.float32, jnp.bfloat16
    groups = lax.axis_size("grp")
    place_z = lax.axis_index("grp")
    where = place_scalars()
    toks, width = tokens.shape
    shard = norm_gain.shape[0]
    head_part = query_gain.shape[0]
    head_size = head_part * groups
    hidden_width, own_hidden = gate_weight.shape[1], down_weight.shape[0]
    sizes = (query_weight.shape[1], key_weight.shape[1], head_size)
    w_chunk, g_chunk = chunks_of(shard, width, own_hidden, groups)
    tokens_t, out_grad_t = tokens.T, out_grad.T

    fence = lax.optimization_barrier
    own_first, own_second = run_pack(
        where, w_chunk, query_weight, key_weight, value_weight,
        gate_weight, up_weight, down_weight.T, output_weight,
    )
    first_z = [own_first] + [shift(own_first, step) for step in range(1, groups)]
    second_z = [own_second] + [shift(own_second, step) for step in range(1, groups)]

    gain_rows = -(-shard // LANES)
    seg_rows = -(-toks // LANES)
    _, segs = fence((own_first, segments))
    small = jnp.zeros((SMALL * LANES,), bf16)
    at = 0
    for line, count in (
        (norm_gain, gain_rows),
        (second_gain, gain_rows),
        (query_gain, 1),
        (key_gain, 1),
        (segs.astype(bf16), seg_rows),
    ):
        small = small + jnp.pad(line, (at, SMALL * LANES - at - line.shape[0]))
        at += count * LANES
    small = small.reshape(SMALL, LANES)
    small_behind = jnp.stack([small] + [shift(small, step) for step in range(1, groups)])

    small_behind = small_behind.astype(f32)
    small_all = small_behind[lax.rem(place_z + groups - jnp.arange(groups), groups)]
    at = 0
    gains = []
    for count, length in ((gain_rows, shard), (gain_rows, shard), (1, head_part), (1, head_part)):
        gains.append(lined(small_all[:, at : at + count], length))
        at += count
    gain_first, gain_second, gain_query, gain_key = gains
    head_gains = jnp.concatenate([gain_query, gain_key])
    segs = small_behind[:, at : at + seg_rows].reshape(groups, -1)[:, :toks]
    there = (place_z >= jnp.arange(groups))[:, None]
    key_seg = jnp.where(there, segs, -1.0).reshape(1, -1)
    own_seg = segs[0][:, None]
    earlier = ((key_seg < own_seg) & (key_seg >= 0.0)).astype(jnp.int32)
    positions = place_z * toks + jnp.arange(toks, dtype=jnp.int32) - jnp.sum(earlier, axis=1)
    half = head_size // 2
    inverse = ROPE_BASE ** (-(jnp.arange(half, dtype=f32) * 2.0 / head_size))
    angles = positions.astype(f32)[:, None] * inverse[None, :]
    cosine, sine = jnp.cos(angles), jnp.sin(angles)

    near = spread_chip(jnp.stack(first_z))
    near, second_z = fence((near, second_z))
    whole = jnp.stack(second_z)
    near, gain_first, gain_second, head_gains, cosine, sine, own_seg, key_seg = fence(
        (near, gain_first, gain_second, head_gains, cosine, sine, own_seg, key_seg)
    )
    normed, raw, query, key_value, proj_weights = run_proj(
        where, near, hop(near, 1), tokens_t, gain_first, head_gains, cosine, sine, sizes
    )
    held = [key_value]
    for step in range(1, groups):
        ahead = [(i, i + step) for i in range(groups - step)]
        held.append(lax.ppermute(key_value, "grp", ahead))
    whole = jnp.stack([whole, hop_split(whole, 4, 2)])
    far_whole = hop_split(whole, 2, 4)
    whole, held = fence((whole, held))
    other = hop(whole, 1)
    attended, exact, probs = run_attend(query, own_seg, key_seg, held, sizes)
    far_whole, attended, other = fence((far_whole, attended, other))
    pieces = [whole, far_whole, other, hop(far_whole, 1)]
    layer_out_t, mixed_grad, attended_grad, second_sum, keep, send = run_mlp(
        where, w_chunk, g_chunk, pieces, attended, tokens_t, out_grad_t, gain_second
    )
    got = hop(send, 1)
    query_grad, *kv_parts = run_attend_back(query, attended_grad, exact, probs, held, sizes)
    got, query_grad, kv_parts = fence((got, query_grad, kv_parts))
    kv_back = [kv_parts[0]]
    for step in range(1, groups):
        back = [(i + step, i) for i in range(groups - step)]
        kv_back.append(lax.ppermute(kv_parts[step], "grp", back))
    near_got = hop_split(add_low(keep[1], got[1]), 2, 4)
    query_parts = run_query_back(
        query_grad, raw, normed, head_gains, cosine, sine, proj_weights, sizes
    )
    near_got, kv_back, query_parts = fence((near_got, kv_back, query_parts))
    far_got = hop_split(add_low(keep[0, 1], got[0, 1], near_got[1]), 4, 2)
    token_grad_t, late_keep, late_send = run_last(
        where, *query_parts, raw, normed, tokens_t, mixed_grad, gain_first, head_gains, cosine, sine,
        proj_weights, second_sum, kv_back, sizes,
    )
    late_got = hop(late_send, 1)
    far_got, late_got = fence((far_got, late_got))
    early = fold_grp(
        [add_low(keep[0, 0, d], got[0, 0, d], near_got[0, d], far_got[d]) for d in range(groups)]
    )
    late = fold_blocks(late_keep, late_got)
    near = spread_chip(jnp.concatenate([early, fold_grp(late)]))
    far = hop(near, 1)
    (
        gate_sum, up_sum, down_sum_t, output_sum, query_sum, key_sum, value_sum,
        first_sum, second_sum, query_gsum, key_gsum,
    ) = run_unpack(where, g_chunk, sizes, near, far, hidden_width, own_hidden, head_part)
    return (
        layer_out_t.T,
        token_grad_t.T,
        first_sum.reshape(-1),
        query_gsum.reshape(-1),
        key_gsum.reshape(-1),
        query_sum,
        key_sum,
        value_sum,
        output_sum,
        second_sum.reshape(-1),
        gate_sum,
        up_sum,
        down_sum_t.T,
    )


def solution(mesh):
    placed = (
        P(("rep", "grp"), None),
        P(("rep", "grp")),
        P(("rep", "grp"), None),
        P("grp"),
        P("grp"),
        P("grp"),
        P("grp", None),
        P("grp", None),
        P("grp", None),
        P("grp", None),
        P("grp"),
        P("grp", None),
        P("grp", None),
        P("grp", None),
    )
    return jax.shard_map(
        body,
        mesh=mesh,
        in_specs=placed,
        out_specs=(
            P(("rep", "grp"), None),
            P(("rep", "grp"), None),
            P("grp"),
            P("grp"),
            P("grp"),
            P("grp", None),
            P("grp", None),
            P("grp", None),
            P("grp", None),
            P("grp"),
            P("grp", None),
            P("grp", None),
            P("grp", None),
        ),
        check_vma=False,
    )
```

time: 196 us -> 189 us (0.964)
  starting transfers between devices: 45.6 us -> 61.5 us
  waiting for transfers between devices: 69.7 us -> 57.3 us
  Pallas kernels: 57.4 us -> 51.1 us
  local copies, waits for them, and re-layouts: 6.87 us -> 3.73 us
    ppermute x12 -> x15, waiting for transfers between devices: 23 us -> 6.01 us  [shift(): lax.ppermute(value, 'grp', [(i, (i + step) % count) for i in range(count)])]
    ppermute x12 -> x15, starting transfers between devices: 17.8 us -> 29.1 us  [shift(): lax.ppermute(value, 'grp', [(i, (i + step) % count) for i in range(count)])]
    ppermute x15, waiting for transfers between devices: 15.3 us -> 24.9 us  [hop(): return lax.ppermute(value, 'rep', [(i, i ^ bit) for i in range(count)])]
    ppermute x3, waiting for transfers between devices: 19.2 us -> 12 us  [body(): kv_back.append(lax.ppermute(kv_parts[step], 'grp', back))]
    pallas_call x8, Pallas kernels: 57.4 us -> 51.1 us  [staged_call(): pl.pallas_call(whole, out_shape=out_shape, in_specs=[specs[kind]() for ki...]
    ppermute x4, waiting for transfers between devices: 7.17 us -> 10.1 us  [hop_split(): lax.ppermute(value, 'rep', [(i, i ^ (odd if i % 2 else even)) for i in ra...]
    ppermute x3, starting transfers between devices: 5.15 us -> 7.83 us  [body(): held.append(lax.ppermute(key_value, 'grp', ahead))]
    another operation x9 -> x0, local copies, waits for them, and re-layouts: 2.28 us -> none  [the longest x1 0.8 us: body(): own_seg = segs[0][:, None]]
  transfers between devices with their start and end apart: 37 -> 40, of which waited for: 17 -> 19; matrix products, arithmetic and copies ran while one was open for 6% -> 5% of each run, Pallas kernels for 17% -> 17%
where the time goes in v1:
time: 189 us; the launch traced here: 188 us
  starting transfers between devices  61.5 us (33%)
  waiting for transfers between devices  57.3 us (30%)
  Pallas kernels  51.1 us (27%)
  other arithmetic  13.6 us (7%)
  local copies, waits for them, and re-layouts  3.73 us (2%)
    pallas_call x8, Pallas kernels, staged_call(): pl.pallas_call(whole, out_shape=out_shape, in_specs=[specs[kind]() for ki...  51.1 us
    ppermute x15, starting transfers between devices, shift(): lax.ppermute(value, 'grp', [(i, (i + step) % count) for i in range(count)])  29.1 us
    ppermute x15, waiting for transfers between devices, hop(): return lax.ppermute(value, 'rep', [(i, i ^ bit) for i in range(count)])  24.9 us
    ppermute x15, starting transfers between devices, hop(): return lax.ppermute(value, 'rep', [(i, i ^ bit) for i in range(count)])  14.6 us
    ppermute x3, waiting for transfers between devices, body(): kv_back.append(lax.ppermute(kv_parts[step], 'grp', back))  12 us
    ppermute x4, waiting for transfers between devices, hop_split(): lax.ppermute(value, 'rep', [(i, i ^ (odd if i % 2 else even)) for i in ra...  10.1 us
    ppermute x3, starting transfers between devices, body(): held.append(lax.ppermute(key_value, 'grp', ahead))  7.83 us
    ppermute x4, starting transfers between devices, hop_split(): lax.ppermute(value, 'rep', [(i, i ^ (odd if i % 2 else even)) for i in ra...  6.09 us
  transfers between devices with their start and end apart: 40, of which 19 were waited for; matrix products, arithmetic and copies ran while one was open for 5% of the time, Pallas kernels for 17%

profile of v1, /device:TPU:0, one launch (start us, length us, event | category | flops | bytes accessed | tf_op | source)
XLA Modules:
  0.0 188.5 jit_solution(1348540496626945172)
XLA Ops:
  0.7 0.6 pad_add_fusion.1.refs_0_
  1.3 3.2 %pack.1 = (bf16[144,128]{1,0:T(8,128)(2,1)}, bf16[752,128]{1,0:T(8,128)(2,1)}) custom-call(s32[4]{0:T(128)} %pad_add_fusion.1.refs_0_, bf16[144,576]{1,0:T(8,128)(2,1)} %refs_1_.1, bf16[144,192]{1,0:T(8,128)(2,1)} %refs_2_.1, bf16[144,192]{1,0:T(8,128)(2,1)} %refs_3_.1, bf16[144,1536]{1,0:T(8,128)(2,1)} %refs_4_.1, bf16[144,1536]{1,0:T(8,128)(2,1)} %refs_5_.1, ...), custom_call_target="tpu_custom_call" | custom-call | flops 1 | bytes 1024 | tf_op jit(solution)/shard_map/pack/pallas_call | solution.py:84
  4.6 5.1 %collective-permute-start.13 = (bf16[16,128]{1,0:T(8,128)(2,1)S(1)}, bf16[16,128]{1,0:T(8,128)(2,1)S(1)}, u32[]{:S(2)}, u32[]{:S(2)}) collective-permute-start(bf16[16,128]{1,0:T(8,128)(2,1)S(1)} %get-tuple-element.190), channel_id=1, source_target_pairs={{0,3},{1,0},{2,1},{3,2},{4,7},{5,4},{6,5},{7,6},{8,11},{9,8},{10,9... | collective-permute-start | bytes 12296 | tf_op jit(solution)/shard_map/ppermute | solution.py:107
  9.7 1.0 collective-permute-start.11
  10.7 2.8 %collective-permute-start.2 = (bf16[144,128]{1,0:T(8,128)(2,1)}, bf16[144,128]{1,0:T(8,128)(2,1)S(1)}, u32[]{:S(2)}, u32[]{:S(2)}) collective-permute-start(bf16[144,128]{1,0:T(8,128)(2,1)} %get-tuple-element.89), channel_id=1, source_target_pairs={{0,3},{1,0},{2,1},{3,2},{4,7},{5,4},{6,5},{7,6},{8,11},{9,8},{10,9... | collective-permute-start | bytes 110600 | tf_op jit(solution)/shard_map/ppermute | solution.py:107
  13.5 1.1 collective-permute-start.1
  14.9 3.8 %collective-permute-start.8 = (bf16[752,128]{1,0:T(8,128)(2,1)}, bf16[752,128]{1,0:T(8,128)(2,1)S(1)}, u32[]{:S(2)}, u32[]{:S(2)}) collective-permute-start(bf16[752,128]{1,0:T(8,128)(2,1)} %get-tuple-element.91), channel_id=1, source_target_pairs={{0,3},{1,0},{2,1},{3,2},{4,7},{5,4},{6,5},{7,6},{8,11},{9,8},{10,9... | collective-permute-start | bytes 577544 | tf_op jit(solution)/shard_map/ppermute | solution.py:107
  20.2 0.7 collective-permute-start.6
  21.4 0.8 fusion.33
  22.2 1.6 collective-permute-start.4
  23.8 1.5 collective-permute-start.3
  25.3 2.7 %collective-permute-done.4 = bf16[4,144,128]{2,1,0:T(8,128)(2,1)S(1)} collective-permute-done((bf16[4,144,128]{2,1,0:T(8,128)(2,1)S(1)}, bf16[4,144,128]{2,1,0:T(8,128)(2,1)S(1)}, u32[]{:S(2)}, u32[]{:S(2)}) %collective-permute-start.4) | collective-permute-done | bytes 147488 | tf_op jit(solution)/shard_map/ppermute | solution.py:102
  27.9 3.5 %collective-permute-start.5 = (bf16[4,144,128]{2,1,0:T(8,128)(2,1)S(1)}, bf16[4,144,128]{2,1,0:T(8,128)(2,1)S(1)}, u32[]{:S(2)}, u32[]{:S(2)}) collective-permute-start(bf16[4,144,128]{2,1,0:T(8,128)(2,1)S(1)} %get-tuple-element.182), channel_id=1, source_target_pairs={{0,24},{4,28},{8,16},{12,20},{16,8},{20,12},{24,0},{28,4},{1,25},{... | collective-permute-start | bytes 442376 | tf_op jit(solution)/shard_map/ppermute | solution.py:102
  31.4 3.1 %collective-permute-done.5 = bf16[4,144,128]{2,1,0:T(8,128)(2,1)S(1)} collective-permute-done((bf16[4,144,128]{2,1,0:T(8,128)(2,1)S(1)}, bf16[4,144,128]{2,1,0:T(8,128)(2,1)S(1)}, u32[]{:S(2)}, u32[]{:S(2)}) %collective-permute-start.5) | collective-permute-done | bytes 147488 | tf_op jit(solution)/shard_map/ppermute | solution.py:102
  34.6 1.0 collective-permute-done.7
  35.6 1.3 fusion.34
  36.9 1.5 collective-permute-start.9
  38.4 0.6 broadcast_select_fusion.refs_2_
  39.2 0.7 reshape.259.refs_4_
  40.0 2.0 %collective-permute-done.14.refs_2_ = bf16[4,4,144,128]{3,2,1,0:T(8,128)(2,1)S(1)} collective-permute-done((bf16[4,4,144,128]{3,2,1,0:T(8,128)(2,1)S(1)}, bf16[4,4,144,128]{3,2,1,0:T(8,128)(2,1)S(1)}, u32[]{:S(2)}, u32[]{:S(2)}) %collective-permute-start.14) | collective-permute-done | bytes 589856 | tf_op jit(solution)/shard_map/ppermute | solution.py:102
  42.0 5.1 %proj.1 = (bf16[256,576]{1,0:T(8,128)(2,1)S(1)}, f32[256,768]{1,0:T(8,128)S(1)}, bf16[256,576]{1,0:T(8,128)(2,1)S(1)}, bf16[256,384]{1,0:T(8,128)(2,1)S(1)}, bf16[576,1024]{1,0:T(8,128)(2,1)S(1)}) custom-call(s32[4]{0:T(128)S(1)} %copy-done.7, bf16[4,4,144,128]{3,2,1,0:T(8,128)(2,1)S(1)} %pad_maximum_fusion.3.refs_1_, ...), custom_call_target="tpu_custom_call" | custom-call | flops 1 | bytes 1024 | tf_op jit(solution)/shard_map/proj/pallas_call | solution.py:84
  47.2 3.3 %collective-permute-start.17 = (bf16[256,384]{1,0:T(8,128)(2,1)S(1)}, bf16[256,384]{1,0:T(8,128)(2,1)S(1)}, u32[]{:S(2)}, u32[]{:S(2)}) collective-permute-start(bf16[256,384]{1,0:T(8,128)(2,1)S(1)} %get-tuple-element.106.refs_3_), channel_id=1, source_target_pairs={{0,3},{4,7},{8,11},{12,15},{16,19},{20,23},{24,27},{28,31}} | collective-permute-start | bytes 589832 | tf_op jit(solution)/shard_map/ppermute | solution.py:900
  50.5 3.1 %collective-permute-start.16 = (bf16[256,384]{1,0:T(8,128)(2,1)S(1)}, bf16[256,384]{1,0:T(8,128)(2,1)S(1)}, u32[]{:S(2)}, u32[]{:S(2)}) collective-permute-start(bf16[256,384]{1,0:T(8,128)(2,1)S(1)} %get-tuple-element.106.refs_3_), channel_id=1, source_target_pairs={{0,2},{1,3},{4,6},{5,7},{8,10},{9,11},{12,14},{13,15},{16,18},{17,... | collective-permute-start | bytes 589832 | tf_op jit(solution)/shard_map/ppermute | solution.py:900
  53.5 1.5 collective-permute-start.15
  55.0 2.5 %pad_maximum_fusion.refs_5_ = bf16[2,4,752,128]{3,2,1,0:T(8,128)(2,1)} fusion(bf16[1,4,752,128]{3,2,1,0:T(8,128)(2,1)} %bitcast.18, bf16[1,4,752,128]{3,2,1,0:T(8,128)(2,1)S(1)} %copy-done.10), kind=kLoop, calls=%fused_computation.3 | loop fusion | flops 770048 | bytes 3080192 | tf_op jit(solution)/shard_map/stack | solution.py:901
  57.5 1.5 collective-permute-start.10
  59.0 0.9 collective-permute-done.16.refs_5_
  60.0 3.4 %collective-permute-done.15.refs_4_ = bf16[256,384]{1,0:T(8,128)(2,1)S(1)} collective-permute-done((bf16[256,384]{1,0:T(8,128)(2,1)S(1)}, bf16[256,384]{1,0:T(8,128)(2,1)S(1)}, u32[]{:S(2)}, u32[]{:S(2)}) %collective-permute-start.15) | collective-permute-done | bytes 196640 | tf_op jit(solution)/shard_map/ppermute | solution.py:900
  63.4 0.8 copy.28.refs_1_
  64.2 7.5 %attend.1 = (bf16[256,576]{1,0:T(8,128)(2,1)}, f32[256,576]{1,0:T(8,128)}, bf16[9,256,1024]{2,1,0:T(8,128)(2,1)}) custom-call(bf16[256,576]{1,0:T(8,128)(2,1)} %copy-done.2, f32[256,1]{1,0:T(8,128)} %copy.28.refs_1_, f32[1,1024]{1,0:T(1,128)} %broadcast_select_fusion.refs_2_, bf16[256,384]{1,0:T(8,128)(2,1)} %copy-done.3, bf16[256,384]{1,0:T(8,128)(2,1)} %copy-done.15, ...), custom_call_target="tpu_custom_call" | custom-call | flops 1 | bytes 1024 | tf_op jit(solution)/shard_map/attend/pallas_call | solution.py:84
  71.6 6.3 %collective-permute-done.10.refs_6_ = bf16[2,4,752,128]{3,2,1,0:T(8,128)(2,1)} collective-permute-done((bf16[2,4,752,128]{3,2,1,0:T(8,128)(2,1)}, bf16[2,4,752,128]{3,2,1,0:T(8,128)(2,1)}, u32[]{:S(2)}, u32[]{:S(2)}) %collective-permute-start.10) | collective-permute-done | bytes 1540128 | tf_op jit(solution)/shard_map/ppermute | solution.py:117
  77.9 3.6 %collective-permute-done.19.refs_8_ = bf16[2,4,752,128]{3,2,1,0:T(8,128)(2,1)S(1)} collective-permute-done((bf16[2,4,752,128]{3,2,1,0:T(8,128)(2,1)}, bf16[2,4,752,128]{3,2,1,0:T(8,128)(2,1)S(1)}, u32[]{:S(2)}, u32[]{:S(2)}) %collective-permute-start.19) | collective-permute-done | bytes 1540128 | tf_op jit(solution)/shard_map/ppermute | solution.py:102
  81.5 1.2 copy-done.12
  82.7 14.0 %mlp.1 = (bf16[576,256]{1,0:T(8,128)(2,1)}, f32[256,576]{1,0:T(8,128)}, bf16[256,576]{1,0:T(8,128)(2,1)}, f32[1,576]{1,0:T(1,128)}, bf16[2,2,4,752,128]{4,3,2,1,...) custom-call(s32[4]{0:T(128)} %pad_add_fusion.1.refs_0_, bf16[256,576]{1,0:T(8,128)(2,1)} %get-tuple-element.112.refs_1_, ...), custom_call_target="tpu_custom_call" | custom-call | flops 1 | bytes 1024 | tf_op jit(solution)/shard_map/mlp/pallas_call | solution.py:84
  96.6 0.7 collective-permute-start.20
  97.3 10.1 %attend_back.1 = (f32[256,576]{1,0:T(8,128)}, bf16[256,384]{1,0:T(8,128)(2,1)}, bf16[256,384]{1,0:T(8,128)(2,1)}, bf16[256,384]{1,0:T(8,128)(2,1)}, bf16[256,384]{1,0:T(8,128)(2,1)}) custom-call(bf16[256,576]{1,0:T(8,128)(2,1)} %copy-done.2, bf16[256,576]{1,0:T(8,128)(2,1)} %get-tuple-element.119.refs_1_, f32[256,576]{1,0:T(8,128)} %get-tuple-element.120.refs_2_, ...), custom_call_target="tpu_custom_call" | custom-call | flops 1 | bytes 1024 | tf_op jit(solution)/shard_map/attend_back/pallas_call | solution.py:84
  107.5 2.4 %fusion = bf16[2,4,752,128]{3,2,1,0:T(8,128)(2,1)S(1)} fusion(bf16[2,2,4,752,128]{4,3,2,1,0:T(8,128)(2,1)} %collective-permute-done.20, bf16[2,2,4,752,128]{4,3,2,1,0:T(8,128)(2,1)} %get-tuple-element.117), kind=kLoop, calls=%fused_computation.2 | loop fusion | flops 3080192 | bytes 4620288 | tf_op jit(solution)/shard_map/convert_element_type | solution.py:124
  109.8 1.6 collective-permute-start.21
  111.4 1.3 collective-permute-start.22
  112.7 1.3 collective-permute-start.23
  114.0 1.3 collective-permute-start.24
  115.3 4.3 %query_back.1 = (bf16[576,576]{1,0:T(8,128)(2,1)S(1)}, f32[256,576]{1,0:T(8,128)S(1)}, f32[1,64]{1,0:T(1,128)S(1)}) custom-call(f32[256,576]{1,0:T(8,128)S(1)} %copy-done.5, f32[256,768]{1,0:T(8,128)S(1)} %get-tuple-element.133.refs_1_.refs_4_, bf16[256,576]{1,0:T(8,128)(2,1)S(1)} %get-tuple-element.134.refs_2_.refs_5_, ...), custom_call_target="tpu_custom_call" | custom-call | flops 1 | bytes 1024 | tf_op jit(solution)/shard_map/query_back/pallas_call | solution.py:84
  119.6 0.6 collective-permute-done.22.refs_15_
  120.2 11.4 %collective-permute-done.23.refs_16_ = bf16[256,384]{1,0:T(8,128)(2,1)S(1)} collective-permute-done((bf16[256,384]{1,0:T(8,128)(2,1)S(1)}, bf16[256,384]{1,0:T(8,128)(2,1)S(1)}, u32[]{:S(2)}, u32[]{:S(2)}) %collective-permute-start.23) | collective-permute-done | bytes 196640 | tf_op jit(solution)/shard_map/ppermute | solution.py:917
  131.7 1.6 fusion.1
  133.3 1.5 collective-permute-start.25
  134.8 4.3 %last.1 = (f32[576,256]{1,0:T(8,128)}, bf16[4,4,160,128]{3,2,1,0:T(8,128)(2,1)S(1)}, bf16[4,4,160,128]{3,2,1,0:T(8,128)(2,1)S(1)}) custom-call(s32[4]{0:T(128)S(1)} %copy-done.8, bf16[576,576]{1,0:T(8,128)(2,1)S(1)} %get-tuple-element.139.refs_1_, f32[256,576]{1,0:T(8,128)S(1)} %get-tuple-element.140.refs_2_, f32[1,64]{1,0:T(1,128)S(1)} %get-tuple-element.141.refs_3_, ...), custom_call_target="tpu_custom_call" | custom-call | flops 1 | bytes 1024 | tf_op jit(solution)/shard_map/last/pallas_call | solution.py:84
  139.2 2.1 %collective-permute-done.26 = bf16[4,4,160,128]{3,2,1,0:T(8,128)(2,1)S(1)} collective-permute-done((bf16[4,4,160,128]{3,2,1,0:T(8,128)(2,1)S(1)}, bf16[4,4,160,128]{3,2,1,0:T(8,128)(2,1)S(1)}, u32[]{:S(2)}, u32[]{:S(2)}) %collective-permute-start.26) | collective-permute-done | bytes 655392 | tf_op jit(solution)/shard_map/ppermute | solution.py:102
  141.3 3.8 %collective-permute-done.25 = bf16[4,752,128]{2,1,0:T(8,128)(2,1)S(1)} collective-permute-done((bf16[4,752,128]{2,1,0:T(8,128)(2,1)S(1)}, bf16[4,752,128]{2,1,0:T(8,128)(2,1)S(1)}, u32[]{:S(2)}, u32[]{:S(2)}) %collective-permute-start.25) | collective-permute-done | bytes 770080 | tf_op jit(solution)/shard_map/ppermute | solution.py:117
  145.3 2.4 %collective-permute-start.32 = (bf16[4,160,128]{2,1,0:T(8,128)(2,1)S(1)}, bf16[4,160,128]{2,1,0:T(8,128)(2,1)S(1)}, u32[]{:S(2)}, u32[]{:S(2)}) collective-permute-start(bf16[4,160,128]{2,1,0:T(8,128)(2,1)S(1)} %get-tuple-element.171), channel_id=1, source_target_pairs={{0,24},{4,28},{8,16},{12,20},{16,8},{20,12},{24,0},{28,4},{1,25},{... | collective-permute-start | bytes 491528 | tf_op jit(solution)/shard_map/ppermute | solution.py:102
  148.3 0.6 collective-permute-start.30
  148.9 1.4 fusion.4
  150.4 3.8 %collective-permute-start.29 = (bf16[752,128]{1,0:T(8,128)(2,1)S(1)}, bf16[752,128]{1,0:T(8,128)(2,1)S(1)}, u32[]{:S(2)}, u32[]{:S(2)}) collective-permute-start(bf16[752,128]{1,0:T(8,128)(2,1)S(1)} %get-tuple-element.168), channel_id=1, source_target_pairs={{0,3},{1,0},{2,1},{3,2},{4,7},{5,4},{6,5},{7,6},{8,11},{9,8},{10,9... | collective-permute-start | bytes 577544 | tf_op jit(solution)/shard_map/ppermute | solution.py:107
  154.9 3.8 %collective-permute-start.35 = (bf16[160,128]{1,0:T(8,128)(2,1)S(1)}, bf16[160,128]{1,0:T(8,128)(2,1)S(1)}, u32[]{:S(2)}, u32[]{:S(2)}) collective-permute-start(bf16[160,128]{1,0:T(8,128)(2,1)S(1)} %get-tuple-element.177), channel_id=1, source_target_pairs={{0,3},{1,0},{2,1},{3,2},{4,7},{5,4},{6,5},{7,6},{8,11},{9,8},{10,9... | collective-permute-start | bytes 122888 | tf_op jit(solution)/shard_map/ppermute | solution.py:107
  158.7 1.3 collective-permute-done.27
  160.0 6.8 %collective-permute-start.34 = (bf16[160,128]{1,0:T(8,128)(2,1)S(1)}, bf16[160,128]{1,0:T(8,128)(2,1)S(1)}, u32[]{:S(2)}, u32[]{:S(2)}) collective-permute-start(bf16[160,128]{1,0:T(8,128)(2,1)S(1)} %get-tuple-element.178), channel_id=1, source_target_pairs={{0,2},{1,3},{2,0},{3,1},{4,6},{5,7},{6,4},{7,5},{8,10},{9,11},{10,... | collective-permute-start | bytes 122888 | tf_op jit(solution)/shard_map/ppermute | solution.py:107
  166.8 3.1 %collective-permute-done.28 = bf16[752,128]{1,0:T(8,128)(2,1)S(1)} collective-permute-done((bf16[752,128]{1,0:T(8,128)(2,1)S(1)}, bf16[752,128]{1,0:T(8,128)(2,1)S(1)}, u32[]{:S(2)}, u32[]{:S(2)}) %collective-permute-start.28) | collective-permute-done | bytes 192544 | tf_op jit(solution)/shard_map/ppermute | solution.py:107
  169.9 1.1 add_convert_fusion.1
  171.2 1.5 collective-permute-start.37
  172.6 1.7 collective-permute-start.36
  174.7 4.7 %collective-permute-done.37 = bf16[912,128]{1,0:T(8,128)(2,1)S(1)} collective-permute-done((bf16[912,128]{1,0:T(8,128)(2,1)S(1)}, bf16[912,128]{1,0:T(8,128)(2,1)S(1)}, u32[]{:S(2)}, u32[]{:S(2)}) %collective-permute-start.37) | collective-permute-done | bytes 233504 | tf_op jit(solution)/shard_map/ppermute | solution.py:102
  179.4 3.8 %collective-permute-done.36 = bf16[912,128]{1,0:T(8,128)(2,1)S(1)} collective-permute-done((bf16[912,128]{1,0:T(8,128)(2,1)S(1)}, bf16[912,128]{1,0:T(8,128)(2,1)S(1)}, u32[]{:S(2)}, u32[]{:S(2)}) %collective-permute-start.36) | collective-permute-done | bytes 233504 | tf_op jit(solution)/shard_map/ppermute | solution.py:102
  183.4 2.5 %collective-permute-done.39.refs_2_ = bf16[4,912,128]{2,1,0:T(8,128)(2,1)S(1)} collective-permute-done((bf16[4,912,128]{2,1,0:T(8,128)(2,1)S(1)}, bf16[4,912,128]{2,1,0:T(8,128)(2,1)S(1)}, u32[]{:S(2)}, u32[]{:S(2)}) %collective-permute-start.39) | collective-permute-done | bytes 933920 | tf_op jit(solution)/shard_map/ppermute | solution.py:102
  185.8 2.7 %unpack.1 = (f32[144,1536]{1,0:T(8,128)}, f32[144,1536]{1,0:T(8,128)}, f32[576,384]{1,0:T(8,128)}, f32[144,576]{1,0:T(8,128)}, f32[144,576]{1,0:T(8,128)}, /*ind...) custom-call(s32[4]{0:T(128)S(1)} %copy-done.8, ...), custom_call_target="tpu_custom_call" | custom-call | flops 1 | bytes 1024 | tf_op jit(solution)/shard_map/unpack/pallas_call | solution.py:84
  (116 shorter events, 5.0 us)
Async XLA Ops:
  0.6 3.8 %copy-start.24 = (s32[256]{0:T(256)S(1)}, s32[256]{0:T(256)}, u32[]{:S(2)}) copy-start(s32[256]{0:T(256)} %param.15) | copy-start | bytes 3076
  0.7 3.8 %copy-start.19 = (bf16[144]{0:T(256)(128)(2,1)S(1)}, bf16[144]{0:T(256)(128)(2,1)}, u32[]{:S(2)}) copy-start(bf16[144]{0:T(256)(128)(2,1)} %param.24) | copy-start | bytes 868
  0.7 3.8 %copy-start.17 = (bf16[16]{0:T(256)(128)(2,1)S(1)}, bf16[16]{0:T(256)(128)(2,1)}, u32[]{:S(2)}) copy-start(bf16[16]{0:T(256)(128)(2,1)} %param.19) | copy-start | bytes 100
  0.7 3.8 %copy-start.18 = (bf16[16]{0:T(256)(128)(2,1)S(1)}, bf16[16]{0:T(256)(128)(2,1)}, u32[]{:S(2)}) copy-start(bf16[16]{0:T(256)(128)(2,1)} %param.18) | copy-start | bytes 100
  0.7 3.8 %copy-start.20 = (bf16[144]{0:T(256)(128)(2,1)S(1)}, bf16[144]{0:T(256)(128)(2,1)}, u32[]{:S(2)}) copy-start(bf16[144]{0:T(256)(128)(2,1)} %param.17) | copy-start | bytes 868
  4.5 31.1 %copy-start.16 = (bf16[752,128]{1,0:T(8,128)(2,1)S(1)}, bf16[752,128]{1,0:T(8,128)(2,1)}, u32[]{:S(2)}) copy-start(bf16[752,128]{1,0:T(8,128)(2,1)} %get-tuple-element.91) | copy-start | bytes 577540
  4.6 10.3 %collective-permute-start.13 = (bf16[16,128]{1,0:T(8,128)(2,1)S(1)}, bf16[16,128]{1,0:T(8,128)(2,1)S(1)}, u32[]{:S(2)}, u32[]{:S(2)}) collective-permute-start(bf16[16,128]{1,0:T(8,128)(2,1)S(1)} %get-tuple-element.190), channel_id=1, source_target_pairs={{0,3},{1,0},{2,1},{3,2},{4,7},{5,4},{6,5},{7,6},{8,11},{9,8},{10,9... | collective-permute-start | bytes 12296 | tf_op jit(solution)/shard_map/ppermute | solution.py:107
  9.7 5.2 %collective-permute-start.12 = (bf16[16,128]{1,0:T(8,128)(2,1)S(1)}, bf16[16,128]{1,0:T(8,128)(2,1)S(1)}, u32[]{:S(2)}, u32[]{:S(2)}) collective-permute-start(bf16[16,128]{1,0:T(8,128)(2,1)S(1)} %get-tuple-element.190), channel_id=1, source_target_pairs={{0,2},{1,3},{2,0},{3,1},{4,6},{5,7},{6,4},{7,5},{8,10},{9,11},{10,... | collective-permute-start | bytes 12296 | tf_op jit(solution)/shard_map/ppermute | solution.py:107
  9.7 9.0 %collective-permute-start.11 = (bf16[16,128]{1,0:T(8,128)(2,1)S(1)}, bf16[16,128]{1,0:T(8,128)(2,1)S(1)}, u32[]{:S(2)}, u32[]{:S(2)}) collective-permute-start(bf16[16,128]{1,0:T(8,128)(2,1)S(1)} %get-tuple-element.190), channel_id=1, source_target_pairs={{0,1},{1,2},{2,3},{3,0},{4,5},{5,6},{6,7},{7,4},{8,9},{9,10},{10,1... | collective-permute-start | bytes 12296 | tf_op jit(solution)/shard_map/ppermute | solution.py:107
  10.7 9.5 %collective-permute-start.2 = (bf16[144,128]{1,0:T(8,128)(2,1)}, bf16[144,128]{1,0:T(8,128)(2,1)S(1)}, u32[]{:S(2)}, u32[]{:S(2)}) collective-permute-start(bf16[144,128]{1,0:T(8,128)(2,1)} %get-tuple-element.89), channel_id=1, source_target_pairs={{0,3},{1,0},{2,1},{3,2},{4,7},{5,4},{6,5},{7,6},{8,11},{9,8},{10,9... | collective-permute-start | bytes 110600 | tf_op jit(solution)/shard_map/ppermute | solution.py:107
  13.5 7.4 %collective-permute-start.1 = (bf16[144,128]{1,0:T(8,128)(2,1)}, bf16[144,128]{1,0:T(8,128)(2,1)S(1)}, u32[]{:S(2)}, u32[]{:S(2)}) collective-permute-start(bf16[144,128]{1,0:T(8,128)(2,1)} %get-tuple-element.89), channel_id=1, source_target_pairs={{0,2},{1,3},{2,0},{3,1},{4,6},{5,7},{6,4},{7,5},{8,10},{9,11},{10,... | collective-permute-start | bytes 110600 | tf_op jit(solution)/shard_map/ppermute | solution.py:107
  14.8 6.6 %collective-permute-start = (bf16[144,128]{1,0:T(8,128)(2,1)}, bf16[144,128]{1,0:T(8,128)(2,1)S(1)}, u32[]{:S(2)}, u32[]{:S(2)}) collective-permute-start(bf16[144,128]{1,0:T(8,128)(2,1)} %get-tuple-element.89), channel_id=1, source_target_pairs={{0,1},{1,2},{2,3},{3,0},{4,5},{5,6},{6,7},{7,4},{8,9},{9,10},{10,1... | collective-permute-start | bytes 110600 | tf_op jit(solution)/shard_map/ppermute | solution.py:107
  14.9 19.7 %collective-permute-start.8 = (bf16[752,128]{1,0:T(8,128)(2,1)}, bf16[752,128]{1,0:T(8,128)(2,1)S(1)}, u32[]{:S(2)}, u32[]{:S(2)}) collective-permute-start(bf16[752,128]{1,0:T(8,128)(2,1)} %get-tuple-element.91), channel_id=1, source_target_pairs={{0,3},{1,0},{2,1},{3,2},{4,7},{5,4},{6,5},{7,6},{8,11},{9,8},{10,9... | collective-permute-start | bytes 577544 | tf_op jit(solution)/shard_map/ppermute | solution.py:107
  18.7 16.9 %collective-permute-start.7 = (bf16[752,128]{1,0:T(8,128)(2,1)}, bf16[752,128]{1,0:T(8,128)(2,1)S(1)}, u32[]{:S(2)}, u32[]{:S(2)}) collective-permute-start(bf16[752,128]{1,0:T(8,128)(2,1)} %get-tuple-element.91), channel_id=1, source_target_pairs={{0,2},{1,3},{2,0},{3,1},{4,6},{5,7},{6,4},{7,5},{8,10},{9,11},{10,... | collective-permute-start | bytes 577544 | tf_op jit(solution)/shard_map/ppermute | solution.py:107
  20.2 15.4 %collective-permute-start.6 = (bf16[752,128]{1,0:T(8,128)(2,1)}, bf16[752,128]{1,0:T(8,128)(2,1)S(1)}, u32[]{:S(2)}, u32[]{:S(2)}) collective-permute-start(bf16[752,128]{1,0:T(8,128)(2,1)} %get-tuple-element.91), channel_id=1, source_target_pairs={{0,1},{1,2},{2,3},{3,0},{4,5},{5,6},{6,7},{7,4},{8,9},{9,10},{10,1... | collective-permute-start | bytes 577544 | tf_op jit(solution)/shard_map/ppermute | solution.py:107
  22.2 5.7 %collective-permute-start.4 = (bf16[4,144,128]{2,1,0:T(8,128)(2,1)S(1)}, bf16[4,144,128]{2,1,0:T(8,128)(2,1)S(1)}, u32[]{:S(2)}, u32[]{:S(2)}) collective-permute-start(bf16[4,144,128]{2,1,0:T(8,128)(2,1)S(1)} %get-tuple-element.182), channel_id=1, source_target_pairs={{0,8},{4,12},{8,0},{12,4},{16,24},{20,28},{24,16},{28,20},{1,9},{5... | collective-permute-start | bytes 442376 | tf_op jit(solution)/shard_map/ppermute | solution.py:102
  23.8 7.7 %collective-permute-start.3 = (bf16[4,144,128]{2,1,0:T(8,128)(2,1)S(1)}, bf16[4,144,128]{2,1,0:T(8,128)(2,1)S(1)}, u32[]{:S(2)}, u32[]{:S(2)}) collective-permute-start(bf16[4,144,128]{2,1,0:T(8,128)(2,1)S(1)} %get-tuple-element.182), channel_id=1, source_target_pairs={{0,16},{4,20},{8,24},{12,28},{16,0},{20,4},{24,8},{28,12},{1,17},{... | collective-permute-start | bytes 442376 | tf_op jit(solution)/shard_map/ppermute | solution.py:102
  27.9 6.6 %collective-permute-start.5 = (bf16[4,144,128]{2,1,0:T(8,128)(2,1)S(1)}, bf16[4,144,128]{2,1,0:T(8,128)(2,1)S(1)}, u32[]{:S(2)}, u32[]{:S(2)}) collective-permute-start(bf16[4,144,128]{2,1,0:T(8,128)(2,1)S(1)} %get-tuple-element.182), channel_id=1, source_target_pairs={{0,24},{4,28},{8,16},{12,20},{16,8},{20,12},{24,0},{28,4},{1,25},{... | collective-permute-start | bytes 442376 | tf_op jit(solution)/shard_map/ppermute | solution.py:102
  34.5 7.5 %copy-start = (bf16[256,576]{0,1:T(8,128)(2,1)S(1)}, bf16[256,576]{0,1:T(8,128)(2,1)}, u32[]{:S(2)}) copy-start(bf16[256,576]{0,1:T(8,128)(2,1)} %param.14) | copy-start | bytes 884740
  34.5 7.5 %copy-start.7 = (s32[4]{0:T(128)S(1)}, s32[4]{0:T(128)}, u32[]{:S(2)}) copy-start(s32[4]{0:T(128)} %pad_add_fusion.1.refs_0_) | copy-start | bytes 52
  36.9 18.2 %collective-permute-start.9 = (bf16[4,752,128]{2,1,0:T(8,128)(2,1)}, bf16[4,752,128]{2,1,0:T(8,128)(2,1)}, u32[]{:S(2)}, u32[]{:S(2)}) collective-permute-start(bf16[4,752,128]{2,1,0:T(8,128)(2,1)} %get-tuple-element.175), channel_id=1, source_target_pairs={{0,16},{4,12},{8,24},{12,4},{16,0},{20,28},{24,8},{28,20},{1,17},{... | collective-permute-start | bytes 2310152 | tf_op jit(solution)/shard_map/ppermute | solution.py:117
  39.9 15.1 %copy-start.10 = (bf16[1,4,752,128]{3,2,1,0:T(8,128)(2,1)S(1)}, bf16[1,4,752,128]{3,2,1,0:T(8,128)(2,1)}, u32[]{:S(2)}) copy-start(bf16[1,4,752,128]{3,2,1,0:T(8,128)(2,1)} %get-tuple-element.174) | copy-start | bytes 2310148
  39.9 2.1 %collective-permute-start.14 = (bf16[4,4,144,128]{3,2,1,0:T(8,128)(2,1)S(1)}, bf16[4,4,144,128]{3,2,1,0:T(8,128)(2,1)S(1)}, u32[]{:S(2)}, u32[]{:S(2)}) collective-permute-start(bf16[4,4,144,128]{3,2,1,0:T(8,128)(2,1)S(1)} %pad_maximum_fusion.3.refs_1_), channel_id=1, source_target_pairs={{0,4},{4,0},{8,12},{12,8},{16,20},{20,16},{24,28},{28,24},{1,5},{5... | collective-permute-start | bytes 1769480 | tf_op jit(solution)/shard_map/ppermute | solution.py:102
  47.1 10.4 %copy-start.2 = (bf16[256,576]{1,0:T(8,128)(2,1)}, bf16[256,576]{1,0:T(8,128)(2,1)S(1)}, u32[]{:S(2)}) copy-start(bf16[256,576]{1,0:T(8,128)(2,1)S(1)} %get-tuple-element.102.refs_0_) | copy-start | bytes 884740
  47.2 10.4 %copy-start.3 = (bf16[256,384]{1,0:T(8,128)(2,1)}, bf16[256,384]{1,0:T(8,128)(2,1)S(1)}, u32[]{:S(2)}) copy-start(bf16[256,384]{1,0:T(8,128)(2,1)S(1)} %get-tuple-element.106.refs_3_) | copy-start | bytes 589828
  47.2 11.9 %collective-permute-start.17 = (bf16[256,384]{1,0:T(8,128)(2,1)S(1)}, bf16[256,384]{1,0:T(8,128)(2,1)S(1)}, u32[]{:S(2)}, u32[]{:S(2)}) collective-permute-start(bf16[256,384]{1,0:T(8,128)(2,1)S(1)} %get-tuple-element.106.refs_3_), channel_id=1, source_target_pairs={{0,3},{4,7},{8,11},{12,15},{16,19},{20,23},{24,27},{28,31}} | collective-permute-start | bytes 589832 | tf_op jit(solution)/shard_map/ppermute | solution.py:900
  50.5 9.5 %collective-permute-start.16 = (bf16[256,384]{1,0:T(8,128)(2,1)S(1)}, bf16[256,384]{1,0:T(8,128)(2,1)S(1)}, u32[]{:S(2)}, u32[]{:S(2)}) collective-permute-start(bf16[256,384]{1,0:T(8,128)(2,1)S(1)} %get-tuple-element.106.refs_3_), channel_id=1, source_target_pairs={{0,2},{1,3},{4,6},{5,7},{8,10},{9,11},{12,14},{13,15},{16,18},{17,... | collective-permute-start | bytes 589832 | tf_op jit(solution)/shard_map/ppermute | solution.py:900
  53.5 9.8 %collective-permute-start.15 = (bf16[256,384]{1,0:T(8,128)(2,1)S(1)}, bf16[256,384]{1,0:T(8,128)(2,1)S(1)}, u32[]{:S(2)}, u32[]{:S(2)}) collective-permute-start(bf16[256,384]{1,0:T(8,128)(2,1)S(1)} %get-tuple-element.106.refs_3_), channel_id=1, source_target_pairs={{0,1},{1,2},{2,3},{4,5},{5,6},{6,7},{8,9},{9,10},{10,11},{12,13},{... | collective-permute-start | bytes 589832 | tf_op jit(solution)/shard_map/ppermute | solution.py:900
  57.5 20.4 %collective-permute-start.10 = (bf16[2,4,752,128]{3,2,1,0:T(8,128)(2,1)}, bf16[2,4,752,128]{3,2,1,0:T(8,128)(2,1)}, u32[]{:S(2)}, u32[]{:S(2)}) collective-permute-start(bf16[2,4,752,128]{3,2,1,0:T(8,128)(2,1)} %pad_maximum_fusion.refs_5_), channel_id=1, source_target_pairs={{0,8},{4,20},{8,0},{12,28},{16,24},{20,4},{24,16},{28,12},{1,9},{5... | collective-permute-start | bytes 4620296 | tf_op jit(solution)/shard_map/ppermute | solution.py:117
  59.0 5.1 %copy-start.13 = (bf16[256,384]{1,0:T(8,128)(2,1)}, bf16[256,384]{1,0:T(8,128)(2,1)S(1)}, u32[]{:S(2)}) copy-start(bf16[256,384]{1,0:T(8,128)(2,1)S(1)} %collective-permute-done.17.refs_6_) | copy-start | bytes 589828
  60.0 4.2 %copy-start.14 = (bf16[256,384]{1,0:T(8,128)(2,1)}, bf16[256,384]{1,0:T(8,128)(2,1)S(1)}, u32[]{:S(2)}) copy-start(bf16[256,384]{1,0:T(8,128)(2,1)S(1)} %collective-permute-done.16.refs_5_) | copy-start | bytes 589828
  63.4 14.5 %collective-permute-start.18 = (bf16[2,4,752,128]{3,2,1,0:T(8,128)(2,1)}, bf16[2,4,752,128]{3,2,1,0:T(8,128)(2,1)}, u32[]{:S(2)}, u32[]{:S(2)}) collective-permute-start(bf16[2,4,752,128]{3,2,1,0:T(8,128)(2,1)} %pad_maximum_fusion.refs_5_), channel_id=1, source_target_pairs={{0,4},{4,0},{8,12},{12,8},{16,20},{20,16},{24,28},{28,24},{1,5},{5... | collective-permute-start | bytes 4620296 | tf_op jit(solution)/shard_map/ppermute | solution.py:102
  77.9 3.6 %collective-permute-start.19 = (bf16[2,4,752,128]{3,2,1,0:T(8,128)(2,1)}, bf16[2,4,752,128]{3,2,1,0:T(8,128)(2,1)S(1)}, u32[]{:S(2)}, u32[]{:S(2)}) collective-permute-start(bf16[2,4,752,128]{3,2,1,0:T(8,128)(2,1)} %collective-permute-done.10.refs_6_), channel_id=1, source_target_pairs={{0,4},{4,0},{8,12},{12,8},{16,20},{20,16},{24,28},{28,24},{1,5},{5... | collective-permute-start | bytes 4620296 | tf_op jit(solution)/shard_map/ppermute | solution.py:102
  81.5 1.2 copy-start.12
  96.6 10.8 %collective-permute-start.20 = (bf16[2,2,4,752,128]{4,3,2,1,0:T(8,128)(2,1)}, bf16[2,2,4,752,128]{4,3,2,1,0:T(8,128)(2,1)}, u32[]{:S(2)}, u32[]{:S(2)}) collective-permute-start(bf16[2,2,4,752,128]{4,3,2,1,0:T(8,128)(2,1)} %get-tuple-element.118), channel_id=1, source_target_pairs={{0,4},{4,0},{8,12},{12,8},{16,20},{20,16},{24,28},{28,24},{1,5},{5... | collective-permute-start | bytes 9240584 | tf_op jit(solution)/shard_map/ppermute | solution.py:102
  107.4 4.0 %copy-start.23 = (bf16[256,384]{1,0:T(8,128)(2,1)S(1)}, bf16[256,384]{1,0:T(8,128)(2,1)}, u32[]{:S(2)}) copy-start(bf16[256,384]{1,0:T(8,128)(2,1)} %get-tuple-element.129) | copy-start | bytes 589828
  107.5 5.2 %copy-start.22 = (bf16[256,384]{1,0:T(8,128)(2,1)S(1)}, bf16[256,384]{1,0:T(8,128)(2,1)}, u32[]{:S(2)}) copy-start(bf16[256,384]{1,0:T(8,128)(2,1)} %get-tuple-element.130) | copy-start | bytes 589828
  107.5 6.5 %copy-start.21 = (bf16[256,384]{1,0:T(8,128)(2,1)S(1)}, bf16[256,384]{1,0:T(8,128)(2,1)}, u32[]{:S(2)}) copy-start(bf16[256,384]{1,0:T(8,128)(2,1)} %get-tuple-element.131) | copy-start | bytes 589828
  107.5 7.8 %copy-start.5 = (f32[256,576]{1,0:T(8,128)S(1)}, f32[256,576]{1,0:T(8,128)}, u32[]{:S(2)}) copy-start(f32[256,576]{1,0:T(8,128)} %get-tuple-element.132.refs_0_) | copy-start | bytes 1769476
  109.8 21.7 %collective-permute-start.21 = (bf16[2,4,752,128]{3,2,1,0:T(8,128)(2,1)S(1)}, bf16[2,4,752,128]{3,2,1,0:T(8,128)(2,1)S(1)}, u32[]{:S(2)}, u32[]{:S(2)}) collective-permute-start(bf16[2,4,752,128]{3,2,1,0:T(8,128)(2,1)S(1)} %fusion), channel_id=1, source_target_pairs={{0,8},{4,20},{8,0},{12,28},{16,24},{20,4},{24,16},{28,12},{1,9},{5... | collective-permute-start | bytes 4620296 | tf_op jit(solution)/shard_map/ppermute | solution.py:117
  111.4 8.8 %collective-permute-start.22 = (bf16[256,384]{1,0:T(8,128)(2,1)S(1)}, bf16[256,384]{1,0:T(8,128)(2,1)S(1)}, u32[]{:S(2)}, u32[]{:S(2)}) collective-permute-start(bf16[256,384]{1,0:T(8,128)(2,1)S(1)} %copy-done.23), channel_id=1, source_target_pairs={{1,0},{2,1},{3,2},{5,4},{6,5},{7,6},{9,8},{10,9},{11,10},{13,12},{... | collective-permute-start | bytes 589832 | tf_op jit(solution)/shard_map/ppermute | solution.py:917
  112.7 18.9 %collective-permute-start.23 = (bf16[256,384]{1,0:T(8,128)(2,1)S(1)}, bf16[256,384]{1,0:T(8,128)(2,1)S(1)}, u32[]{:S(2)}, u32[]{:S(2)}) collective-permute-start(bf16[256,384]{1,0:T(8,128)(2,1)S(1)} %copy-done.22), channel_id=1, source_target_pairs={{2,0},{3,1},{6,4},{7,5},{10,8},{11,9},{14,12},{15,13},{18,16},{19,... | collective-permute-start | bytes 589832 | tf_op jit(solution)/shard_map/ppermute | solution.py:917
  114.0 17.6 %collective-permute-start.24 = (bf16[256,384]{1,0:T(8,128)(2,1)S(1)}, bf16[256,384]{1,0:T(8,128)(2,1)S(1)}, u32[]{:S(2)}, u32[]{:S(2)}) collective-permute-start(bf16[256,384]{1,0:T(8,128)(2,1)S(1)} %copy-done.21), channel_id=1, source_target_pairs={{3,0},{7,4},{11,8},{15,12},{19,16},{23,20},{27,24},{31,28}} | collective-permute-start | bytes 589832 | tf_op jit(solution)/shard_map/ppermute | solution.py:917
  115.3 16.3 %copy-start.11 = (bf16[2,2,4,752,128]{4,3,2,1,0:T(8,128)(2,1)S(1)}, bf16[2,2,4,752,128]{4,3,2,1,0:T(8,128)(2,1)}, u32[]{:S(2)}) copy-start(bf16[2,2,4,752,128]{4,3,2,1,0:T(8,128)(2,1)} %get-tuple-element.117) | copy-start | bytes 9240580
  131.6 3.2 %copy-start.1 = (bf16[256,576]{0,1:T(8,128)(2,1)S(1)}, bf16[256,576]{0,1:T(8,128)(2,1)}, u32[]{:S(2)}) copy-start(bf16[256,576]{0,1:T(8,128)(2,1)} %param.14) | copy-start | bytes 884740
  131.6 3.2 %copy-start.4 = (f32[256,576]{1,0:T(8,128)S(1)}, f32[256,576]{1,0:T(8,128)}, u32[]{:S(2)}) copy-start(f32[256,576]{1,0:T(8,128)} %get-tuple-element.142.refs_7_) | copy-start | bytes 1769476
  131.6 3.2 %copy-start.6 = (bf16[256,384]{1,0:T(8,128)(2,1)S(1)}, bf16[256,384]{1,0:T(8,128)(2,1)}, u32[]{:S(2)}) copy-start(bf16[256,384]{1,0:T(8,128)(2,1)} %get-tuple-element.144.refs_14_) | copy-start | bytes 589828
  131.6 3.2 %copy-start.8 = (s32[4]{0:T(128)S(1)}, s32[4]{0:T(128)}, u32[]{:S(2)}) copy-start(s32[4]{0:T(128)} %pad_add_fusion.1.refs_0_) | copy-start | bytes 52
  131.6 3.2 %copy-start.9 = (f32[1,576]{1,0:T(1,128)S(1)}, f32[1,576]{1,0:T(1,128)}, u32[]{:S(2)}) copy-start(f32[1,576]{1,0:T(1,128)} %get-tuple-element.143.refs_13_) | copy-start | bytes 6916
  133.3 11.9 %collective-permute-start.25 = (bf16[4,752,128]{2,1,0:T(8,128)(2,1)S(1)}, bf16[4,752,128]{2,1,0:T(8,128)(2,1)S(1)}, u32[]{:S(2)}, u32[]{:S(2)}) collective-permute-start(bf16[4,752,128]{2,1,0:T(8,128)(2,1)S(1)} %fusion.1), channel_id=1, source_target_pairs={{0,16},{4,12},{8,24},{12,4},{16,0},{20,28},{24,8},{28,20},{1,17},{... | collective-permute-start | bytes 2310152 | tf_op jit(solution)/shard_map/ppermute | solution.py:117
  139.1 2.2 %collective-permute-start.26 = (bf16[4,4,160,128]{3,2,1,0:T(8,128)(2,1)S(1)}, bf16[4,4,160,128]{3,2,1,0:T(8,128)(2,1)S(1)}, u32[]{:S(2)}, u32[]{:S(2)}) collective-permute-start(bf16[4,4,160,128]{3,2,1,0:T(8,128)(2,1)S(1)} %get-tuple-element.150), channel_id=1, source_target_pairs={{0,4},{4,0},{8,12},{12,8},{16,20},{20,16},{24,28},{28,24},{1,5},{5... | collective-permute-start | bytes 1966088 | tf_op jit(solution)/shard_map/ppermute | solution.py:102
  145.3 8.9 %collective-permute-start.32 = (bf16[4,160,128]{2,1,0:T(8,128)(2,1)S(1)}, bf16[4,160,128]{2,1,0:T(8,128)(2,1)S(1)}, u32[]{:S(2)}, u32[]{:S(2)}) collective-permute-start(bf16[4,160,128]{2,1,0:T(8,128)(2,1)S(1)} %get-tuple-element.171), channel_id=1, source_target_pairs={{0,24},{4,28},{8,16},{12,20},{16,8},{20,12},{24,0},{28,4},{1,25},{... | collective-permute-start | bytes 491528 | tf_op jit(solution)/shard_map/ppermute | solution.py:102
  147.8 7.0 %collective-permute-start.31 = (bf16[4,160,128]{2,1,0:T(8,128)(2,1)S(1)}, bf16[4,160,128]{2,1,0:T(8,128)(2,1)S(1)}, u32[]{:S(2)}, u32[]{:S(2)}) collective-permute-start(bf16[4,160,128]{2,1,0:T(8,128)(2,1)S(1)} %get-tuple-element.172), channel_id=1, source_target_pairs={{0,16},{4,20},{8,24},{12,28},{16,0},{20,4},{24,8},{28,12},{1,17},{... | collective-permute-start | bytes 491528 | tf_op jit(solution)/shard_map/ppermute | solution.py:102
  148.3 6.5 %collective-permute-start.30 = (bf16[4,160,128]{2,1,0:T(8,128)(2,1)S(1)}, bf16[4,160,128]{2,1,0:T(8,128)(2,1)S(1)}, u32[]{:S(2)}, u32[]{:S(2)}) collective-permute-start(bf16[4,160,128]{2,1,0:T(8,128)(2,1)S(1)} %get-tuple-element.173), channel_id=1, source_target_pairs={{0,8},{4,12},{8,0},{12,4},{16,24},{20,28},{24,16},{28,20},{1,9},{5... | collective-permute-start | bytes 491528 | tf_op jit(solution)/shard_map/ppermute | solution.py:102
  150.3 9.7 %collective-permute-start.27 = (bf16[752,128]{1,0:T(8,128)(2,1)S(1)}, bf16[752,128]{1,0:T(8,128)(2,1)S(1)}, u32[]{:S(2)}, u32[]{:S(2)}) collective-permute-start(bf16[752,128]{1,0:T(8,128)(2,1)S(1)} %get-tuple-element.167), channel_id=1, source_target_pairs={{0,1},{1,2},{2,3},{3,0},{4,5},{5,6},{6,7},{7,4},{8,9},{9,10},{10,1... | collective-permute-start | bytes 577544 | tf_op jit(solution)/shard_map/ppermute | solution.py:107
  150.4 16.4 %collective-permute-start.29 = (bf16[752,128]{1,0:T(8,128)(2,1)S(1)}, bf16[752,128]{1,0:T(8,128)(2,1)S(1)}, u32[]{:S(2)}, u32[]{:S(2)}) collective-permute-start(bf16[752,128]{1,0:T(8,128)(2,1)S(1)} %get-tuple-element.168), channel_id=1, source_target_pairs={{0,3},{1,0},{2,1},{3,2},{4,7},{5,4},{6,5},{7,6},{8,11},{9,8},{10,9... | collective-permute-start | bytes 577544 | tf_op jit(solution)/shard_map/ppermute | solution.py:107
  154.2 15.7 %collective-permute-start.28 = (bf16[752,128]{1,0:T(8,128)(2,1)S(1)}, bf16[752,128]{1,0:T(8,128)(2,1)S(1)}, u32[]{:S(2)}, u32[]{:S(2)}) collective-permute-start(bf16[752,128]{1,0:T(8,128)(2,1)S(1)} %get-tuple-element.169), channel_id=1, source_target_pairs={{0,2},{1,3},{2,0},{3,1},{4,6},{5,7},{6,4},{7,5},{8,10},{9,11},{10,... | collective-permute-start | bytes 577544 | tf_op jit(solution)/shard_map/ppermute | solution.py:107
  154.8 16.2 %collective-permute-start.33 = (bf16[160,128]{1,0:T(8,128)(2,1)S(1)}, bf16[160,128]{1,0:T(8,128)(2,1)S(1)}, u32[]{:S(2)}, u32[]{:S(2)}) collective-permute-start(bf16[160,128]{1,0:T(8,128)(2,1)S(1)} %get-tuple-element.176), channel_id=1, source_target_pairs={{0,1},{1,2},{2,3},{3,0},{4,5},{5,6},{6,7},{7,4},{8,9},{9,10},{10,1... | collective-permute-start | bytes 122888 | tf_op jit(solution)/shard_map/ppermute | solution.py:107
  154.9 16.2 %collective-permute-start.35 = (bf16[160,128]{1,0:T(8,128)(2,1)S(1)}, bf16[160,128]{1,0:T(8,128)(2,1)S(1)}, u32[]{:S(2)}, u32[]{:S(2)}) collective-permute-start(bf16[160,128]{1,0:T(8,128)(2,1)S(1)} %get-tuple-element.177), channel_id=1, source_target_pairs={{0,3},{1,0},{2,1},{3,2},{4,7},{5,4},{6,5},{7,6},{8,11},{9,8},{10,9... | collective-permute-start | bytes 122888 | tf_op jit(solution)/shard_map/ppermute | solution.py:107
  160.0 11.1 %collective-permute-start.34 = (bf16[160,128]{1,0:T(8,128)(2,1)S(1)}, bf16[160,128]{1,0:T(8,128)(2,1)S(1)}, u32[]{:S(2)}, u32[]{:S(2)}) collective-permute-start(bf16[160,128]{1,0:T(8,128)(2,1)S(1)} %get-tuple-element.178), channel_id=1, source_target_pairs={{0,2},{1,3},{2,0},{3,1},{4,6},{5,7},{6,4},{7,5},{8,10},{9,11},{10,... | collective-permute-start | bytes 122888 | tf_op jit(solution)/shard_map/ppermute | solution.py:107
  171.2 8.2 %collective-permute-start.37 = (bf16[912,128]{1,0:T(8,128)(2,1)S(1)}, bf16[912,128]{1,0:T(8,128)(2,1)S(1)}, u32[]{:S(2)}, u32[]{:S(2)}) collective-permute-start(bf16[912,128]{1,0:T(8,128)(2,1)S(1)} %get-tuple-element.180), channel_id=1, source_target_pairs={{0,8},{4,12},{8,0},{12,4},{16,24},{20,28},{24,16},{28,20},{1,9},{5... | collective-permute-start | bytes 700424 | tf_op jit(solution)/shard_map/ppermute | solution.py:102
  172.6 10.5 %collective-permute-start.36 = (bf16[912,128]{1,0:T(8,128)(2,1)S(1)}, bf16[912,128]{1,0:T(8,128)(2,1)S(1)}, u32[]{:S(2)}, u32[]{:S(2)}) collective-permute-start(bf16[912,128]{1,0:T(8,128)(2,1)S(1)} %get-tuple-element.180), channel_id=1, source_target_pairs={{0,16},{4,20},{8,24},{12,28},{16,0},{20,4},{24,8},{28,12},{1,17},{... | collective-permute-start | bytes 700424 | tf_op jit(solution)/shard_map/ppermute | solution.py:102
  174.3 8.8 %collective-permute-start.38 = (bf16[912,128]{1,0:T(8,128)(2,1)S(1)}, bf16[912,128]{1,0:T(8,128)(2,1)S(1)}, u32[]{:S(2)}, u32[]{:S(2)}) collective-permute-start(bf16[912,128]{1,0:T(8,128)(2,1)S(1)} %get-tuple-element.180), channel_id=1, source_target_pairs={{0,24},{4,28},{8,16},{12,20},{16,8},{20,12},{24,0},{28,4},{1,25},{... | collective-permute-start | bytes 700424 | tf_op jit(solution)/shard_map/ppermute | solution.py:102
  183.3 2.6 %collective-permute-start.39 = (bf16[4,912,128]{2,1,0:T(8,128)(2,1)S(1)}, bf16[4,912,128]{2,1,0:T(8,128)(2,1)S(1)}, u32[]{:S(2)}, u32[]{:S(2)}) collective-permute-start(bf16[4,912,128]{2,1,0:T(8,128)(2,1)S(1)} %pad_maximum_fusion.1.refs_1_), channel_id=1, source_target_pairs={{0,4},{4,0},{8,12},{12,8},{16,20},{20,16},{24,28},{28,24},{1,5},{5... | collective-permute-start | bytes 2801672 | tf_op jit(solution)/shard_map/ppermute | solution.py:102
  (1 other events, 0.8 us)

commit v2 on v1

--- a/solution.py
+++ b/solution.py
@@ -12,6 +12,8 @@
 LANES = 128
 SMALL = 16
 MIB = 1024 * 1024
+PROBS_AHEAD = 2
+AHEAD = 4
 BIG = 58
 
 
@@ -419,7 +421,7 @@
         pltpu.make_async_copy(probs_in.at[head], probs.at[head], sems.at[head])
         for head in range(probs.shape[0])
     ]
-    for copy in copies:
+    for copy in copies[:PROBS_AHEAD]:
         copy.start()
     held = refs[:groups]
     query_grad = refs[groups]
@@ -438,6 +440,8 @@
         for head in range(g * per, (g + 1) * per):
             cols = slice(head * head_size, (head + 1) * head_size)
             copies[head].wait()
+            if head + PROBS_AHEAD < len(copies):
+                copies[head + PROBS_AHEAD].start()
             low = probs[head]
             inner = jnp.sum(grad[:, cols].astype(f32) * exact[:, cols], axis=1, keepdims=True)
             scores = dot(grad[:, cols], values, (1, 1)) - inner
@@ -484,23 +488,30 @@
         first, second = (where[2], where[3]) if core == 0 else (where[3], where[2])
         return where[1] ^ core, first ^ (number // 2 % 2), second ^ (number % 2)
 
-    for number in range(8):
+    def fetch(number):
         core, high, low = piece_place(number)
         for place in range(4):
 
             @pl.when(core * 2 + high == place)
-            def _(number=number, low=low, place=place):
+            def _():
                 pltpu.make_async_copy(
                     pieces[place].at[low],
                     weights.at[:, pl.ds(number * w_chunk.part, w_chunk.part)],
                     sem_in.at[number],
                 ).start()
 
-    waited = 0
+    fetched = waited = 0
+
+    def fetch_to(count):
+        nonlocal fetched
+        while fetched < min(count, 8):
+            fetch(fetched)
+            fetched += 1
 
     def need(rows):
         nonlocal waited
         while waited < 8 and waited * w_chunk.part < rows:
+            fetch_to(waited + AHEAD)
             here = weights.at[:, pl.ds(waited * w_chunk.part, w_chunk.part)]
             pltpu.make_async_copy(here, here, sem_in.at[waited]).wait()
             waited += 1
@@ -535,6 +546,7 @@
         for owner in range(groups):
             grads[ahead_of[owner], at : at + shard, :] = block[owner * shard : (owner + 1) * shard]
 
+    fetch_to(AHEAD)
     out_t = out_grad_t[...]
     upstream = turned(out_t)
     inputs = tokens_t[...].astype(f32).T

time: 189 us -> 187 us (0.989)
  starting transfers between devices: 61.5 us -> 57.9 us
  waiting for transfers between devices: 57.3 us -> 60.7 us
    ppermute x15, starting transfers between devices: 29.1 us -> 25.9 us  [shift(): lax.ppermute(value, 'grp', [(i, (i + step) % count) for i in range(count)])]
    ppermute x15, waiting for transfers between devices: 6.01 us -> 9.2 us  [shift(): lax.ppermute(value, 'grp', [(i, (i + step) % count) for i in range(count)])]
  transfers between devices with their start and end apart: 40 -> 40, of which waited for: 19 -> 19; matrix products, arithmetic and copies ran while one was open for 5% -> 5% of each run, Pallas kernels for 17% -> 16%
where the time goes in v2:
time: 187 us; the launch traced here: 186 us
  waiting for transfers between devices  60.7 us (32%)
  starting transfers between devices  57.9 us (31%)
  Pallas kernels  49.3 us (26%)
  other arithmetic  13.6 us (7%)
  local copies, waits for them, and re-layouts  3.73 us (2%)
    pallas_call x8, Pallas kernels, staged_call(): pl.pallas_call(whole, out_shape=out_shape, in_specs=[specs[kind]() for ki...  49.3 us
    ppermute x15, starting transfers between devices, shift(): lax.ppermute(value, 'grp', [(i, (i + step) % count) for i in range(count)])  25.9 us
    ppermute x15, waiting for transfers between devices, hop(): return lax.ppermute(value, 'rep', [(i, i ^ bit) for i in range(count)])  24.7 us
    ppermute x15, starting transfers between devices, hop(): return lax.ppermute(value, 'rep', [(i, i ^ bit) for i in range(count)])  14.2 us
    ppermute x3, waiting for transfers between devices, body(): kv_back.append(lax.ppermute(kv_parts[step], 'grp', back))  12.4 us
    ppermute x4, waiting for transfers between devices, hop_split(): lax.ppermute(value, 'rep', [(i, i ^ (odd if i % 2 else even)) for i in ra...  10 us
    ppermute x15, waiting for transfers between devices, shift(): lax.ppermute(value, 'grp', [(i, (i + step) % count) for i in range(count)])  9.2 us
    ppermute x3, starting transfers between devices, body(): held.append(lax.ppermute(key_value, 'grp', ahead))  7.83 us
  transfers between devices with their start and end apart: 40, of which 19 were waited for; matrix products, arithmetic and copies ran while one was open for 5% of the time, Pallas kernels for 16%

profile of v2, /device:TPU:0, one launch (start us, length us, event | category | flops | bytes accessed | tf_op | source)
XLA Modules:
  0.0 186.5 jit_solution(3618166635865844463)
XLA Ops:
  0.7 0.6 pad_add_fusion.1.refs_0_
  1.3 3.2 %pack.1 = (bf16[144,128]{1,0:T(8,128)(2,1)}, bf16[752,128]{1,0:T(8,128)(2,1)}) custom-call(s32[4]{0:T(128)} %pad_add_fusion.1.refs_0_, bf16[144,576]{1,0:T(8,128)(2,1)} %refs_1_.1, bf16[144,192]{1,0:T(8,128)(2,1)} %refs_2_.1, bf16[144,192]{1,0:T(8,128)(2,1)} %refs_3_.1, bf16[144,1536]{1,0:T(8,128)(2,1)} %refs_4_.1, bf16[144,1536]{1,0:T(8,128)(2,1)} %refs_5_.1, ...), custom_call_target="tpu_custom_call" | custom-call | flops 1 | bytes 1024 | tf_op jit(solution)/shard_map/pack/pallas_call | solution.py:86
  4.6 5.1 %collective-permute-start.13 = (bf16[16,128]{1,0:T(8,128)(2,1)S(1)}, bf16[16,128]{1,0:T(8,128)(2,1)S(1)}, u32[]{:S(2)}, u32[]{:S(2)}) collective-permute-start(bf16[16,128]{1,0:T(8,128)(2,1)S(1)} %get-tuple-element.190), channel_id=1, source_target_pairs={{0,3},{1,0},{2,1},{3,2},{4,7},{5,4},{6,5},{7,6},{8,11},{9,8},{10,9... | collective-permute-start | bytes 12296 | tf_op jit(solution)/shard_map/ppermute | solution.py:109
  9.7 1.0 collective-permute-start.11
  10.7 2.8 %collective-permute-start.2 = (bf16[144,128]{1,0:T(8,128)(2,1)}, bf16[144,128]{1,0:T(8,128)(2,1)S(1)}, u32[]{:S(2)}, u32[]{:S(2)}) collective-permute-start(bf16[144,128]{1,0:T(8,128)(2,1)} %get-tuple-element.89), channel_id=1, source_target_pairs={{0,3},{1,0},{2,1},{3,2},{4,7},{5,4},{6,5},{7,6},{8,11},{9,8},{10,9... | collective-permute-start | bytes 110600 | tf_op jit(solution)/shard_map/ppermute | solution.py:109
  13.5 1.1 collective-permute-start.1
  14.9 3.8 %collective-permute-start.8 = (bf16[752,128]{1,0:T(8,128)(2,1)}, bf16[752,128]{1,0:T(8,128)(2,1)S(1)}, u32[]{:S(2)}, u32[]{:S(2)}) collective-permute-start(bf16[752,128]{1,0:T(8,128)(2,1)} %get-tuple-element.91), channel_id=1, source_target_pairs={{0,3},{1,0},{2,1},{3,2},{4,7},{5,4},{6,5},{7,6},{8,11},{9,8},{10,9... | collective-permute-start | bytes 577544 | tf_op jit(solution)/shard_map/ppermute | solution.py:109
  18.8 0.6 gather_fusion
  20.2 0.7 collective-permute-start.6
  21.4 0.8 fusion.33
  22.2 1.6 collective-permute-start.4
  23.8 1.5 collective-permute-start.3
  25.3 2.7 %collective-permute-done.4 = bf16[4,144,128]{2,1,0:T(8,128)(2,1)S(1)} collective-permute-done((bf16[4,144,128]{2,1,0:T(8,128)(2,1)S(1)}, bf16[4,144,128]{2,1,0:T(8,128)(2,1)S(1)}, u32[]{:S(2)}, u32[]{:S(2)}) %collective-permute-start.4) | collective-permute-done | bytes 147488 | tf_op jit(solution)/shard_map/ppermute | solution.py:104
  27.9 3.5 %collective-permute-start.5 = (bf16[4,144,128]{2,1,0:T(8,128)(2,1)S(1)}, bf16[4,144,128]{2,1,0:T(8,128)(2,1)S(1)}, u32[]{:S(2)}, u32[]{:S(2)}) collective-permute-start(bf16[4,144,128]{2,1,0:T(8,128)(2,1)S(1)} %get-tuple-element.182), channel_id=1, source_target_pairs={{0,24},{4,28},{8,16},{12,20},{16,8},{20,12},{24,0},{28,4},{1,25},{... | collective-permute-start | bytes 442376 | tf_op jit(solution)/shard_map/ppermute | solution.py:104
  31.4 3.1 %collective-permute-done.5 = bf16[4,144,128]{2,1,0:T(8,128)(2,1)S(1)} collective-permute-done((bf16[4,144,128]{2,1,0:T(8,128)(2,1)S(1)}, bf16[4,144,128]{2,1,0:T(8,128)(2,1)S(1)}, u32[]{:S(2)}, u32[]{:S(2)}) %collective-permute-start.5) | collective-permute-done | bytes 147488 | tf_op jit(solution)/shard_map/ppermute | solution.py:104
  34.6 1.0 collective-permute-done.7
  35.6 1.3 fusion.34
  36.9 1.5 collective-permute-start.9
  38.4 0.6 broadcast_select_fusion.refs_2_
  39.2 0.7 reshape.259.refs_4_
  40.0 2.0 %collective-permute-done.14.refs_2_ = bf16[4,4,144,128]{3,2,1,0:T(8,128)(2,1)S(1)} collective-permute-done((bf16[4,4,144,128]{3,2,1,0:T(8,128)(2,1)S(1)}, bf16[4,4,144,128]{3,2,1,0:T(8,128)(2,1)S(1)}, u32[]{:S(2)}, u32[]{:S(2)}) %collective-permute-start.14) | collective-permute-done | bytes 589856 | tf_op jit(solution)/shard_map/ppermute | solution.py:104
  42.0 5.1 %proj.1 = (bf16[256,576]{1,0:T(8,128)(2,1)S(1)}, f32[256,768]{1,0:T(8,128)S(1)}, bf16[256,576]{1,0:T(8,128)(2,1)S(1)}, bf16[256,384]{1,0:T(8,128)(2,1)S(1)}, bf16[576,1024]{1,0:T(8,128)(2,1)S(1)}) custom-call(s32[4]{0:T(128)S(1)} %copy-done.7, bf16[4,4,144,128]{3,2,1,0:T(8,128)(2,1)S(1)} %pad_maximum_fusion.3.refs_1_, ...), custom_call_target="tpu_custom_call" | custom-call | flops 1 | bytes 1024 | tf_op jit(solution)/shard_map/proj/pallas_call | solution.py:86
  47.2 3.3 %collective-permute-start.17 = (bf16[256,384]{1,0:T(8,128)(2,1)S(1)}, bf16[256,384]{1,0:T(8,128)(2,1)S(1)}, u32[]{:S(2)}, u32[]{:S(2)}) collective-permute-start(bf16[256,384]{1,0:T(8,128)(2,1)S(1)} %get-tuple-element.106.refs_3_), channel_id=1, source_target_pairs={{0,3},{4,7},{8,11},{12,15},{16,19},{20,23},{24,27},{28,31}} | collective-permute-start | bytes 589832 | tf_op jit(solution)/shard_map/ppermute | solution.py:912
  50.5 3.1 %collective-permute-start.16 = (bf16[256,384]{1,0:T(8,128)(2,1)S(1)}, bf16[256,384]{1,0:T(8,128)(2,1)S(1)}, u32[]{:S(2)}, u32[]{:S(2)}) collective-permute-start(bf16[256,384]{1,0:T(8,128)(2,1)S(1)} %get-tuple-element.106.refs_3_), channel_id=1, source_target_pairs={{0,2},{1,3},{4,6},{5,7},{8,10},{9,11},{12,14},{13,15},{16,18},{17,... | collective-permute-start | bytes 589832 | tf_op jit(solution)/shard_map/ppermute | solution.py:912
  53.5 1.5 collective-permute-start.15
  55.0 2.5 %pad_maximum_fusion.refs_5_ = bf16[2,4,752,128]{3,2,1,0:T(8,128)(2,1)} fusion(bf16[1,4,752,128]{3,2,1,0:T(8,128)(2,1)} %bitcast.18, bf16[1,4,752,128]{3,2,1,0:T(8,128)(2,1)S(1)} %copy-done.10), kind=kLoop, calls=%fused_computation.3 | loop fusion | flops 770048 | bytes 3080192 | tf_op jit(solution)/shard_map/stack | solution.py:913
  57.5 1.5 collective-permute-start.10
  59.0 0.9 collective-permute-done.16.refs_5_
  60.0 3.4 %collective-permute-done.15.refs_4_ = bf16[256,384]{1,0:T(8,128)(2,1)S(1)} collective-permute-done((bf16[256,384]{1,0:T(8,128)(2,1)S(1)}, bf16[256,384]{1,0:T(8,128)(2,1)S(1)}, u32[]{:S(2)}, u32[]{:S(2)}) %collective-permute-start.15) | collective-permute-done | bytes 196640 | tf_op jit(solution)/shard_map/ppermute | solution.py:912
  63.4 0.8 copy.28.refs_1_
  64.2 7.5 %attend.1 = (bf16[256,576]{1,0:T(8,128)(2,1)}, f32[256,576]{1,0:T(8,128)}, bf16[9,256,1024]{2,1,0:T(8,128)(2,1)}) custom-call(bf16[256,576]{1,0:T(8,128)(2,1)} %copy-done.2, f32[256,1]{1,0:T(8,128)} %copy.28.refs_1_, f32[1,1024]{1,0:T(1,128)} %broadcast_select_fusion.refs_2_, bf16[256,384]{1,0:T(8,128)(2,1)} %copy-done.3, bf16[256,384]{1,0:T(8,128)(2,1)} %copy-done.15, ...), custom_call_target="tpu_custom_call" | custom-call | flops 1 | bytes 1024 | tf_op jit(solution)/shard_map/attend/pallas_call | solution.py:86
  71.6 6.3 %collective-permute-done.10.refs_6_ = bf16[2,4,752,128]{3,2,1,0:T(8,128)(2,1)} collective-permute-done((bf16[2,4,752,128]{3,2,1,0:T(8,128)(2,1)}, bf16[2,4,752,128]{3,2,1,0:T(8,128)(2,1)}, u32[]{:S(2)}, u32[]{:S(2)}) %collective-permute-start.10) | collective-permute-done | bytes 1540128 | tf_op jit(solution)/shard_map/ppermute | solution.py:119
  77.9 3.6 %collective-permute-done.19.refs_8_ = bf16[2,4,752,128]{3,2,1,0:T(8,128)(2,1)S(1)} collective-permute-done((bf16[2,4,752,128]{3,2,1,0:T(8,128)(2,1)}, bf16[2,4,752,128]{3,2,1,0:T(8,128)(2,1)S(1)}, u32[]{:S(2)}, u32[]{:S(2)}) %collective-permute-start.19) | collective-permute-done | bytes 1540128 | tf_op jit(solution)/shard_map/ppermute | solution.py:104
  81.5 1.2 copy-done.12
  82.7 13.3 %mlp.1 = (bf16[576,256]{1,0:T(8,128)(2,1)}, f32[256,576]{1,0:T(8,128)}, bf16[256,576]{1,0:T(8,128)(2,1)}, f32[1,576]{1,0:T(1,128)}, bf16[2,2,4,752,128]{4,3,2,1,...) custom-call(s32[4]{0:T(128)} %pad_add_fusion.1.refs_0_, bf16[256,576]{1,0:T(8,128)(2,1)} %get-tuple-element.112.refs_1_, ...), custom_call_target="tpu_custom_call" | custom-call | flops 1 | bytes 1024 | tf_op jit(solution)/shard_map/mlp/pallas_call | solution.py:86
  96.3 9.0 %attend_back.1 = (f32[256,576]{1,0:T(8,128)}, bf16[256,384]{1,0:T(8,128)(2,1)}, bf16[256,384]{1,0:T(8,128)(2,1)}, bf16[256,384]{1,0:T(8,128)(2,1)}, bf16[256,384]{1,0:T(8,128)(2,1)}) custom-call(bf16[256,576]{1,0:T(8,128)(2,1)} %copy-done.2, bf16[256,576]{1,0:T(8,128)(2,1)} %get-tuple-element.119.refs_1_, f32[256,576]{1,0:T(8,128)} %get-tuple-element.120.refs_2_, ...), custom_call_target="tpu_custom_call" | custom-call | flops 1 | bytes 1024 | tf_op jit(solution)/shard_map/attend_back/pallas_call | solution.py:86
  105.3 2.4 %fusion = bf16[2,4,752,128]{3,2,1,0:T(8,128)(2,1)S(1)} fusion(bf16[2,2,4,752,128]{4,3,2,1,0:T(8,128)(2,1)} %collective-permute-done.20, bf16[2,2,4,752,128]{4,3,2,1,0:T(8,128)(2,1)} %get-tuple-element.117), kind=kLoop, calls=%fused_computation.2 | loop fusion | flops 3080192 | bytes 4620288 | tf_op jit(solution)/shard_map/convert_element_type | solution.py:126
  107.7 1.5 collective-permute-start.21
  109.2 1.3 collective-permute-start.22
  110.5 1.3 collective-permute-start.23
  111.8 1.3 collective-permute-start.24
  113.1 4.3 %query_back.1 = (bf16[576,576]{1,0:T(8,128)(2,1)S(1)}, f32[256,576]{1,0:T(8,128)S(1)}, f32[1,64]{1,0:T(1,128)S(1)}) custom-call(f32[256,576]{1,0:T(8,128)S(1)} %copy-done.5, f32[256,768]{1,0:T(8,128)S(1)} %get-tuple-element.133.refs_1_.refs_4_, bf16[256,576]{1,0:T(8,128)(2,1)S(1)} %get-tuple-element.134.refs_2_.refs_5_, ...), custom_call_target="tpu_custom_call" | custom-call | flops 1 | bytes 1024 | tf_op jit(solution)/shard_map/query_back/pallas_call | solution.py:86
  117.4 0.9 collective-permute-done.22.refs_15_
  118.3 11.5 %collective-permute-done.23.refs_16_ = bf16[256,384]{1,0:T(8,128)(2,1)S(1)} collective-permute-done((bf16[256,384]{1,0:T(8,128)(2,1)S(1)}, bf16[256,384]{1,0:T(8,128)(2,1)S(1)}, u32[]{:S(2)}, u32[]{:S(2)}) %collective-permute-start.23) | collective-permute-done | bytes 196640 | tf_op jit(solution)/shard_map/ppermute | solution.py:929
  129.8 1.6 fusion.1
  131.4 1.6 collective-permute-start.25
  133.0 4.3 %last.1 = (f32[576,256]{1,0:T(8,128)}, bf16[4,4,160,128]{3,2,1,0:T(8,128)(2,1)S(1)}, bf16[4,4,160,128]{3,2,1,0:T(8,128)(2,1)S(1)}) custom-call(s32[4]{0:T(128)S(1)} %copy-done.8, bf16[576,576]{1,0:T(8,128)(2,1)S(1)} %get-tuple-element.139.refs_1_, f32[256,576]{1,0:T(8,128)S(1)} %get-tuple-element.140.refs_2_, f32[1,64]{1,0:T(1,128)S(1)} %get-tuple-element.141.refs_3_, ...), custom_call_target="tpu_custom_call" | custom-call | flops 1 | bytes 1024 | tf_op jit(solution)/shard_map/last/pallas_call | solution.py:86
  137.5 2.1 %collective-permute-done.26 = bf16[4,4,160,128]{3,2,1,0:T(8,128)(2,1)S(1)} collective-permute-done((bf16[4,4,160,128]{3,2,1,0:T(8,128)(2,1)S(1)}, bf16[4,4,160,128]{3,2,1,0:T(8,128)(2,1)S(1)}, u32[]{:S(2)}, u32[]{:S(2)}) %collective-permute-start.26) | collective-permute-done | bytes 655392 | tf_op jit(solution)/shard_map/ppermute | solution.py:104
  139.5 3.8 %collective-permute-done.25 = bf16[4,752,128]{2,1,0:T(8,128)(2,1)S(1)} collective-permute-done((bf16[4,752,128]{2,1,0:T(8,128)(2,1)S(1)}, bf16[4,752,128]{2,1,0:T(8,128)(2,1)S(1)}, u32[]{:S(2)}, u32[]{:S(2)}) %collective-permute-start.25) | collective-permute-done | bytes 770080 | tf_op jit(solution)/shard_map/ppermute | solution.py:119
  143.5 2.1 %collective-permute-start.32 = (bf16[4,160,128]{2,1,0:T(8,128)(2,1)S(1)}, bf16[4,160,128]{2,1,0:T(8,128)(2,1)S(1)}, u32[]{:S(2)}, u32[]{:S(2)}) collective-permute-start(bf16[4,160,128]{2,1,0:T(8,128)(2,1)S(1)} %get-tuple-element.171), channel_id=1, source_target_pairs={{0,24},{4,28},{8,16},{12,20},{16,8},{20,12},{24,0},{28,4},{1,25},{... | collective-permute-start | bytes 491528 | tf_op jit(solution)/shard_map/ppermute | solution.py:104
  145.6 0.9 collective-permute-start.31
  147.0 1.4 fusion.4
  148.5 3.8 %collective-permute-start.29 = (bf16[752,128]{1,0:T(8,128)(2,1)S(1)}, bf16[752,128]{1,0:T(8,128)(2,1)S(1)}, u32[]{:S(2)}, u32[]{:S(2)}) collective-permute-start(bf16[752,128]{1,0:T(8,128)(2,1)S(1)} %get-tuple-element.168), channel_id=1, source_target_pairs={{0,3},{1,0},{2,1},{3,2},{4,7},{5,4},{6,5},{7,6},{8,11},{9,8},{10,9... | collective-permute-start | bytes 577544 | tf_op jit(solution)/shard_map/ppermute | solution.py:109
  153.1 3.6 %collective-permute-start.35 = (bf16[160,128]{1,0:T(8,128)(2,1)S(1)}, bf16[160,128]{1,0:T(8,128)(2,1)S(1)}, u32[]{:S(2)}, u32[]{:S(2)}) collective-permute-start(bf16[160,128]{1,0:T(8,128)(2,1)S(1)} %get-tuple-element.177), channel_id=1, source_target_pairs={{0,3},{1,0},{2,1},{3,2},{4,7},{5,4},{6,5},{7,6},{8,11},{9,8},{10,9... | collective-permute-start | bytes 122888 | tf_op jit(solution)/shard_map/ppermute | solution.py:109
  156.7 1.5 collective-permute-done.27
  158.2 3.6 %collective-permute-start.34 = (bf16[160,128]{1,0:T(8,128)(2,1)S(1)}, bf16[160,128]{1,0:T(8,128)(2,1)S(1)}, u32[]{:S(2)}, u32[]{:S(2)}) collective-permute-start(bf16[160,128]{1,0:T(8,128)(2,1)S(1)} %get-tuple-element.178), channel_id=1, source_target_pairs={{0,2},{1,3},{2,0},{3,1},{4,6},{5,7},{6,4},{7,5},{8,10},{9,11},{10,... | collective-permute-start | bytes 122888 | tf_op jit(solution)/shard_map/ppermute | solution.py:109
  161.8 6.2 %collective-permute-done.28 = bf16[752,128]{1,0:T(8,128)(2,1)S(1)} collective-permute-done((bf16[752,128]{1,0:T(8,128)(2,1)S(1)}, bf16[752,128]{1,0:T(8,128)(2,1)S(1)}, u32[]{:S(2)}, u32[]{:S(2)}) %collective-permute-start.28) | collective-permute-done | bytes 192544 | tf_op jit(solution)/shard_map/ppermute | solution.py:109
  167.9 1.1 add_convert_fusion.1
  169.1 1.5 collective-permute-start.37
  170.6 1.7 collective-permute-start.36
  172.7 4.7 %collective-permute-done.37 = bf16[912,128]{1,0:T(8,128)(2,1)S(1)} collective-permute-done((bf16[912,128]{1,0:T(8,128)(2,1)S(1)}, bf16[912,128]{1,0:T(8,128)(2,1)S(1)}, u32[]{:S(2)}, u32[]{:S(2)}) %collective-permute-start.37) | collective-permute-done | bytes 233504 | tf_op jit(solution)/shard_map/ppermute | solution.py:104
  177.4 3.8 %collective-permute-done.36 = bf16[912,128]{1,0:T(8,128)(2,1)S(1)} collective-permute-done((bf16[912,128]{1,0:T(8,128)(2,1)S(1)}, bf16[912,128]{1,0:T(8,128)(2,1)S(1)}, u32[]{:S(2)}, u32[]{:S(2)}) %collective-permute-start.36) | collective-permute-done | bytes 233504 | tf_op jit(solution)/shard_map/ppermute | solution.py:104
  181.4 2.5 %collective-permute-done.39.refs_2_ = bf16[4,912,128]{2,1,0:T(8,128)(2,1)S(1)} collective-permute-done((bf16[4,912,128]{2,1,0:T(8,128)(2,1)S(1)}, bf16[4,912,128]{2,1,0:T(8,128)(2,1)S(1)}, u32[]{:S(2)}, u32[]{:S(2)}) %collective-permute-start.39) | collective-permute-done | bytes 933920 | tf_op jit(solution)/shard_map/ppermute | solution.py:104
  183.8 2.7 %unpack.1 = (f32[144,1536]{1,0:T(8,128)}, f32[144,1536]{1,0:T(8,128)}, f32[576,384]{1,0:T(8,128)}, f32[144,576]{1,0:T(8,128)}, f32[144,576]{1,0:T(8,128)}, /*ind...) custom-call(s32[4]{0:T(128)S(1)} %copy-done.8, ...), custom_call_target="tpu_custom_call" | custom-call | flops 1 | bytes 1024 | tf_op jit(solution)/shard_map/unpack/pallas_call | solution.py:86
  (116 shorter events, 4.7 us)
Async XLA Ops:
  0.6 3.8 %copy-start.24 = (s32[256]{0:T(256)S(1)}, s32[256]{0:T(256)}, u32[]{:S(2)}) copy-start(s32[256]{0:T(256)} %param.15) | copy-start | bytes 3076
  0.7 3.8 %copy-start.19 = (bf16[144]{0:T(256)(128)(2,1)S(1)}, bf16[144]{0:T(256)(128)(2,1)}, u32[]{:S(2)}) copy-start(bf16[144]{0:T(256)(128)(2,1)} %param.24) | copy-start | bytes 868
  0.7 3.8 %copy-start.17 = (bf16[16]{0:T(256)(128)(2,1)S(1)}, bf16[16]{0:T(256)(128)(2,1)}, u32[]{:S(2)}) copy-start(bf16[16]{0:T(256)(128)(2,1)} %param.19) | copy-start | bytes 100
  0.7 3.8 %copy-start.18 = (bf16[16]{0:T(256)(128)(2,1)S(1)}, bf16[16]{0:T(256)(128)(2,1)}, u32[]{:S(2)}) copy-start(bf16[16]{0:T(256)(128)(2,1)} %param.18) | copy-start | bytes 100
  0.7 3.8 %copy-start.20 = (bf16[144]{0:T(256)(128)(2,1)S(1)}, bf16[144]{0:T(256)(128)(2,1)}, u32[]{:S(2)}) copy-start(bf16[144]{0:T(256)(128)(2,1)} %param.17) | copy-start | bytes 868
  4.5 31.1 %copy-start.16 = (bf16[752,128]{1,0:T(8,128)(2,1)S(1)}, bf16[752,128]{1,0:T(8,128)(2,1)}, u32[]{:S(2)}) copy-start(bf16[752,128]{1,0:T(8,128)(2,1)} %get-tuple-element.91) | copy-start | bytes 577540
  4.6 10.3 %collective-permute-start.13 = (bf16[16,128]{1,0:T(8,128)(2,1)S(1)}, bf16[16,128]{1,0:T(8,128)(2,1)S(1)}, u32[]{:S(2)}, u32[]{:S(2)}) collective-permute-start(bf16[16,128]{1,0:T(8,128)(2,1)S(1)} %get-tuple-element.190), channel_id=1, source_target_pairs={{0,3},{1,0},{2,1},{3,2},{4,7},{5,4},{6,5},{7,6},{8,11},{9,8},{10,9... | collective-permute-start | bytes 12296 | tf_op jit(solution)/shard_map/ppermute | solution.py:109
  9.7 5.2 %collective-permute-start.12 = (bf16[16,128]{1,0:T(8,128)(2,1)S(1)}, bf16[16,128]{1,0:T(8,128)(2,1)S(1)}, u32[]{:S(2)}, u32[]{:S(2)}) collective-permute-start(bf16[16,128]{1,0:T(8,128)(2,1)S(1)} %get-tuple-element.190), channel_id=1, source_target_pairs={{0,2},{1,3},{2,0},{3,1},{4,6},{5,7},{6,4},{7,5},{8,10},{9,11},{10,... | collective-permute-start | bytes 12296 | tf_op jit(solution)/shard_map/ppermute | solution.py:109
  9.7 9.0 %collective-permute-start.11 = (bf16[16,128]{1,0:T(8,128)(2,1)S(1)}, bf16[16,128]{1,0:T(8,128)(2,1)S(1)}, u32[]{:S(2)}, u32[]{:S(2)}) collective-permute-start(bf16[16,128]{1,0:T(8,128)(2,1)S(1)} %get-tuple-element.190), channel_id=1, source_target_pairs={{0,1},{1,2},{2,3},{3,0},{4,5},{5,6},{6,7},{7,4},{8,9},{9,10},{10,1... | collective-permute-start | bytes 12296 | tf_op jit(solution)/shard_map/ppermute | solution.py:109
  10.7 9.5 %collective-permute-start.2 = (bf16[144,128]{1,0:T(8,128)(2,1)}, bf16[144,128]{1,0:T(8,128)(2,1)S(1)}, u32[]{:S(2)}, u32[]{:S(2)}) collective-permute-start(bf16[144,128]{1,0:T(8,128)(2,1)} %get-tuple-element.89), channel_id=1, source_target_pairs={{0,3},{1,0},{2,1},{3,2},{4,7},{5,4},{6,5},{7,6},{8,11},{9,8},{10,9... | collective-permute-start | bytes 110600 | tf_op jit(solution)/shard_map/ppermute | solution.py:109
  13.5 7.4 %collective-permute-start.1 = (bf16[144,128]{1,0:T(8,128)(2,1)}, bf16[144,128]{1,0:T(8,128)(2,1)S(1)}, u32[]{:S(2)}, u32[]{:S(2)}) collective-permute-start(bf16[144,128]{1,0:T(8,128)(2,1)} %get-tuple-element.89), channel_id=1, source_target_pairs={{0,2},{1,3},{2,0},{3,1},{4,6},{5,7},{6,4},{7,5},{8,10},{9,11},{10,... | collective-permute-start | bytes 110600 | tf_op jit(solution)/shard_map/ppermute | solution.py:109
  14.8 6.6 %collective-permute-start = (bf16[144,128]{1,0:T(8,128)(2,1)}, bf16[144,128]{1,0:T(8,128)(2,1)S(1)}, u32[]{:S(2)}, u32[]{:S(2)}) collective-permute-start(bf16[144,128]{1,0:T(8,128)(2,1)} %get-tuple-element.89), channel_id=1, source_target_pairs={{0,1},{1,2},{2,3},{3,0},{4,5},{5,6},{6,7},{7,4},{8,9},{9,10},{10,1... | collective-permute-start | bytes 110600 | tf_op jit(solution)/shard_map/ppermute | solution.py:109
  14.9 19.7 %collective-permute-start.8 = (bf16[752,128]{1,0:T(8,128)(2,1)}, bf16[752,128]{1,0:T(8,128)(2,1)S(1)}, u32[]{:S(2)}, u32[]{:S(2)}) collective-permute-start(bf16[752,128]{1,0:T(8,128)(2,1)} %get-tuple-element.91), channel_id=1, source_target_pairs={{0,3},{1,0},{2,1},{3,2},{4,7},{5,4},{6,5},{7,6},{8,11},{9,8},{10,9... | collective-permute-start | bytes 577544 | tf_op jit(solution)/shard_map/ppermute | solution.py:109
  18.7 16.9 %collective-permute-start.7 = (bf16[752,128]{1,0:T(8,128)(2,1)}, bf16[752,128]{1,0:T(8,128)(2,1)S(1)}, u32[]{:S(2)}, u32[]{:S(2)}) collective-permute-start(bf16[752,128]{1,0:T(8,128)(2,1)} %get-tuple-element.91), channel_id=1, source_target_pairs={{0,2},{1,3},{2,0},{3,1},{4,6},{5,7},{6,4},{7,5},{8,10},{9,11},{10,... | collective-permute-start | bytes 577544 | tf_op jit(solution)/shard_map/ppermute | solution.py:109
  20.2 15.4 %collective-permute-start.6 = (bf16[752,128]{1,0:T(8,128)(2,1)}, bf16[752,128]{1,0:T(8,128)(2,1)S(1)}, u32[]{:S(2)}, u32[]{:S(2)}) collective-permute-start(bf16[752,128]{1,0:T(8,128)(2,1)} %get-tuple-element.91), channel_id=1, source_target_pairs={{0,1},{1,2},{2,3},{3,0},{4,5},{5,6},{6,7},{7,4},{8,9},{9,10},{10,1... | collective-permute-start | bytes 577544 | tf_op jit(solution)/shard_map/ppermute | solution.py:109
  22.2 5.7 %collective-permute-start.4 = (bf16[4,144,128]{2,1,0:T(8,128)(2,1)S(1)}, bf16[4,144,128]{2,1,0:T(8,128)(2,1)S(1)}, u32[]{:S(2)}, u32[]{:S(2)}) collective-permute-start(bf16[4,144,128]{2,1,0:T(8,128)(2,1)S(1)} %get-tuple-element.182), channel_id=1, source_target_pairs={{0,8},{4,12},{8,0},{12,4},{16,24},{20,28},{24,16},{28,20},{1,9},{5... | collective-permute-start | bytes 442376 | tf_op jit(solution)/shard_map/ppermute | solution.py:104
  23.8 7.7 %collective-permute-start.3 = (bf16[4,144,128]{2,1,0:T(8,128)(2,1)S(1)}, bf16[4,144,128]{2,1,0:T(8,128)(2,1)S(1)}, u32[]{:S(2)}, u32[]{:S(2)}) collective-permute-start(bf16[4,144,128]{2,1,0:T(8,128)(2,1)S(1)} %get-tuple-element.182), channel_id=1, source_target_pairs={{0,16},{4,20},{8,24},{12,28},{16,0},{20,4},{24,8},{28,12},{1,17},{... | collective-permute-start | bytes 442376 | tf_op jit(solution)/shard_map/ppermute | solution.py:104
  27.9 6.6 %collective-permute-start.5 = (bf16[4,144,128]{2,1,0:T(8,128)(2,1)S(1)}, bf16[4,144,128]{2,1,0:T(8,128)(2,1)S(1)}, u32[]{:S(2)}, u32[]{:S(2)}) collective-permute-start(bf16[4,144,128]{2,1,0:T(8,128)(2,1)S(1)} %get-tuple-element.182), channel_id=1, source_target_pairs={{0,24},{4,28},{8,16},{12,20},{16,8},{20,12},{24,0},{28,4},{1,25},{... | collective-permute-start | bytes 442376 | tf_op jit(solution)/shard_map/ppermute | solution.py:104
  34.5 7.5 %copy-start = (bf16[256,576]{0,1:T(8,128)(2,1)S(1)}, bf16[256,576]{0,1:T(8,128)(2,1)}, u32[]{:S(2)}) copy-start(bf16[256,576]{0,1:T(8,128)(2,1)} %param.14) | copy-start | bytes 884740
  34.5 7.5 %copy-start.7 = (s32[4]{0:T(128)S(1)}, s32[4]{0:T(128)}, u32[]{:S(2)}) copy-start(s32[4]{0:T(128)} %pad_add_fusion.1.refs_0_) | copy-start | bytes 52
  36.9 18.2 %collective-permute-start.9 = (bf16[4,752,128]{2,1,0:T(8,128)(2,1)}, bf16[4,752,128]{2,1,0:T(8,128)(2,1)}, u32[]{:S(2)}, u32[]{:S(2)}) collective-permute-start(bf16[4,752,128]{2,1,0:T(8,128)(2,1)} %get-tuple-element.175), channel_id=1, source_target_pairs={{0,16},{4,12},{8,24},{12,4},{16,0},{20,28},{24,8},{28,20},{1,17},{... | collective-permute-start | bytes 2310152 | tf_op jit(solution)/shard_map/ppermute | solution.py:119
  39.9 15.1 %copy-start.10 = (bf16[1,4,752,128]{3,2,1,0:T(8,128)(2,1)S(1)}, bf16[1,4,752,128]{3,2,1,0:T(8,128)(2,1)}, u32[]{:S(2)}) copy-start(bf16[1,4,752,128]{3,2,1,0:T(8,128)(2,1)} %get-tuple-element.174) | copy-start | bytes 2310148
  39.9 2.1 %collective-permute-start.14 = (bf16[4,4,144,128]{3,2,1,0:T(8,128)(2,1)S(1)}, bf16[4,4,144,128]{3,2,1,0:T(8,128)(2,1)S(1)}, u32[]{:S(2)}, u32[]{:S(2)}) collective-permute-start(bf16[4,4,144,128]{3,2,1,0:T(8,128)(2,1)S(1)} %pad_maximum_fusion.3.refs_1_), channel_id=1, source_target_pairs={{0,4},{4,0},{8,12},{12,8},{16,20},{20,16},{24,28},{28,24},{1,5},{5... | collective-permute-start | bytes 1769480 | tf_op jit(solution)/shard_map/ppermute | solution.py:104
  47.1 10.4 %copy-start.2 = (bf16[256,576]{1,0:T(8,128)(2,1)}, bf16[256,576]{1,0:T(8,128)(2,1)S(1)}, u32[]{:S(2)}) copy-start(bf16[256,576]{1,0:T(8,128)(2,1)S(1)} %get-tuple-element.102.refs_0_) | copy-start | bytes 884740
  47.2 10.4 %copy-start.3 = (bf16[256,384]{1,0:T(8,128)(2,1)}, bf16[256,384]{1,0:T(8,128)(2,1)S(1)}, u32[]{:S(2)}) copy-start(bf16[256,384]{1,0:T(8,128)(2,1)S(1)} %get-tuple-element.106.refs_3_) | copy-start | bytes 589828
  47.2 11.9 %collective-permute-start.17 = (bf16[256,384]{1,0:T(8,128)(2,1)S(1)}, bf16[256,384]{1,0:T(8,128)(2,1)S(1)}, u32[]{:S(2)}, u32[]{:S(2)}) collective-permute-start(bf16[256,384]{1,0:T(8,128)(2,1)S(1)} %get-tuple-element.106.refs_3_), channel_id=1, source_target_pairs={{0,3},{4,7},{8,11},{12,15},{16,19},{20,23},{24,27},{28,31}} | collective-permute-start | bytes 589832 | tf_op jit(solution)/shard_map/ppermute | solution.py:912
  50.5 9.5 %collective-permute-start.16 = (bf16[256,384]{1,0:T(8,128)(2,1)S(1)}, bf16[256,384]{1,0:T(8,128)(2,1)S(1)}, u32[]{:S(2)}, u32[]{:S(2)}) collective-permute-start(bf16[256,384]{1,0:T(8,128)(2,1)S(1)} %get-tuple-element.106.refs_3_), channel_id=1, source_target_pairs={{0,2},{1,3},{4,6},{5,7},{8,10},{9,11},{12,14},{13,15},{16,18},{17,... | collective-permute-start | bytes 589832 | tf_op jit(solution)/shard_map/ppermute | solution.py:912
  53.5 9.8 %collective-permute-start.15 = (bf16[256,384]{1,0:T(8,128)(2,1)S(1)}, bf16[256,384]{1,0:T(8,128)(2,1)S(1)}, u32[]{:S(2)}, u32[]{:S(2)}) collective-permute-start(bf16[256,384]{1,0:T(8,128)(2,1)S(1)} %get-tuple-element.106.refs_3_), channel_id=1, source_target_pairs={{0,1},{1,2},{2,3},{4,5},{5,6},{6,7},{8,9},{9,10},{10,11},{12,13},{... | collective-permute-start | bytes 589832 | tf_op jit(solution)/shard_map/ppermute | solution.py:912
  57.5 20.4 %collective-permute-start.10 = (bf16[2,4,752,128]{3,2,1,0:T(8,128)(2,1)}, bf16[2,4,752,128]{3,2,1,0:T(8,128)(2,1)}, u32[]{:S(2)}, u32[]{:S(2)}) collective-permute-start(bf16[2,4,752,128]{3,2,1,0:T(8,128)(2,1)} %pad_maximum_fusion.refs_5_), channel_id=1, source_target_pairs={{0,8},{4,20},{8,0},{12,28},{16,24},{20,4},{24,16},{28,12},{1,9},{5... | collective-permute-start | bytes 4620296 | tf_op jit(solution)/shard_map/ppermute | solution.py:119
  59.0 5.1 %copy-start.13 = (bf16[256,384]{1,0:T(8,128)(2,1)}, bf16[256,384]{1,0:T(8,128)(2,1)S(1)}, u32[]{:S(2)}) copy-start(bf16[256,384]{1,0:T(8,128)(2,1)S(1)} %collective-permute-done.17.refs_6_) | copy-start | bytes 589828
  60.0 4.2 %copy-start.14 = (bf16[256,384]{1,0:T(8,128)(2,1)}, bf16[256,384]{1,0:T(8,128)(2,1)S(1)}, u32[]{:S(2)}) copy-start(bf16[256,384]{1,0:T(8,128)(2,1)S(1)} %collective-permute-done.16.refs_5_) | copy-start | bytes 589828
  63.4 14.5 %collective-permute-start.18 = (bf16[2,4,752,128]{3,2,1,0:T(8,128)(2,1)}, bf16[2,4,752,128]{3,2,1,0:T(8,128)(2,1)}, u32[]{:S(2)}, u32[]{:S(2)}) collective-permute-start(bf16[2,4,752,128]{3,2,1,0:T(8,128)(2,1)} %pad_maximum_fusion.refs_5_), channel_id=1, source_target_pairs={{0,4},{4,0},{8,12},{12,8},{16,20},{20,16},{24,28},{28,24},{1,5},{5... | collective-permute-start | bytes 4620296 | tf_op jit(solution)/shard_map/ppermute | solution.py:104
  77.9 3.6 %collective-permute-start.19 = (bf16[2,4,752,128]{3,2,1,0:T(8,128)(2,1)}, bf16[2,4,752,128]{3,2,1,0:T(8,128)(2,1)S(1)}, u32[]{:S(2)}, u32[]{:S(2)}) collective-permute-start(bf16[2,4,752,128]{3,2,1,0:T(8,128)(2,1)} %collective-permute-done.10.refs_6_), channel_id=1, source_target_pairs={{0,4},{4,0},{8,12},{12,8},{16,20},{20,16},{24,28},{28,24},{1,5},{5... | collective-permute-start | bytes 4620296 | tf_op jit(solution)/shard_map/ppermute | solution.py:104
  81.5 1.2 copy-start.12
  96.0 9.3 %collective-permute-start.20 = (bf16[2,2,4,752,128]{4,3,2,1,0:T(8,128)(2,1)}, bf16[2,2,4,752,128]{4,3,2,1,0:T(8,128)(2,1)}, u32[]{:S(2)}, u32[]{:S(2)}) collective-permute-start(bf16[2,2,4,752,128]{4,3,2,1,0:T(8,128)(2,1)} %get-tuple-element.118), channel_id=1, source_target_pairs={{0,4},{4,0},{8,12},{12,8},{16,20},{20,16},{24,28},{28,24},{1,5},{5... | collective-permute-start | bytes 9240584 | tf_op jit(solution)/shard_map/ppermute | solution.py:104
  105.3 3.9 %copy-start.23 = (bf16[256,384]{1,0:T(8,128)(2,1)S(1)}, bf16[256,384]{1,0:T(8,128)(2,1)}, u32[]{:S(2)}) copy-start(bf16[256,384]{1,0:T(8,128)(2,1)} %get-tuple-element.129) | copy-start | bytes 589828
  105.3 5.2 %copy-start.22 = (bf16[256,384]{1,0:T(8,128)(2,1)S(1)}, bf16[256,384]{1,0:T(8,128)(2,1)}, u32[]{:S(2)}) copy-start(bf16[256,384]{1,0:T(8,128)(2,1)} %get-tuple-element.130) | copy-start | bytes 589828
  105.3 6.5 %copy-start.21 = (bf16[256,384]{1,0:T(8,128)(2,1)S(1)}, bf16[256,384]{1,0:T(8,128)(2,1)}, u32[]{:S(2)}) copy-start(bf16[256,384]{1,0:T(8,128)(2,1)} %get-tuple-element.131) | copy-start | bytes 589828
  105.3 7.8 %copy-start.5 = (f32[256,576]{1,0:T(8,128)S(1)}, f32[256,576]{1,0:T(8,128)}, u32[]{:S(2)}) copy-start(f32[256,576]{1,0:T(8,128)} %get-tuple-element.132.refs_0_) | copy-start | bytes 1769476
  107.7 22.1 %collective-permute-start.21 = (bf16[2,4,752,128]{3,2,1,0:T(8,128)(2,1)S(1)}, bf16[2,4,752,128]{3,2,1,0:T(8,128)(2,1)S(1)}, u32[]{:S(2)}, u32[]{:S(2)}) collective-permute-start(bf16[2,4,752,128]{3,2,1,0:T(8,128)(2,1)S(1)} %fusion), channel_id=1, source_target_pairs={{0,8},{4,20},{8,0},{12,28},{16,24},{20,4},{24,16},{28,12},{1,9},{5... | collective-permute-start | bytes 4620296 | tf_op jit(solution)/shard_map/ppermute | solution.py:119
  109.2 9.1 %collective-permute-start.22 = (bf16[256,384]{1,0:T(8,128)(2,1)S(1)}, bf16[256,384]{1,0:T(8,128)(2,1)S(1)}, u32[]{:S(2)}, u32[]{:S(2)}) collective-permute-start(bf16[256,384]{1,0:T(8,128)(2,1)S(1)} %copy-done.23), channel_id=1, source_target_pairs={{1,0},{2,1},{3,2},{5,4},{6,5},{7,6},{9,8},{10,9},{11,10},{13,12},{... | collective-permute-start | bytes 589832 | tf_op jit(solution)/shard_map/ppermute | solution.py:929
  110.5 19.3 %collective-permute-start.23 = (bf16[256,384]{1,0:T(8,128)(2,1)S(1)}, bf16[256,384]{1,0:T(8,128)(2,1)S(1)}, u32[]{:S(2)}, u32[]{:S(2)}) collective-permute-start(bf16[256,384]{1,0:T(8,128)(2,1)S(1)} %copy-done.22), channel_id=1, source_target_pairs={{2,0},{3,1},{6,4},{7,5},{10,8},{11,9},{14,12},{15,13},{18,16},{19,... | collective-permute-start | bytes 589832 | tf_op jit(solution)/shard_map/ppermute | solution.py:929
  111.8 18.0 %collective-permute-start.24 = (bf16[256,384]{1,0:T(8,128)(2,1)S(1)}, bf16[256,384]{1,0:T(8,128)(2,1)S(1)}, u32[]{:S(2)}, u32[]{:S(2)}) collective-permute-start(bf16[256,384]{1,0:T(8,128)(2,1)S(1)} %copy-done.21), channel_id=1, source_target_pairs={{3,0},{7,4},{11,8},{15,12},{19,16},{23,20},{27,24},{31,28}} | collective-permute-start | bytes 589832 | tf_op jit(solution)/shard_map/ppermute | solution.py:929
  113.1 16.7 %copy-start.11 = (bf16[2,2,4,752,128]{4,3,2,1,0:T(8,128)(2,1)S(1)}, bf16[2,2,4,752,128]{4,3,2,1,0:T(8,128)(2,1)}, u32[]{:S(2)}) copy-start(bf16[2,2,4,752,128]{4,3,2,1,0:T(8,128)(2,1)} %get-tuple-element.117) | copy-start | bytes 9240580
  129.8 3.3 %copy-start.1 = (bf16[256,576]{0,1:T(8,128)(2,1)S(1)}, bf16[256,576]{0,1:T(8,128)(2,1)}, u32[]{:S(2)}) copy-start(bf16[256,576]{0,1:T(8,128)(2,1)} %param.14) | copy-start | bytes 884740
  129.8 3.3 %copy-start.4 = (f32[256,576]{1,0:T(8,128)S(1)}, f32[256,576]{1,0:T(8,128)}, u32[]{:S(2)}) copy-start(f32[256,576]{1,0:T(8,128)} %get-tuple-element.142.refs_7_) | copy-start | bytes 1769476
  129.8 3.2 %copy-start.6 = (bf16[256,384]{1,0:T(8,128)(2,1)S(1)}, bf16[256,384]{1,0:T(8,128)(2,1)}, u32[]{:S(2)}) copy-start(bf16[256,384]{1,0:T(8,128)(2,1)} %get-tuple-element.144.refs_14_) | copy-start | bytes 589828
  129.8 3.2 %copy-start.8 = (s32[4]{0:T(128)S(1)}, s32[4]{0:T(128)}, u32[]{:S(2)}) copy-start(s32[4]{0:T(128)} %pad_add_fusion.1.refs_0_) | copy-start | bytes 52
  129.8 3.2 %copy-start.9 = (f32[1,576]{1,0:T(1,128)S(1)}, f32[1,576]{1,0:T(1,128)}, u32[]{:S(2)}) copy-start(f32[1,576]{1,0:T(1,128)} %get-tuple-element.143.refs_13_) | copy-start | bytes 6916
  131.4 11.9 %collective-permute-start.25 = (bf16[4,752,128]{2,1,0:T(8,128)(2,1)S(1)}, bf16[4,752,128]{2,1,0:T(8,128)(2,1)S(1)}, u32[]{:S(2)}, u32[]{:S(2)}) collective-permute-start(bf16[4,752,128]{2,1,0:T(8,128)(2,1)S(1)} %fusion.1), channel_id=1, source_target_pairs={{0,16},{4,12},{8,24},{12,4},{16,0},{20,28},{24,8},{28,20},{1,17},{... | collective-permute-start | bytes 2310152 | tf_op jit(solution)/shard_map/ppermute | solution.py:119
  137.4 2.2 %collective-permute-start.26 = (bf16[4,4,160,128]{3,2,1,0:T(8,128)(2,1)S(1)}, bf16[4,4,160,128]{3,2,1,0:T(8,128)(2,1)S(1)}, u32[]{:S(2)}, u32[]{:S(2)}) collective-permute-start(bf16[4,4,160,128]{3,2,1,0:T(8,128)(2,1)S(1)} %get-tuple-element.150), channel_id=1, source_target_pairs={{0,4},{4,0},{8,12},{12,8},{16,20},{20,16},{24,28},{28,24},{1,5},{5... | collective-permute-start | bytes 1966088 | tf_op jit(solution)/shard_map/ppermute | solution.py:104
  143.5 8.9 %collective-permute-start.32 = (bf16[4,160,128]{2,1,0:T(8,128)(2,1)S(1)}, bf16[4,160,128]{2,1,0:T(8,128)(2,1)S(1)}, u32[]{:S(2)}, u32[]{:S(2)}) collective-permute-start(bf16[4,160,128]{2,1,0:T(8,128)(2,1)S(1)} %get-tuple-element.171), channel_id=1, source_target_pairs={{0,24},{4,28},{8,16},{12,20},{16,8},{20,12},{24,0},{28,4},{1,25},{... | collective-permute-start | bytes 491528 | tf_op jit(solution)/shard_map/ppermute | solution.py:104
  145.6 7.1 %collective-permute-start.31 = (bf16[4,160,128]{2,1,0:T(8,128)(2,1)S(1)}, bf16[4,160,128]{2,1,0:T(8,128)(2,1)S(1)}, u32[]{:S(2)}, u32[]{:S(2)}) collective-permute-start(bf16[4,160,128]{2,1,0:T(8,128)(2,1)S(1)} %get-tuple-element.172), channel_id=1, source_target_pairs={{0,16},{4,20},{8,24},{12,28},{16,0},{20,4},{24,8},{28,12},{1,17},{... | collective-permute-start | bytes 491528 | tf_op jit(solution)/shard_map/ppermute | solution.py:104
  146.5 6.2 %collective-permute-start.30 = (bf16[4,160,128]{2,1,0:T(8,128)(2,1)S(1)}, bf16[4,160,128]{2,1,0:T(8,128)(2,1)S(1)}, u32[]{:S(2)}, u32[]{:S(2)}) collective-permute-start(bf16[4,160,128]{2,1,0:T(8,128)(2,1)S(1)} %get-tuple-element.173), channel_id=1, source_target_pairs={{0,8},{4,12},{8,0},{12,4},{16,24},{20,28},{24,16},{28,20},{1,9},{5... | collective-permute-start | bytes 491528 | tf_op jit(solution)/shard_map/ppermute | solution.py:104
  148.5 9.7 %collective-permute-start.27 = (bf16[752,128]{1,0:T(8,128)(2,1)S(1)}, bf16[752,128]{1,0:T(8,128)(2,1)S(1)}, u32[]{:S(2)}, u32[]{:S(2)}) collective-permute-start(bf16[752,128]{1,0:T(8,128)(2,1)S(1)} %get-tuple-element.167), channel_id=1, source_target_pairs={{0,1},{1,2},{2,3},{3,0},{4,5},{5,6},{6,7},{7,4},{8,9},{9,10},{10,1... | collective-permute-start | bytes 577544 | tf_op jit(solution)/shard_map/ppermute | solution.py:109
  148.5 13.2 %collective-permute-start.29 = (bf16[752,128]{1,0:T(8,128)(2,1)S(1)}, bf16[752,128]{1,0:T(8,128)(2,1)S(1)}, u32[]{:S(2)}, u32[]{:S(2)}) collective-permute-start(bf16[752,128]{1,0:T(8,128)(2,1)S(1)} %get-tuple-element.168), channel_id=1, source_target_pairs={{0,3},{1,0},{2,1},{3,2},{4,7},{5,4},{6,5},{7,6},{8,11},{9,8},{10,9... | collective-permute-start | bytes 577544 | tf_op jit(solution)/shard_map/ppermute | solution.py:109
  152.4 15.6 %collective-permute-start.28 = (bf16[752,128]{1,0:T(8,128)(2,1)S(1)}, bf16[752,128]{1,0:T(8,128)(2,1)S(1)}, u32[]{:S(2)}, u32[]{:S(2)}) collective-permute-start(bf16[752,128]{1,0:T(8,128)(2,1)S(1)} %get-tuple-element.169), channel_id=1, source_target_pairs={{0,2},{1,3},{2,0},{3,1},{4,6},{5,7},{6,4},{7,5},{8,10},{9,11},{10,... | collective-permute-start | bytes 577544 | tf_op jit(solution)/shard_map/ppermute | solution.py:109
  152.8 16.2 %collective-permute-start.33 = (bf16[160,128]{1,0:T(8,128)(2,1)S(1)}, bf16[160,128]{1,0:T(8,128)(2,1)S(1)}, u32[]{:S(2)}, u32[]{:S(2)}) collective-permute-start(bf16[160,128]{1,0:T(8,128)(2,1)S(1)} %get-tuple-element.176), channel_id=1, source_target_pairs={{0,1},{1,2},{2,3},{3,0},{4,5},{5,6},{6,7},{7,4},{8,9},{9,10},{10,1... | collective-permute-start | bytes 122888 | tf_op jit(solution)/shard_map/ppermute | solution.py:109
  153.1 16.0 %collective-permute-start.35 = (bf16[160,128]{1,0:T(8,128)(2,1)S(1)}, bf16[160,128]{1,0:T(8,128)(2,1)S(1)}, u32[]{:S(2)}, u32[]{:S(2)}) collective-permute-start(bf16[160,128]{1,0:T(8,128)(2,1)S(1)} %get-tuple-element.177), channel_id=1, source_target_pairs={{0,3},{1,0},{2,1},{3,2},{4,7},{5,4},{6,5},{7,6},{8,11},{9,8},{10,9... | collective-permute-start | bytes 122888 | tf_op jit(solution)/shard_map/ppermute | solution.py:109
  158.2 10.9 %collective-permute-start.34 = (bf16[160,128]{1,0:T(8,128)(2,1)S(1)}, bf16[160,128]{1,0:T(8,128)(2,1)S(1)}, u32[]{:S(2)}, u32[]{:S(2)}) collective-permute-start(bf16[160,128]{1,0:T(8,128)(2,1)S(1)} %get-tuple-element.178), channel_id=1, source_target_pairs={{0,2},{1,3},{2,0},{3,1},{4,6},{5,7},{6,4},{7,5},{8,10},{9,11},{10,... | collective-permute-start | bytes 122888 | tf_op jit(solution)/shard_map/ppermute | solution.py:109
  169.1 8.2 %collective-permute-start.37 = (bf16[912,128]{1,0:T(8,128)(2,1)S(1)}, bf16[912,128]{1,0:T(8,128)(2,1)S(1)}, u32[]{:S(2)}, u32[]{:S(2)}) collective-permute-start(bf16[912,128]{1,0:T(8,128)(2,1)S(1)} %get-tuple-element.180), channel_id=1, source_target_pairs={{0,8},{4,12},{8,0},{12,4},{16,24},{20,28},{24,16},{28,20},{1,9},{5... | collective-permute-start | bytes 700424 | tf_op jit(solution)/shard_map/ppermute | solution.py:104
  170.6 10.5 %collective-permute-start.36 = (bf16[912,128]{1,0:T(8,128)(2,1)S(1)}, bf16[912,128]{1,0:T(8,128)(2,1)S(1)}, u32[]{:S(2)}, u32[]{:S(2)}) collective-permute-start(bf16[912,128]{1,0:T(8,128)(2,1)S(1)} %get-tuple-element.180), channel_id=1, source_target_pairs={{0,16},{4,20},{8,24},{12,28},{16,0},{20,4},{24,8},{28,12},{1,17},{... | collective-permute-start | bytes 700424 | tf_op jit(solution)/shard_map/ppermute | solution.py:104
  172.3 8.8 %collective-permute-start.38 = (bf16[912,128]{1,0:T(8,128)(2,1)S(1)}, bf16[912,128]{1,0:T(8,128)(2,1)S(1)}, u32[]{:S(2)}, u32[]{:S(2)}) collective-permute-start(bf16[912,128]{1,0:T(8,128)(2,1)S(1)} %get-tuple-element.180), channel_id=1, source_target_pairs={{0,24},{4,28},{8,16},{12,20},{16,8},{20,12},{24,0},{28,4},{1,25},{... | collective-permute-start | bytes 700424 | tf_op jit(solution)/shard_map/ppermute | solution.py:104
  181.3 2.6 %collective-permute-start.39 = (bf16[4,912,128]{2,1,0:T(8,128)(2,1)S(1)}, bf16[4,912,128]{2,1,0:T(8,128)(2,1)S(1)}, u32[]{:S(2)}, u32[]{:S(2)}) collective-permute-start(bf16[4,912,128]{2,1,0:T(8,128)(2,1)S(1)} %pad_maximum_fusion.1.refs_1_), channel_id=1, source_target_pairs={{0,4},{4,0},{8,12},{12,8},{16,20},{20,16},{24,28},{28,24},{1,5},{5... | collective-permute-start | bytes 2801672 | tf_op jit(solution)/shard_map/ppermute | solution.py:104
  (1 other events, 0.8 us)

commit v3 on v2

--- a/solution.py
+++ b/solution.py
@@ -471,7 +471,7 @@
         (shape((toks, q_width), f32),) + tuple(shape((toks, 2 * kv_width), bf16) for _ in held),
         (vmem(),) * (1 + len(held)),
         [pltpu.VMEM(probs.shape, bf16), pltpu.SemaphoreType.DMA((probs.shape[0],))],
-        BIG,
+        36,
     )
 
 
@@ -570,8 +570,8 @@
         blocks = w_chunk.blocks(share)
         down_at = w_chunk.rows_at["down", share]
         down_to = g_chunk.rows_at["down", share]
-        for pair in range(0, len(blocks), 2):
-            some = blocks[pair : pair + 2]
+        for pair in range(0, len(blocks), 4):
+            some = blocks[pair : pair + 4]
             gate_w = jnp.concatenate([column("gate", f) for f in some], 1)
             up_w = jnp.concatenate([column("up", f) for f in some], 1)
             down_w = jnp.concatenate(

time: 187 us -> 185 us (0.989)
  other arithmetic: 13.6 us -> 8.38 us
  waiting for transfers between devices: 60.7 us -> 65.1 us
  starting transfers between devices: 57.9 us -> 54.1 us
  local copies, waits for them, and re-layouts: 3.73 us -> 7.03 us
    convert_element_type x4, other arithmetic: 5.58 us -> 1.18 us  [add_low(): return total.astype(values[0].dtype)]
    ppermute x15, starting transfers between devices: 25.9 us -> 22.3 us  [shift(): lax.ppermute(value, 'grp', [(i, (i + step) % count) for i in range(count)])]
    unnamed x53 -> x59, local copies, waits for them, and re-layouts: 1.36 us -> 4.64 us
    ppermute x15, waiting for transfers between devices: 9.2 us -> 12.3 us  [shift(): lax.ppermute(value, 'grp', [(i, (i + step) % count) for i in range(count)])]
  transfers between devices with their start and end apart: 40 -> 40, of which waited for: 19 -> 21; matrix products, arithmetic and copies ran while one was open for 5% -> 4% of each run, Pallas kernels for 16% -> 16%
where the time goes in v3:
time: 185 us
  waiting for transfers between devices  65.1 us (35%)
  starting transfers between devices  54.1 us (29%)
  Pallas kernels  48.8 us (26%)
  other arithmetic  8.38 us (5%)
  local copies, waits for them, and re-layouts  7.03 us (4%)
    pallas_call x8, Pallas kernels, staged_call(): pl.pallas_call(whole, out_shape=out_shape, in_specs=[specs[kind]() for ki...  48.8 us
    ppermute x15, waiting for transfers between devices, hop(): return lax.ppermute(value, 'rep', [(i, i ^ bit) for i in range(count)])  26.1 us
    ppermute x15, starting transfers between devices, shift(): lax.ppermute(value, 'grp', [(i, (i + step) % count) for i in range(count)])  22.3 us
    ppermute x15, starting transfers between devices, hop(): return lax.ppermute(value, 'rep', [(i, i ^ bit) for i in range(count)])  13.9 us
    ppermute x3, waiting for transfers between devices, body(): kv_back.append(lax.ppermute(kv_parts[step], 'grp', back))  12.4 us
    ppermute x15, waiting for transfers between devices, shift(): lax.ppermute(value, 'grp', [(i, (i + step) % count) for i in range(count)])  12.3 us
    ppermute x4, waiting for transfers between devices, hop_split(): lax.ppermute(value, 'rep', [(i, i ^ (odd if i % 2 else even)) for i in ra...  9.95 us
    ppermute x3, starting transfers between devices, body(): held.append(lax.ppermute(key_value, 'grp', ahead))  7.83 us
  transfers between devices with their start and end apart: 40, of which 21 were waited for; matrix products, arithmetic and copies ran while one was open for 4% of the time, Pallas kernels for 16%

profile of v3, /device:TPU:0, one launch (start us, length us, event | category | flops | bytes accessed | tf_op | source)
XLA Modules:
  0.0 184.7 jit_solution(5809855607436587578)
XLA Ops:
  0.7 0.6 pad_add_fusion.1.refs_0_
  1.3 3.2 %pack.1 = (bf16[144,128]{1,0:T(8,128)(2,1)}, bf16[752,128]{1,0:T(8,128)(2,1)}) custom-call(s32[4]{0:T(128)} %pad_add_fusion.1.refs_0_, bf16[144,576]{1,0:T(8,128)(2,1)} %refs_1_.1, bf16[144,192]{1,0:T(8,128)(2,1)} %refs_2_.1, bf16[144,192]{1,0:T(8,128)(2,1)} %refs_3_.1, bf16[144,1536]{1,0:T(8,128)(2,1)} %refs_4_.1, bf16[144,1536]{1,0:T(8,128)(2,1)} %refs_5_.1, ...), custom_call_target="tpu_custom_call" | custom-call | flops 1 | bytes 1024 | tf_op jit(solution)/shard_map/pack/pallas_call | solution.py:86
  4.6 5.1 %collective-permute-start.13 = (bf16[16,128]{1,0:T(8,128)(2,1)S(1)}, bf16[16,128]{1,0:T(8,128)(2,1)S(1)}, u32[]{:S(2)}, u32[]{:S(2)}) collective-permute-start(bf16[16,128]{1,0:T(8,128)(2,1)S(1)} %get-tuple-element.190), channel_id=1, source_target_pairs={{0,3},{1,0},{2,1},{3,2},{4,7},{5,4},{6,5},{7,6},{8,11},{9,8},{10,9... | collective-permute-start | bytes 12296 | tf_op jit(solution)/shard_map/ppermute | solution.py:109
  9.7 1.0 collective-permute-start.11
  10.7 2.8 %collective-permute-start.2 = (bf16[144,128]{1,0:T(8,128)(2,1)}, bf16[144,128]{1,0:T(8,128)(2,1)S(1)}, u32[]{:S(2)}, u32[]{:S(2)}) collective-permute-start(bf16[144,128]{1,0:T(8,128)(2,1)} %get-tuple-element.89), channel_id=1, source_target_pairs={{0,3},{1,0},{2,1},{3,2},{4,7},{5,4},{6,5},{7,6},{8,11},{9,8},{10,9... | collective-permute-start | bytes 110600 | tf_op jit(solution)/shard_map/ppermute | solution.py:109
  13.5 1.1 collective-permute-start.1
  14.9 3.8 %collective-permute-start.8 = (bf16[752,128]{1,0:T(8,128)(2,1)}, bf16[752,128]{1,0:T(8,128)(2,1)S(1)}, u32[]{:S(2)}, u32[]{:S(2)}) collective-permute-start(bf16[752,128]{1,0:T(8,128)(2,1)} %get-tuple-element.91), channel_id=1, source_target_pairs={{0,3},{1,0},{2,1},{3,2},{4,7},{5,4},{6,5},{7,6},{8,11},{9,8},{10,9... | collective-permute-start | bytes 577544 | tf_op jit(solution)/shard_map/ppermute | solution.py:109
  18.8 0.6 gather_fusion
  20.2 0.7 collective-permute-start.6
  20.9 0.5 collective-permute-done
  21.4 0.8 fusion.33
  22.2 1.6 collective-permute-start.4
  23.8 1.5 collective-permute-start.3
  25.3 2.7 %collective-permute-done.4 = bf16[4,144,128]{2,1,0:T(8,128)(2,1)S(1)} collective-permute-done((bf16[4,144,128]{2,1,0:T(8,128)(2,1)S(1)}, bf16[4,144,128]{2,1,0:T(8,128)(2,1)S(1)}, u32[]{:S(2)}, u32[]{:S(2)}) %collective-permute-start.4) | collective-permute-done | bytes 147488 | tf_op jit(solution)/shard_map/ppermute | solution.py:104
  28.0 3.5 %collective-permute-start.5 = (bf16[4,144,128]{2,1,0:T(8,128)(2,1)S(1)}, bf16[4,144,128]{2,1,0:T(8,128)(2,1)S(1)}, u32[]{:S(2)}, u32[]{:S(2)}) collective-permute-start(bf16[4,144,128]{2,1,0:T(8,128)(2,1)S(1)} %get-tuple-element.182), channel_id=1, source_target_pairs={{0,24},{4,28},{8,16},{12,20},{16,8},{20,12},{24,0},{28,4},{1,25},{... | collective-permute-start | bytes 442376 | tf_op jit(solution)/shard_map/ppermute | solution.py:104
  31.4 3.1 %collective-permute-done.5 = bf16[4,144,128]{2,1,0:T(8,128)(2,1)S(1)} collective-permute-done((bf16[4,144,128]{2,1,0:T(8,128)(2,1)S(1)}, bf16[4,144,128]{2,1,0:T(8,128)(2,1)S(1)}, u32[]{:S(2)}, u32[]{:S(2)}) %collective-permute-start.5) | collective-permute-done | bytes 147488 | tf_op jit(solution)/shard_map/ppermute | solution.py:104
  34.6 1.0 collective-permute-done.7
  35.6 1.3 fusion.34
  36.9 1.5 collective-permute-start.9
  38.4 0.6 broadcast_select_fusion.refs_2_
  39.2 0.7 reshape.259.refs_4_
  40.0 2.0 %collective-permute-done.14.refs_2_ = bf16[4,4,144,128]{3,2,1,0:T(8,128)(2,1)S(1)} collective-permute-done((bf16[4,4,144,128]{3,2,1,0:T(8,128)(2,1)S(1)}, bf16[4,4,144,128]{3,2,1,0:T(8,128)(2,1)S(1)}, u32[]{:S(2)}, u32[]{:S(2)}) %collective-permute-start.14) | collective-permute-done | bytes 589856 | tf_op jit(solution)/shard_map/ppermute | solution.py:104
  42.0 5.1 %proj.1 = (bf16[256,576]{1,0:T(8,128)(2,1)S(1)}, f32[256,768]{1,0:T(8,128)S(1)}, bf16[256,576]{1,0:T(8,128)(2,1)S(1)}, bf16[256,384]{1,0:T(8,128)(2,1)S(1)}, bf16[576,1024]{1,0:T(8,128)(2,1)S(1)}) custom-call(s32[4]{0:T(128)S(1)} %copy-done.16, bf16[4,4,144,128]{3,2,1,0:T(8,128)(2,1)S(1)} %pad_maximum_fusion.3.refs_1_, ...), custom_call_target="tpu_custom_call" | custom-call | flops 1 | bytes 1024 | tf_op jit(solution)/shard_map/proj/pallas_call | solution.py:86
  47.2 3.3 %collective-permute-start.17 = (bf16[256,384]{1,0:T(8,128)(2,1)S(1)}, bf16[256,384]{1,0:T(8,128)(2,1)S(1)}, u32[]{:S(2)}, u32[]{:S(2)}) collective-permute-start(bf16[256,384]{1,0:T(8,128)(2,1)S(1)} %get-tuple-element.106.refs_3_), channel_id=1, source_target_pairs={{0,3},{4,7},{8,11},{12,15},{16,19},{20,23},{24,27},{28,31}} | collective-permute-start | bytes 589832 | tf_op jit(solution)/shard_map/ppermute | solution.py:912
  50.5 3.1 %collective-permute-start.16 = (bf16[256,384]{1,0:T(8,128)(2,1)S(1)}, bf16[256,384]{1,0:T(8,128)(2,1)S(1)}, u32[]{:S(2)}, u32[]{:S(2)}) collective-permute-start(bf16[256,384]{1,0:T(8,128)(2,1)S(1)} %get-tuple-element.106.refs_3_), channel_id=1, source_target_pairs={{0,2},{1,3},{4,6},{5,7},{8,10},{9,11},{12,14},{13,15},{16,18},{17,... | collective-permute-start | bytes 589832 | tf_op jit(solution)/shard_map/ppermute | solution.py:912
  53.5 1.5 collective-permute-start.15
  55.1 2.5 %pad_maximum_fusion.refs_5_ = bf16[2,4,752,128]{3,2,1,0:T(8,128)(2,1)} fusion(bf16[1,4,752,128]{3,2,1,0:T(8,128)(2,1)} %bitcast.18, bf16[1,4,752,128]{3,2,1,0:T(8,128)(2,1)S(1)} %copy-done.19), kind=kLoop, calls=%fused_computation.3 | loop fusion | flops 770048 | bytes 3080192 | tf_op jit(solution)/shard_map/stack | solution.py:913
  57.6 1.5 collective-permute-start.10
  59.1 0.9 collective-permute-done.16.refs_5_
  60.0 3.4 %collective-permute-done.15.refs_4_ = bf16[256,384]{1,0:T(8,128)(2,1)S(1)} collective-permute-done((bf16[256,384]{1,0:T(8,128)(2,1)S(1)}, bf16[256,384]{1,0:T(8,128)(2,1)S(1)}, u32[]{:S(2)}, u32[]{:S(2)}) %collective-permute-start.15) | collective-permute-done | bytes 196640 | tf_op jit(solution)/shard_map/ppermute | solution.py:912
  63.4 0.8 copy.28.refs_1_
  64.2 7.4 %attend.1 = (bf16[256,576]{1,0:T(8,128)(2,1)}, f32[256,576]{1,0:T(8,128)}, bf16[9,256,1024]{2,1,0:T(8,128)(2,1)}) custom-call(bf16[256,576]{1,0:T(8,128)(2,1)} %copy-done.3, f32[256,1]{1,0:T(8,128)} %copy.28.refs_1_, f32[1,1024]{1,0:T(1,128)} %broadcast_select_fusion.refs_2_, bf16[256,384]{1,0:T(8,128)(2,1)} %copy-done.5, bf16[256,384]{1,0:T(8,128)(2,1)} %copy-done.11, ...), custom_call_target="tpu_custom_call" | custom-call | flops 1 | bytes 1024 | tf_op jit(solution)/shard_map/attend/pallas_call | solution.py:86
  71.6 6.3 %collective-permute-done.10.refs_6_ = bf16[2,4,752,128]{3,2,1,0:T(8,128)(2,1)} collective-permute-done((bf16[2,4,752,128]{3,2,1,0:T(8,128)(2,1)}, bf16[2,4,752,128]{3,2,1,0:T(8,128)(2,1)}, u32[]{:S(2)}, u32[]{:S(2)}) %collective-permute-start.10) | collective-permute-done | bytes 1540128 | tf_op jit(solution)/shard_map/ppermute | solution.py:119
  77.9 3.6 %collective-permute-done.19.refs_8_ = bf16[2,4,752,128]{3,2,1,0:T(8,128)(2,1)S(1)} collective-permute-done((bf16[2,4,752,128]{3,2,1,0:T(8,128)(2,1)}, bf16[2,4,752,128]{3,2,1,0:T(8,128)(2,1)S(1)}, u32[]{:S(2)}, u32[]{:S(2)}) %collective-permute-start.19) | collective-permute-done | bytes 1540128 | tf_op jit(solution)/shard_map/ppermute | solution.py:104
  81.5 1.1 copy-done.21
  82.7 13.1 %mlp.1 = (bf16[576,256]{1,0:T(8,128)(2,1)}, f32[256,576]{1,0:T(8,128)}, bf16[256,576]{1,0:T(8,128)(2,1)}, f32[1,576]{1,0:T(1,128)}, bf16[2,2,4,752,128]{4,3,2,1,...) custom-call(s32[4]{0:T(128)} %pad_add_fusion.1.refs_0_, bf16[256,576]{1,0:T(8,128)(2,1)} %get-tuple-element.112.refs_1_, ...), custom_call_target="tpu_custom_call" | custom-call | flops 1 | bytes 1024 | tf_op jit(solution)/shard_map/mlp/pallas_call | solution.py:86
  96.0 2.3 %copy-done = bf16[9,256,1024]{2,1,0:T(8,128)(2,1)S(1)} copy-done((bf16[9,256,1024]{2,1,0:T(8,128)(2,1)S(1)}, bf16[9,256,1024]{2,1,0:T(8,128)(2,1)}, u32[]{:S(2)}) %copy-start) | copy-done | bytes 4718616
  98.3 1.0 copy-done.15
  99.3 8.6 %attend_back.1 = (f32[256,576]{1,0:T(8,128)S(1)}, bf16[256,384]{1,0:T(8,128)(2,1)S(1)}, bf16[256,384]{1,0:T(8,128)(2,1)S(1)}, bf16[256,384]{1,0:T(8,128)(2,1)S(1)}, bf16[256,384]{1,0:T(8,128)(2,1)S(1)}) custom-call(bf16[256,576]{1,0:T(8,128)(2,1)S(1)} %copy-done.4, bf16[256,576]{1,0:T(8,128)(2,1)S(1)} %copy-done.15, f32[256,576]{1,0:T(8,128)S(1)} %copy-done.14, ...), custom_call_target="tpu_custom_call" | custom-call | flops 1 | bytes 1024 | tf_op jit(solution)/shard_map/attend_back/pallas_call | solution.py:86
  108.3 1.6 collective-permute-start.21
  109.8 1.3 collective-permute-start.22
  111.1 1.3 collective-permute-start.23
  112.4 1.3 collective-permute-start.24
  113.7 4.2 %query_back.1 = (bf16[576,576]{1,0:T(8,128)(2,1)S(1)}, f32[256,576]{1,0:T(8,128)S(1)}, f32[1,64]{1,0:T(1,128)S(1)}) custom-call(f32[256,576]{1,0:T(8,128)S(1)} %get-tuple-element.132.refs_0_, f32[256,768]{1,0:T(8,128)S(1)} %get-tuple-element.133.refs_1_.refs_4_, bf16[256,576]{1,0:T(8,128)(2,1)S(1)} %get-tuple-element.134.refs_2_.refs_5_, ...), custom_call_target="tpu_custom_call" | custom-call | flops 1 | bytes 1024 | tf_op jit(solution)/shard_map/query_back/pallas_call | solution.py:86
  118.0 0.9 collective-permute-done.22.refs_15_
  118.9 11.5 %collective-permute-done.23.refs_16_ = bf16[256,384]{1,0:T(8,128)(2,1)S(1)} collective-permute-done((bf16[256,384]{1,0:T(8,128)(2,1)S(1)}, bf16[256,384]{1,0:T(8,128)(2,1)S(1)}, u32[]{:S(2)}, u32[]{:S(2)}) %collective-permute-start.23) | collective-permute-done | bytes 196640 | tf_op jit(solution)/shard_map/ppermute | solution.py:929
  130.7 1.5 collective-permute-start.25
  132.3 4.5 %last.1 = (f32[576,256]{1,0:T(8,128)}, bf16[4,4,160,128]{3,2,1,0:T(8,128)(2,1)S(1)}, bf16[4,4,160,128]{3,2,1,0:T(8,128)(2,1)S(1)}) custom-call(s32[4]{0:T(128)S(1)} %copy-done.17, bf16[576,576]{1,0:T(8,128)(2,1)S(1)} %get-tuple-element.139.refs_1_, f32[256,576]{1,0:T(8,128)S(1)} %get-tuple-element.140.refs_2_, f32[1,64]{1,0:T(1,128)S(1)} %get-tuple-element.141.refs_3_, ...), custom_call_target="tpu_custom_call" | custom-call | flops 1 | bytes 1024 | tf_op jit(solution)/shard_map/last/pallas_call | solution.py:86
  136.9 2.1 %collective-permute-done.26 = bf16[4,4,160,128]{3,2,1,0:T(8,128)(2,1)S(1)} collective-permute-done((bf16[4,4,160,128]{3,2,1,0:T(8,128)(2,1)S(1)}, bf16[4,4,160,128]{3,2,1,0:T(8,128)(2,1)S(1)}, u32[]{:S(2)}, u32[]{:S(2)}) %collective-permute-start.26) | collective-permute-done | bytes 655392 | tf_op jit(solution)/shard_map/ppermute | solution.py:104
  139.0 3.6 %collective-permute-done.25 = bf16[4,752,128]{2,1,0:T(8,128)(2,1)S(1)} collective-permute-done((bf16[4,752,128]{2,1,0:T(8,128)(2,1)S(1)}, bf16[4,752,128]{2,1,0:T(8,128)(2,1)S(1)}, u32[]{:S(2)}, u32[]{:S(2)}) %collective-permute-start.25) | collective-permute-done | bytes 770080 | tf_op jit(solution)/shard_map/ppermute | solution.py:119
  142.8 2.1 %collective-permute-start.32 = (bf16[4,160,128]{2,1,0:T(8,128)(2,1)S(1)}, bf16[4,160,128]{2,1,0:T(8,128)(2,1)S(1)}, u32[]{:S(2)}, u32[]{:S(2)}) collective-permute-start(bf16[4,160,128]{2,1,0:T(8,128)(2,1)S(1)} %get-tuple-element.171), channel_id=1, source_target_pairs={{0,24},{4,28},{8,16},{12,20},{16,8},{20,12},{24,0},{28,4},{1,25},{... | collective-permute-start | bytes 491528 | tf_op jit(solution)/shard_map/ppermute | solution.py:104
  144.9 0.9 collective-permute-start.31
  146.7 3.8 %collective-permute-start.29 = (bf16[752,128]{1,0:T(8,128)(2,1)S(1)}, bf16[752,128]{1,0:T(8,128)(2,1)S(1)}, u32[]{:S(2)}, u32[]{:S(2)}) collective-permute-start(bf16[752,128]{1,0:T(8,128)(2,1)S(1)} %get-tuple-element.168), channel_id=1, source_target_pairs={{0,3},{1,0},{2,1},{3,2},{4,7},{5,4},{6,5},{7,6},{8,11},{9,8},{10,9... | collective-permute-start | bytes 577544 | tf_op jit(solution)/shard_map/ppermute | solution.py:109
  150.6 1.5 collective-permute-done.31
  152.2 3.8 %collective-permute-start.35 = (bf16[160,128]{1,0:T(8,128)(2,1)S(1)}, bf16[160,128]{1,0:T(8,128)(2,1)S(1)}, u32[]{:S(2)}, u32[]{:S(2)}) collective-permute-start(bf16[160,128]{1,0:T(8,128)(2,1)S(1)} %get-tuple-element.177), channel_id=1, source_target_pairs={{0,3},{1,0},{2,1},{3,2},{4,7},{5,4},{6,5},{7,6},{8,11},{9,8},{10,9... | collective-permute-start | bytes 122888 | tf_op jit(solution)/shard_map/ppermute | solution.py:109
  156.4 0.7 collective-permute-done.29
  157.1 9.0 %collective-permute-done.28 = bf16[752,128]{1,0:T(8,128)(2,1)S(1)} collective-permute-done((bf16[752,128]{1,0:T(8,128)(2,1)S(1)}, bf16[752,128]{1,0:T(8,128)(2,1)S(1)}, u32[]{:S(2)}, u32[]{:S(2)}) %collective-permute-start.28) | collective-permute-done | bytes 192544 | tf_op jit(solution)/shard_map/ppermute | solution.py:109
  166.3 0.7 collective-permute-done.34
  167.1 1.5 collective-permute-start.37
  168.5 1.7 collective-permute-start.36
  170.6 5.0 %collective-permute-done.37 = bf16[912,128]{1,0:T(8,128)(2,1)S(1)} collective-permute-done((bf16[912,128]{1,0:T(8,128)(2,1)S(1)}, bf16[912,128]{1,0:T(8,128)(2,1)S(1)}, u32[]{:S(2)}, u32[]{:S(2)}) %collective-permute-start.37) | collective-permute-done | bytes 233504 | tf_op jit(solution)/shard_map/ppermute | solution.py:104
  175.6 3.7 %collective-permute-done.36 = bf16[912,128]{1,0:T(8,128)(2,1)S(1)} collective-permute-done((bf16[912,128]{1,0:T(8,128)(2,1)S(1)}, bf16[912,128]{1,0:T(8,128)(2,1)S(1)}, u32[]{:S(2)}, u32[]{:S(2)}) %collective-permute-start.36) | collective-permute-done | bytes 233504 | tf_op jit(solution)/shard_map/ppermute | solution.py:104
  179.5 2.5 %collective-permute-done.39.refs_2_ = bf16[4,912,128]{2,1,0:T(8,128)(2,1)S(1)} collective-permute-done((bf16[4,912,128]{2,1,0:T(8,128)(2,1)S(1)}, bf16[4,912,128]{2,1,0:T(8,128)(2,1)S(1)}, u32[]{:S(2)}, u32[]{:S(2)}) %collective-permute-start.39) | collective-permute-done | bytes 933920 | tf_op jit(solution)/shard_map/ppermute | solution.py:104
  182.0 2.7 %unpack.1 = (f32[144,1536]{1,0:T(8,128)}, f32[144,1536]{1,0:T(8,128)}, f32[576,384]{1,0:T(8,128)}, f32[144,576]{1,0:T(8,128)}, f32[144,576]{1,0:T(8,128)}, /*ind...) custom-call(s32[4]{0:T(128)S(1)} %copy-done.17, ...), custom_call_target="tpu_custom_call" | custom-call | flops 1 | bytes 1024 | tf_op jit(solution)/shard_map/unpack/pallas_call | solution.py:86
  (122 shorter events, 5.0 us)
Async XLA Ops:
  0.6 3.8 %copy-start.27 = (s32[256]{0:T(256)S(1)}, s32[256]{0:T(256)}, u32[]{:S(2)}) copy-start(s32[256]{0:T(256)} %param.15) | copy-start | bytes 3076
  0.7 3.9 %copy-start.25 = (bf16[144]{0:T(256)(128)(2,1)S(1)}, bf16[144]{0:T(256)(128)(2,1)}, u32[]{:S(2)}) copy-start(bf16[144]{0:T(256)(128)(2,1)} %param.24) | copy-start | bytes 868
  0.7 3.9 %copy-start.23 = (bf16[16]{0:T(256)(128)(2,1)S(1)}, bf16[16]{0:T(256)(128)(2,1)}, u32[]{:S(2)}) copy-start(bf16[16]{0:T(256)(128)(2,1)} %param.19) | copy-start | bytes 100
  0.7 3.9 %copy-start.24 = (bf16[16]{0:T(256)(128)(2,1)S(1)}, bf16[16]{0:T(256)(128)(2,1)}, u32[]{:S(2)}) copy-start(bf16[16]{0:T(256)(128)(2,1)} %param.18) | copy-start | bytes 100
  0.7 3.9 %copy-start.26 = (bf16[144]{0:T(256)(128)(2,1)S(1)}, bf16[144]{0:T(256)(128)(2,1)}, u32[]{:S(2)}) copy-start(bf16[144]{0:T(256)(128)(2,1)} %param.17) | copy-start | bytes 868
  4.5 31.1 %copy-start.22 = (bf16[752,128]{1,0:T(8,128)(2,1)S(1)}, bf16[752,128]{1,0:T(8,128)(2,1)}, u32[]{:S(2)}) copy-start(bf16[752,128]{1,0:T(8,128)(2,1)} %get-tuple-element.91) | copy-start | bytes 577540
  4.6 10.3 %collective-permute-start.13 = (bf16[16,128]{1,0:T(8,128)(2,1)S(1)}, bf16[16,128]{1,0:T(8,128)(2,1)S(1)}, u32[]{:S(2)}, u32[]{:S(2)}) collective-permute-start(bf16[16,128]{1,0:T(8,128)(2,1)S(1)} %get-tuple-element.190), channel_id=1, source_target_pairs={{0,3},{1,0},{2,1},{3,2},{4,7},{5,4},{6,5},{7,6},{8,11},{9,8},{10,9... | collective-permute-start | bytes 12296 | tf_op jit(solution)/shard_map/ppermute | solution.py:109
  9.7 5.2 %collective-permute-start.12 = (bf16[16,128]{1,0:T(8,128)(2,1)S(1)}, bf16[16,128]{1,0:T(8,128)(2,1)S(1)}, u32[]{:S(2)}, u32[]{:S(2)}) collective-permute-start(bf16[16,128]{1,0:T(8,128)(2,1)S(1)} %get-tuple-element.190), channel_id=1, source_target_pairs={{0,2},{1,3},{2,0},{3,1},{4,6},{5,7},{6,4},{7,5},{8,10},{9,11},{10,... | collective-permute-start | bytes 12296 | tf_op jit(solution)/shard_map/ppermute | solution.py:109
  9.7 9.0 %collective-permute-start.11 = (bf16[16,128]{1,0:T(8,128)(2,1)S(1)}, bf16[16,128]{1,0:T(8,128)(2,1)S(1)}, u32[]{:S(2)}, u32[]{:S(2)}) collective-permute-start(bf16[16,128]{1,0:T(8,128)(2,1)S(1)} %get-tuple-element.190), channel_id=1, source_target_pairs={{0,1},{1,2},{2,3},{3,0},{4,5},{5,6},{6,7},{7,4},{8,9},{9,10},{10,1... | collective-permute-start | bytes 12296 | tf_op jit(solution)/shard_map/ppermute | solution.py:109
  10.7 9.5 %collective-permute-start.2 = (bf16[144,128]{1,0:T(8,128)(2,1)}, bf16[144,128]{1,0:T(8,128)(2,1)S(1)}, u32[]{:S(2)}, u32[]{:S(2)}) collective-permute-start(bf16[144,128]{1,0:T(8,128)(2,1)} %get-tuple-element.89), channel_id=1, source_target_pairs={{0,3},{1,0},{2,1},{3,2},{4,7},{5,4},{6,5},{7,6},{8,11},{9,8},{10,9... | collective-permute-start | bytes 110600 | tf_op jit(solution)/shard_map/ppermute | solution.py:109
  13.5 7.4 %collective-permute-start.1 = (bf16[144,128]{1,0:T(8,128)(2,1)}, bf16[144,128]{1,0:T(8,128)(2,1)S(1)}, u32[]{:S(2)}, u32[]{:S(2)}) collective-permute-start(bf16[144,128]{1,0:T(8,128)(2,1)} %get-tuple-element.89), channel_id=1, source_target_pairs={{0,2},{1,3},{2,0},{3,1},{4,6},{5,7},{6,4},{7,5},{8,10},{9,11},{10,... | collective-permute-start | bytes 110600 | tf_op jit(solution)/shard_map/ppermute | solution.py:109
  14.8 6.6 %collective-permute-start = (bf16[144,128]{1,0:T(8,128)(2,1)}, bf16[144,128]{1,0:T(8,128)(2,1)S(1)}, u32[]{:S(2)}, u32[]{:S(2)}) collective-permute-start(bf16[144,128]{1,0:T(8,128)(2,1)} %get-tuple-element.89), channel_id=1, source_target_pairs={{0,1},{1,2},{2,3},{3,0},{4,5},{5,6},{6,7},{7,4},{8,9},{9,10},{10,1... | collective-permute-start | bytes 110600 | tf_op jit(solution)/shard_map/ppermute | solution.py:109
  14.9 19.7 %collective-permute-start.8 = (bf16[752,128]{1,0:T(8,128)(2,1)}, bf16[752,128]{1,0:T(8,128)(2,1)S(1)}, u32[]{:S(2)}, u32[]{:S(2)}) collective-permute-start(bf16[752,128]{1,0:T(8,128)(2,1)} %get-tuple-element.91), channel_id=1, source_target_pairs={{0,3},{1,0},{2,1},{3,2},{4,7},{5,4},{6,5},{7,6},{8,11},{9,8},{10,9... | collective-permute-start | bytes 577544 | tf_op jit(solution)/shard_map/ppermute | solution.py:109
  18.7 16.9 %collective-permute-start.7 = (bf16[752,128]{1,0:T(8,128)(2,1)}, bf16[752,128]{1,0:T(8,128)(2,1)S(1)}, u32[]{:S(2)}, u32[]{:S(2)}) collective-permute-start(bf16[752,128]{1,0:T(8,128)(2,1)} %get-tuple-element.91), channel_id=1, source_target_pairs={{0,2},{1,3},{2,0},{3,1},{4,6},{5,7},{6,4},{7,5},{8,10},{9,11},{10,... | collective-permute-start | bytes 577544 | tf_op jit(solution)/shard_map/ppermute | solution.py:109
  20.2 15.4 %collective-permute-start.6 = (bf16[752,128]{1,0:T(8,128)(2,1)}, bf16[752,128]{1,0:T(8,128)(2,1)S(1)}, u32[]{:S(2)}, u32[]{:S(2)}) collective-permute-start(bf16[752,128]{1,0:T(8,128)(2,1)} %get-tuple-element.91), channel_id=1, source_target_pairs={{0,1},{1,2},{2,3},{3,0},{4,5},{5,6},{6,7},{7,4},{8,9},{9,10},{10,1... | collective-permute-start | bytes 577544 | tf_op jit(solution)/shard_map/ppermute | solution.py:109
  22.2 5.7 %collective-permute-start.4 = (bf16[4,144,128]{2,1,0:T(8,128)(2,1)S(1)}, bf16[4,144,128]{2,1,0:T(8,128)(2,1)S(1)}, u32[]{:S(2)}, u32[]{:S(2)}) collective-permute-start(bf16[4,144,128]{2,1,0:T(8,128)(2,1)S(1)} %get-tuple-element.182), channel_id=1, source_target_pairs={{0,8},{4,12},{8,0},{12,4},{16,24},{20,28},{24,16},{28,20},{1,9},{5... | collective-permute-start | bytes 442376 | tf_op jit(solution)/shard_map/ppermute | solution.py:104
  23.8 7.7 %collective-permute-start.3 = (bf16[4,144,128]{2,1,0:T(8,128)(2,1)S(1)}, bf16[4,144,128]{2,1,0:T(8,128)(2,1)S(1)}, u32[]{:S(2)}, u32[]{:S(2)}) collective-permute-start(bf16[4,144,128]{2,1,0:T(8,128)(2,1)S(1)} %get-tuple-element.182), channel_id=1, source_target_pairs={{0,16},{4,20},{8,24},{12,28},{16,0},{20,4},{24,8},{28,12},{1,17},{... | collective-permute-start | bytes 442376 | tf_op jit(solution)/shard_map/ppermute | solution.py:104
  28.0 6.6 %collective-permute-start.5 = (bf16[4,144,128]{2,1,0:T(8,128)(2,1)S(1)}, bf16[4,144,128]{2,1,0:T(8,128)(2,1)S(1)}, u32[]{:S(2)}, u32[]{:S(2)}) collective-permute-start(bf16[4,144,128]{2,1,0:T(8,128)(2,1)S(1)} %get-tuple-element.182), channel_id=1, source_target_pairs={{0,24},{4,28},{8,16},{12,20},{16,8},{20,12},{24,0},{28,4},{1,25},{... | collective-permute-start | bytes 442376 | tf_op jit(solution)/shard_map/ppermute | solution.py:104
  34.6 7.5 %copy-start.1 = (bf16[256,576]{0,1:T(8,128)(2,1)S(1)}, bf16[256,576]{0,1:T(8,128)(2,1)}, u32[]{:S(2)}) copy-start(bf16[256,576]{0,1:T(8,128)(2,1)} %param.14) | copy-start | bytes 884740
  34.6 7.5 %copy-start.16 = (s32[4]{0:T(128)S(1)}, s32[4]{0:T(128)}, u32[]{:S(2)}) copy-start(s32[4]{0:T(128)} %pad_add_fusion.1.refs_0_) | copy-start | bytes 52
  36.9 18.2 %collective-permute-start.9 = (bf16[4,752,128]{2,1,0:T(8,128)(2,1)}, bf16[4,752,128]{2,1,0:T(8,128)(2,1)}, u32[]{:S(2)}, u32[]{:S(2)}) collective-permute-start(bf16[4,752,128]{2,1,0:T(8,128)(2,1)} %get-tuple-element.175), channel_id=1, source_target_pairs={{0,16},{4,12},{8,24},{12,4},{16,0},{20,28},{24,8},{28,20},{1,17},{... | collective-permute-start | bytes 2310152 | tf_op jit(solution)/shard_map/ppermute | solution.py:119
  39.9 15.1 %copy-start.19 = (bf16[1,4,752,128]{3,2,1,0:T(8,128)(2,1)S(1)}, bf16[1,4,752,128]{3,2,1,0:T(8,128)(2,1)}, u32[]{:S(2)}) copy-start(bf16[1,4,752,128]{3,2,1,0:T(8,128)(2,1)} %get-tuple-element.174) | copy-start | bytes 2310148
  40.0 2.1 %collective-permute-start.14 = (bf16[4,4,144,128]{3,2,1,0:T(8,128)(2,1)S(1)}, bf16[4,4,144,128]{3,2,1,0:T(8,128)(2,1)S(1)}, u32[]{:S(2)}, u32[]{:S(2)}) collective-permute-start(bf16[4,4,144,128]{3,2,1,0:T(8,128)(2,1)S(1)} %pad_maximum_fusion.3.refs_1_), channel_id=1, source_target_pairs={{0,4},{4,0},{8,12},{12,8},{16,20},{20,16},{24,28},{28,24},{1,5},{5... | collective-permute-start | bytes 1769480 | tf_op jit(solution)/shard_map/ppermute | solution.py:104
  47.2 10.4 %copy-start.3 = (bf16[256,576]{1,0:T(8,128)(2,1)}, bf16[256,576]{1,0:T(8,128)(2,1)S(1)}, u32[]{:S(2)}) copy-start(bf16[256,576]{1,0:T(8,128)(2,1)S(1)} %get-tuple-element.102.refs_0_) | copy-start | bytes 884740
  47.2 10.4 %copy-start.5 = (bf16[256,384]{1,0:T(8,128)(2,1)}, bf16[256,384]{1,0:T(8,128)(2,1)S(1)}, u32[]{:S(2)}) copy-start(bf16[256,384]{1,0:T(8,128)(2,1)S(1)} %get-tuple-element.106.refs_3_) | copy-start | bytes 589828
  47.2 11.9 %collective-permute-start.17 = (bf16[256,384]{1,0:T(8,128)(2,1)S(1)}, bf16[256,384]{1,0:T(8,128)(2,1)S(1)}, u32[]{:S(2)}, u32[]{:S(2)}) collective-permute-start(bf16[256,384]{1,0:T(8,128)(2,1)S(1)} %get-tuple-element.106.refs_3_), channel_id=1, source_target_pairs={{0,3},{4,7},{8,11},{12,15},{16,19},{20,23},{24,27},{28,31}} | collective-permute-start | bytes 589832 | tf_op jit(solution)/shard_map/ppermute | solution.py:912
  50.5 9.5 %collective-permute-start.16 = (bf16[256,384]{1,0:T(8,128)(2,1)S(1)}, bf16[256,384]{1,0:T(8,128)(2,1)S(1)}, u32[]{:S(2)}, u32[]{:S(2)}) collective-permute-start(bf16[256,384]{1,0:T(8,128)(2,1)S(1)} %get-tuple-element.106.refs_3_), channel_id=1, source_target_pairs={{0,2},{1,3},{4,6},{5,7},{8,10},{9,11},{12,14},{13,15},{16,18},{17,... | collective-permute-start | bytes 589832 | tf_op jit(solution)/shard_map/ppermute | solution.py:912
  53.5 9.8 %collective-permute-start.15 = (bf16[256,384]{1,0:T(8,128)(2,1)S(1)}, bf16[256,384]{1,0:T(8,128)(2,1)S(1)}, u32[]{:S(2)}, u32[]{:S(2)}) collective-permute-start(bf16[256,384]{1,0:T(8,128)(2,1)S(1)} %get-tuple-element.106.refs_3_), channel_id=1, source_target_pairs={{0,1},{1,2},{2,3},{4,5},{5,6},{6,7},{8,9},{9,10},{10,11},{12,13},{... | collective-permute-start | bytes 589832 | tf_op jit(solution)/shard_map/ppermute | solution.py:912
  57.6 20.4 %collective-permute-start.10 = (bf16[2,4,752,128]{3,2,1,0:T(8,128)(2,1)}, bf16[2,4,752,128]{3,2,1,0:T(8,128)(2,1)}, u32[]{:S(2)}, u32[]{:S(2)}) collective-permute-start(bf16[2,4,752,128]{3,2,1,0:T(8,128)(2,1)} %pad_maximum_fusion.refs_5_), channel_id=1, source_target_pairs={{0,8},{4,20},{8,0},{12,28},{16,24},{20,4},{24,16},{28,12},{1,9},{5... | collective-permute-start | bytes 4620296 | tf_op jit(solution)/shard_map/ppermute | solution.py:119
  59.1 5.1 %copy-start.7 = (bf16[256,384]{1,0:T(8,128)(2,1)}, bf16[256,384]{1,0:T(8,128)(2,1)S(1)}, u32[]{:S(2)}) copy-start(bf16[256,384]{1,0:T(8,128)(2,1)S(1)} %collective-permute-done.17.refs_6_) | copy-start | bytes 589828
  60.0 4.2 %copy-start.9 = (bf16[256,384]{1,0:T(8,128)(2,1)}, bf16[256,384]{1,0:T(8,128)(2,1)S(1)}, u32[]{:S(2)}) copy-start(bf16[256,384]{1,0:T(8,128)(2,1)S(1)} %collective-permute-done.16.refs_5_) | copy-start | bytes 589828
  63.4 14.6 %collective-permute-start.18 = (bf16[2,4,752,128]{3,2,1,0:T(8,128)(2,1)}, bf16[2,4,752,128]{3,2,1,0:T(8,128)(2,1)}, u32[]{:S(2)}, u32[]{:S(2)}) collective-permute-start(bf16[2,4,752,128]{3,2,1,0:T(8,128)(2,1)} %pad_maximum_fusion.refs_5_), channel_id=1, source_target_pairs={{0,4},{4,0},{8,12},{12,8},{16,20},{20,16},{24,28},{28,24},{1,5},{5... | collective-permute-start | bytes 4620296 | tf_op jit(solution)/shard_map/ppermute | solution.py:104
  77.9 3.6 %collective-permute-start.19 = (bf16[2,4,752,128]{3,2,1,0:T(8,128)(2,1)}, bf16[2,4,752,128]{3,2,1,0:T(8,128)(2,1)S(1)}, u32[]{:S(2)}, u32[]{:S(2)}) collective-permute-start(bf16[2,4,752,128]{3,2,1,0:T(8,128)(2,1)} %collective-permute-done.10.refs_6_), channel_id=1, source_target_pairs={{0,4},{4,0},{8,12},{12,8},{16,20},{20,16},{24,28},{28,24},{1,5},{5... | collective-permute-start | bytes 4620296 | tf_op jit(solution)/shard_map/ppermute | solution.py:104
  82.7 13.3 %copy-start.4 = (bf16[256,576]{1,0:T(8,128)(2,1)S(1)}, bf16[256,576]{1,0:T(8,128)(2,1)}, u32[]{:S(2)}) copy-start(bf16[256,576]{1,0:T(8,128)(2,1)} %copy-done.3) | copy-start | bytes 884740
  82.7 13.3 %copy-start.6 = (bf16[256,384]{1,0:T(8,128)(2,1)S(1)}, bf16[256,384]{1,0:T(8,128)(2,1)}, u32[]{:S(2)}) copy-start(bf16[256,384]{1,0:T(8,128)(2,1)} %copy-done.5) | copy-start | bytes 589828
  82.7 13.3 %copy-start.8 = (bf16[256,384]{1,0:T(8,128)(2,1)S(1)}, bf16[256,384]{1,0:T(8,128)(2,1)}, u32[]{:S(2)}) copy-start(bf16[256,384]{1,0:T(8,128)(2,1)} %copy-done.7) | copy-start | bytes 589828
  82.7 13.3 %copy-start.10 = (bf16[256,384]{1,0:T(8,128)(2,1)S(1)}, bf16[256,384]{1,0:T(8,128)(2,1)}, u32[]{:S(2)}) copy-start(bf16[256,384]{1,0:T(8,128)(2,1)} %copy-done.9) | copy-start | bytes 589828
  82.7 13.3 %copy-start.12 = (bf16[256,384]{1,0:T(8,128)(2,1)S(1)}, bf16[256,384]{1,0:T(8,128)(2,1)}, u32[]{:S(2)}) copy-start(bf16[256,384]{1,0:T(8,128)(2,1)} %copy-done.11) | copy-start | bytes 589828
  82.7 13.3 %copy-start.14 = (f32[256,576]{1,0:T(8,128)S(1)}, f32[256,576]{1,0:T(8,128)}, u32[]{:S(2)}) copy-start(f32[256,576]{1,0:T(8,128)} %get-tuple-element.120.refs_2_) | copy-start | bytes 1769476
  95.8 12.0 %collective-permute-start.20 = (bf16[2,2,4,752,128]{4,3,2,1,0:T(8,128)(2,1)}, bf16[2,2,4,752,128]{4,3,2,1,0:T(8,128)(2,1)S(1)}, u32[]{:S(2)}, u32[]{:S(2)}) collective-permute-start(bf16[2,2,4,752,128]{4,3,2,1,0:T(8,128)(2,1)} %get-tuple-element.118), channel_id=1, source_target_pairs={{0,4},{4,0},{8,12},{12,8},{16,20},{20,16},{24,28},{28,24},{1,5},{5... | collective-permute-start | bytes 9240584 | tf_op jit(solution)/shard_map/ppermute | solution.py:104
  96.0 2.3 %copy-start = (bf16[9,256,1024]{2,1,0:T(8,128)(2,1)S(1)}, bf16[9,256,1024]{2,1,0:T(8,128)(2,1)}, u32[]{:S(2)}) copy-start(bf16[9,256,1024]{2,1,0:T(8,128)(2,1)} %get-tuple-element.121.refs_7_) | copy-start | bytes 14155780
  99.3 8.6 %copy-start.20 = (bf16[2,2,4,752,128]{4,3,2,1,0:T(8,128)(2,1)S(1)}, bf16[2,2,4,752,128]{4,3,2,1,0:T(8,128)(2,1)}, u32[]{:S(2)}) copy-start(bf16[2,2,4,752,128]{4,3,2,1,0:T(8,128)(2,1)} %get-tuple-element.117) | copy-start | bytes 9240580
  108.3 22.1 %collective-permute-start.21 = (bf16[2,4,752,128]{3,2,1,0:T(8,128)(2,1)S(1)}, bf16[2,4,752,128]{3,2,1,0:T(8,128)(2,1)S(1)}, u32[]{:S(2)}, u32[]{:S(2)}) collective-permute-start(bf16[2,4,752,128]{3,2,1,0:T(8,128)(2,1)S(1)} %fusion), channel_id=1, source_target_pairs={{0,8},{4,20},{8,0},{12,28},{16,24},{20,4},{24,16},{28,12},{1,9},{5... | collective-permute-start | bytes 4620296 | tf_op jit(solution)/shard_map/ppermute | solution.py:119
  109.8 9.1 %collective-permute-start.22 = (bf16[256,384]{1,0:T(8,128)(2,1)S(1)}, bf16[256,384]{1,0:T(8,128)(2,1)S(1)}, u32[]{:S(2)}, u32[]{:S(2)}) collective-permute-start(bf16[256,384]{1,0:T(8,128)(2,1)S(1)} %get-tuple-element.129), channel_id=1, source_target_pairs={{1,0},{2,1},{3,2},{5,4},{6,5},{7,6},{9,8},{10,9},{11,10},{13,12},{... | collective-permute-start | bytes 589832 | tf_op jit(solution)/shard_map/ppermute | solution.py:929
  111.1 19.3 %collective-permute-start.23 = (bf16[256,384]{1,0:T(8,128)(2,1)S(1)}, bf16[256,384]{1,0:T(8,128)(2,1)S(1)}, u32[]{:S(2)}, u32[]{:S(2)}) collective-permute-start(bf16[256,384]{1,0:T(8,128)(2,1)S(1)} %get-tuple-element.130), channel_id=1, source_target_pairs={{2,0},{3,1},{6,4},{7,5},{10,8},{11,9},{14,12},{15,13},{18,16},{19,... | collective-permute-start | bytes 589832 | tf_op jit(solution)/shard_map/ppermute | solution.py:929
  112.4 18.0 %collective-permute-start.24 = (bf16[256,384]{1,0:T(8,128)(2,1)S(1)}, bf16[256,384]{1,0:T(8,128)(2,1)S(1)}, u32[]{:S(2)}, u32[]{:S(2)}) collective-permute-start(bf16[256,384]{1,0:T(8,128)(2,1)S(1)} %get-tuple-element.131), channel_id=1, source_target_pairs={{3,0},{7,4},{11,8},{15,12},{19,16},{23,20},{27,24},{31,28}} | collective-permute-start | bytes 589832 | tf_op jit(solution)/shard_map/ppermute | solution.py:929
  130.4 1.9 %copy-start.2 = (bf16[256,576]{0,1:T(8,128)(2,1)S(1)}, bf16[256,576]{0,1:T(8,128)(2,1)}, u32[]{:S(2)}) copy-start(bf16[256,576]{0,1:T(8,128)(2,1)} %param.14) | copy-start | bytes 884740
  130.4 1.9 %copy-start.13 = (f32[256,576]{1,0:T(8,128)S(1)}, f32[256,576]{1,0:T(8,128)}, u32[]{:S(2)}) copy-start(f32[256,576]{1,0:T(8,128)} %get-tuple-element.142.refs_7_) | copy-start | bytes 1769476
  130.4 1.9 %copy-start.17 = (s32[4]{0:T(128)S(1)}, s32[4]{0:T(128)}, u32[]{:S(2)}) copy-start(s32[4]{0:T(128)} %pad_add_fusion.1.refs_0_) | copy-start | bytes 52
  130.7 11.9 %collective-permute-start.25 = (bf16[4,752,128]{2,1,0:T(8,128)(2,1)S(1)}, bf16[4,752,128]{2,1,0:T(8,128)(2,1)S(1)}, u32[]{:S(2)}, u32[]{:S(2)}) collective-permute-start(bf16[4,752,128]{2,1,0:T(8,128)(2,1)S(1)} %fusion.1), channel_id=1, source_target_pairs={{0,16},{4,12},{8,24},{12,4},{16,0},{20,28},{24,8},{28,20},{1,17},{... | collective-permute-start | bytes 2310152 | tf_op jit(solution)/shard_map/ppermute | solution.py:119
  136.8 2.2 %collective-permute-start.26 = (bf16[4,4,160,128]{3,2,1,0:T(8,128)(2,1)S(1)}, bf16[4,4,160,128]{3,2,1,0:T(8,128)(2,1)S(1)}, u32[]{:S(2)}, u32[]{:S(2)}) collective-permute-start(bf16[4,4,160,128]{3,2,1,0:T(8,128)(2,1)S(1)} %get-tuple-element.150), channel_id=1, source_target_pairs={{0,4},{4,0},{8,12},{12,8},{16,20},{20,16},{24,28},{28,24},{1,5},{5... | collective-permute-start | bytes 1966088 | tf_op jit(solution)/shard_map/ppermute | solution.py:104
  142.8 7.8 %collective-permute-start.32 = (bf16[4,160,128]{2,1,0:T(8,128)(2,1)S(1)}, bf16[4,160,128]{2,1,0:T(8,128)(2,1)S(1)}, u32[]{:S(2)}, u32[]{:S(2)}) collective-permute-start(bf16[4,160,128]{2,1,0:T(8,128)(2,1)S(1)} %get-tuple-element.171), channel_id=1, source_target_pairs={{0,24},{4,28},{8,16},{12,20},{16,8},{20,12},{24,0},{28,4},{1,25},{... | collective-permute-start | bytes 491528 | tf_op jit(solution)/shard_map/ppermute | solution.py:104
  144.9 7.1 %collective-permute-start.31 = (bf16[4,160,128]{2,1,0:T(8,128)(2,1)S(1)}, bf16[4,160,128]{2,1,0:T(8,128)(2,1)S(1)}, u32[]{:S(2)}, u32[]{:S(2)}) collective-permute-start(bf16[4,160,128]{2,1,0:T(8,128)(2,1)S(1)} %get-tuple-element.172), channel_id=1, source_target_pairs={{0,16},{4,20},{8,24},{12,28},{16,0},{20,4},{24,8},{28,12},{1,17},{... | collective-permute-start | bytes 491528 | tf_op jit(solution)/shard_map/ppermute | solution.py:104
  145.8 6.2 %collective-permute-start.30 = (bf16[4,160,128]{2,1,0:T(8,128)(2,1)S(1)}, bf16[4,160,128]{2,1,0:T(8,128)(2,1)S(1)}, u32[]{:S(2)}, u32[]{:S(2)}) collective-permute-start(bf16[4,160,128]{2,1,0:T(8,128)(2,1)S(1)} %get-tuple-element.173), channel_id=1, source_target_pairs={{0,8},{4,12},{8,0},{12,4},{16,24},{20,28},{24,16},{28,20},{1,9},{5... | collective-permute-start | bytes 491528 | tf_op jit(solution)/shard_map/ppermute | solution.py:104
  146.7 9.7 %collective-permute-start.27 = (bf16[752,128]{1,0:T(8,128)(2,1)S(1)}, bf16[752,128]{1,0:T(8,128)(2,1)S(1)}, u32[]{:S(2)}, u32[]{:S(2)}) collective-permute-start(bf16[752,128]{1,0:T(8,128)(2,1)S(1)} %get-tuple-element.167), channel_id=1, source_target_pairs={{0,1},{1,2},{2,3},{3,0},{4,5},{5,6},{6,7},{7,4},{8,9},{9,10},{10,1... | collective-permute-start | bytes 577544 | tf_op jit(solution)/shard_map/ppermute | solution.py:109
  146.7 10.3 %collective-permute-start.29 = (bf16[752,128]{1,0:T(8,128)(2,1)S(1)}, bf16[752,128]{1,0:T(8,128)(2,1)S(1)}, u32[]{:S(2)}, u32[]{:S(2)}) collective-permute-start(bf16[752,128]{1,0:T(8,128)(2,1)S(1)} %get-tuple-element.168), channel_id=1, source_target_pairs={{0,3},{1,0},{2,1},{3,2},{4,7},{5,4},{6,5},{7,6},{8,11},{9,8},{10,9... | collective-permute-start | bytes 577544 | tf_op jit(solution)/shard_map/ppermute | solution.py:109
  150.6 15.5 %collective-permute-start.28 = (bf16[752,128]{1,0:T(8,128)(2,1)S(1)}, bf16[752,128]{1,0:T(8,128)(2,1)S(1)}, u32[]{:S(2)}, u32[]{:S(2)}) collective-permute-start(bf16[752,128]{1,0:T(8,128)(2,1)S(1)} %get-tuple-element.169), channel_id=1, source_target_pairs={{0,2},{1,3},{2,0},{3,1},{4,6},{5,7},{6,4},{7,5},{8,10},{9,11},{10,... | collective-permute-start | bytes 577544 | tf_op jit(solution)/shard_map/ppermute | solution.py:109
  152.1 14.2 %collective-permute-start.33 = (bf16[160,128]{1,0:T(8,128)(2,1)S(1)}, bf16[160,128]{1,0:T(8,128)(2,1)S(1)}, u32[]{:S(2)}, u32[]{:S(2)}) collective-permute-start(bf16[160,128]{1,0:T(8,128)(2,1)S(1)} %get-tuple-element.176), channel_id=1, source_target_pairs={{0,1},{1,2},{2,3},{3,0},{4,5},{5,6},{6,7},{7,4},{8,9},{9,10},{10,1... | collective-permute-start | bytes 122888 | tf_op jit(solution)/shard_map/ppermute | solution.py:109
  152.2 14.1 %collective-permute-start.35 = (bf16[160,128]{1,0:T(8,128)(2,1)S(1)}, bf16[160,128]{1,0:T(8,128)(2,1)S(1)}, u32[]{:S(2)}, u32[]{:S(2)}) collective-permute-start(bf16[160,128]{1,0:T(8,128)(2,1)S(1)} %get-tuple-element.177), channel_id=1, source_target_pairs={{0,3},{1,0},{2,1},{3,2},{4,7},{5,4},{6,5},{7,6},{8,11},{9,8},{10,9... | collective-permute-start | bytes 122888 | tf_op jit(solution)/shard_map/ppermute | solution.py:109
  156.4 10.6 %collective-permute-start.34 = (bf16[160,128]{1,0:T(8,128)(2,1)S(1)}, bf16[160,128]{1,0:T(8,128)(2,1)S(1)}, u32[]{:S(2)}, u32[]{:S(2)}) collective-permute-start(bf16[160,128]{1,0:T(8,128)(2,1)S(1)} %get-tuple-element.178), channel_id=1, source_target_pairs={{0,2},{1,3},{2,0},{3,1},{4,6},{5,7},{6,4},{7,5},{8,10},{9,11},{10,... | collective-permute-start | bytes 122888 | tf_op jit(solution)/shard_map/ppermute | solution.py:109
  167.1 8.5 %collective-permute-start.37 = (bf16[912,128]{1,0:T(8,128)(2,1)S(1)}, bf16[912,128]{1,0:T(8,128)(2,1)S(1)}, u32[]{:S(2)}, u32[]{:S(2)}) collective-permute-start(bf16[912,128]{1,0:T(8,128)(2,1)S(1)} %get-tuple-element.180), channel_id=1, source_target_pairs={{0,8},{4,12},{8,0},{12,4},{16,24},{20,28},{24,16},{28,20},{1,9},{5... | collective-permute-start | bytes 700424 | tf_op jit(solution)/shard_map/ppermute | solution.py:104
  168.5 10.8 %collective-permute-start.36 = (bf16[912,128]{1,0:T(8,128)(2,1)S(1)}, bf16[912,128]{1,0:T(8,128)(2,1)S(1)}, u32[]{:S(2)}, u32[]{:S(2)}) collective-permute-start(bf16[912,128]{1,0:T(8,128)(2,1)S(1)} %get-tuple-element.180), channel_id=1, source_target_pairs={{0,16},{4,20},{8,24},{12,28},{16,0},{20,4},{24,8},{28,12},{1,17},{... | collective-permute-start | bytes 700424 | tf_op jit(solution)/shard_map/ppermute | solution.py:104
  170.3 9.1 %collective-permute-start.38 = (bf16[912,128]{1,0:T(8,128)(2,1)S(1)}, bf16[912,128]{1,0:T(8,128)(2,1)S(1)}, u32[]{:S(2)}, u32[]{:S(2)}) collective-permute-start(bf16[912,128]{1,0:T(8,128)(2,1)S(1)} %get-tuple-element.180), channel_id=1, source_target_pairs={{0,24},{4,28},{8,16},{12,20},{16,8},{20,12},{24,0},{28,4},{1,25},{... | collective-permute-start | bytes 700424 | tf_op jit(solution)/shard_map/ppermute | solution.py:104
  179.5 2.6 %collective-permute-start.39 = (bf16[4,912,128]{2,1,0:T(8,128)(2,1)S(1)}, bf16[4,912,128]{2,1,0:T(8,128)(2,1)S(1)}, u32[]{:S(2)}, u32[]{:S(2)}) collective-permute-start(bf16[4,912,128]{2,1,0:T(8,128)(2,1)S(1)} %pad_maximum_fusion.1.refs_1_), channel_id=1, source_target_pairs={{0,4},{4,0},{8,12},{12,8},{16,20},{20,16},{24,28},{28,24},{1,5},{5... | collective-permute-start | bytes 2801672 | tf_op jit(solution)/shard_map/ppermute | solution.py:104
  (4 other events, 4.8 us)

commit v4 on v3

--- a/solution.py
+++ b/solution.py
@@ -12,7 +12,6 @@
 LANES = 128
 SMALL = 16
 MIB = 1024 * 1024
-PROBS_AHEAD = 2
 AHEAD = 4
 BIG = 58
 
@@ -412,17 +411,9 @@
 def attend_back_kernel(sizes, query, grad, exact, *refs):
     f32, bf16 = jnp.float32, jnp.bfloat16
     q_width, kv_width, head_size = sizes
-    probs, sems = refs[-2:]
-    refs = refs[:-2]
     groups = (len(refs) - 2) // 2
-    probs_in = refs[groups]
+    probs = refs[groups]
     refs = refs[:groups] + refs[groups + 1 :]
-    copies = [
-        pltpu.make_async_copy(probs_in.at[head], probs.at[head], sems.at[head])
-        for head in range(probs.shape[0])
-    ]
-    for copy in copies[:PROBS_AHEAD]:
-        copy.start()
     held = refs[:groups]
     query_grad = refs[groups]
     kv_grads = refs[groups + 1 :]
@@ -439,9 +430,6 @@
         key_t = value_t = None
         for head in range(g * per, (g + 1) * per):
             cols = slice(head * head_size, (head + 1) * head_size)
-            copies[head].wait()
-            if head + PROBS_AHEAD < len(copies):
-                copies[head + PROBS_AHEAD].start()
             low = probs[head]
             inner = jnp.sum(grad[:, cols].astype(f32) * exact[:, cols], axis=1, keepdims=True)
             scores = dot(grad[:, cols], values, (1, 1)) - inner
@@ -467,10 +455,10 @@
     return staged_call(
         functools.partial(attend_back_kernel, sizes),
         "attend_back",
-        kept("staged", query, grad, exact, *held) + kept("hbm", probs),
+        kept("staged", query, grad, exact, *held) + kept("vmem", probs),
         (shape((toks, q_width), f32),) + tuple(shape((toks, 2 * kv_width), bf16) for _ in held),
         (vmem(),) * (1 + len(held)),
-        [pltpu.VMEM(probs.shape, bf16), pltpu.SemaphoreType.DMA((probs.shape[0],))],
+        (),
         36,
     )
 

time: 185 us -> 183 us (0.989)
  Pallas kernels: 48.8 us -> 46.7 us
    pallas_call x8, Pallas kernels: 48.8 us -> 46.7 us  [staged_call(): pl.pallas_call(whole, out_shape=out_shape, in_specs=[specs[kind]() for ki...]
  transfers between devices with their start and end apart: 40 -> 40, of which waited for: 21 -> 21; matrix products, arithmetic and copies ran while one was open for 4% -> 4% of each run, Pallas kernels for 16% -> 15%
where the time goes in v4:
time: 183 us
  waiting for transfers between devices  65.1 us (36%)
  starting transfers between devices  54.1 us (30%)
  Pallas kernels  46.7 us (26%)
  other arithmetic  8.38 us (5%)
  local copies, waits for them, and re-layouts  7.03 us (4%)
    pallas_call x8, Pallas kernels, staged_call(): pl.pallas_call(whole, out_shape=out_shape, in_specs=[specs[kind]() for ki...  46.7 us
    ppermute x15, waiting for transfers between devices, hop(): return lax.ppermute(value, 'rep', [(i, i ^ bit) for i in range(count)])  26.1 us
    ppermute x15, starting transfers between devices, shift(): lax.ppermute(value, 'grp', [(i, (i + step) % count) for i in range(count)])  22.3 us
    ppermute x15, starting transfers between devices, hop(): return lax.ppermute(value, 'rep', [(i, i ^ bit) for i in range(count)])  13.9 us
    ppermute x3, waiting for transfers between devices, body(): kv_back.append(lax.ppermute(kv_parts[step], 'grp', back))  12.4 us
    ppermute x15, waiting for transfers between devices, shift(): lax.ppermute(value, 'grp', [(i, (i + step) % count) for i in range(count)])  12.3 us
    ppermute x4, waiting for transfers between devices, hop_split(): lax.ppermute(value, 'rep', [(i, i ^ (odd if i % 2 else even)) for i in ra...  9.95 us
    ppermute x3, starting transfers between devices, body(): held.append(lax.ppermute(key_value, 'grp', ahead))  7.83 us
  transfers between devices with their start and end apart: 40, of which 21 were waited for; matrix products, arithmetic and copies ran while one was open for 4% of the time, Pallas kernels for 15%

profile of v4, /device:TPU:0, one launch (start us, length us, event | category | flops | bytes accessed | tf_op | source)
XLA Modules:
  0.0 182.5 jit_solution(15230535404956600435)
XLA Ops:
  0.7 0.6 pad_add_fusion.1.refs_0_
  1.3 3.2 %pack.1 = (bf16[144,128]{1,0:T(8,128)(2,1)}, bf16[752,128]{1,0:T(8,128)(2,1)}) custom-call(s32[4]{0:T(128)} %pad_add_fusion.1.refs_0_, bf16[144,576]{1,0:T(8,128)(2,1)} %refs_1_.1, bf16[144,192]{1,0:T(8,128)(2,1)} %refs_2_.1, bf16[144,192]{1,0:T(8,128)(2,1)} %refs_3_.1, bf16[144,1536]{1,0:T(8,128)(2,1)} %refs_4_.1, bf16[144,1536]{1,0:T(8,128)(2,1)} %refs_5_.1, ...), custom_call_target="tpu_custom_call" | custom-call | flops 1 | bytes 1024 | tf_op jit(solution)/shard_map/pack/pallas_call | solution.py:85
  4.6 5.1 %collective-permute-start.13 = (bf16[16,128]{1,0:T(8,128)(2,1)S(1)}, bf16[16,128]{1,0:T(8,128)(2,1)S(1)}, u32[]{:S(2)}, u32[]{:S(2)}) collective-permute-start(bf16[16,128]{1,0:T(8,128)(2,1)S(1)} %get-tuple-element.190), channel_id=1, source_target_pairs={{0,3},{1,0},{2,1},{3,2},{4,7},{5,4},{6,5},{7,6},{8,11},{9,8},{10,9... | collective-permute-start | bytes 12296 | tf_op jit(solution)/shard_map/ppermute | solution.py:108
  9.7 1.0 collective-permute-start.11
  10.7 2.8 %collective-permute-start.2 = (bf16[144,128]{1,0:T(8,128)(2,1)}, bf16[144,128]{1,0:T(8,128)(2,1)S(1)}, u32[]{:S(2)}, u32[]{:S(2)}) collective-permute-start(bf16[144,128]{1,0:T(8,128)(2,1)} %get-tuple-element.89), channel_id=1, source_target_pairs={{0,3},{1,0},{2,1},{3,2},{4,7},{5,4},{6,5},{7,6},{8,11},{9,8},{10,9... | collective-permute-start | bytes 110600 | tf_op jit(solution)/shard_map/ppermute | solution.py:108
  13.5 1.1 collective-permute-start.1
  14.9 3.8 %collective-permute-start.8 = (bf16[752,128]{1,0:T(8,128)(2,1)}, bf16[752,128]{1,0:T(8,128)(2,1)S(1)}, u32[]{:S(2)}, u32[]{:S(2)}) collective-permute-start(bf16[752,128]{1,0:T(8,128)(2,1)} %get-tuple-element.91), channel_id=1, source_target_pairs={{0,3},{1,0},{2,1},{3,2},{4,7},{5,4},{6,5},{7,6},{8,11},{9,8},{10,9... | collective-permute-start | bytes 577544 | tf_op jit(solution)/shard_map/ppermute | solution.py:108
  18.8 0.6 gather_fusion
  20.2 0.7 collective-permute-start.6
  20.9 0.5 collective-permute-done
  21.4 0.8 fusion.33
  22.2 1.6 collective-permute-start.4
  23.8 1.5 collective-permute-start.3
  25.3 2.7 %collective-permute-done.4 = bf16[4,144,128]{2,1,0:T(8,128)(2,1)S(1)} collective-permute-done((bf16[4,144,128]{2,1,0:T(8,128)(2,1)S(1)}, bf16[4,144,128]{2,1,0:T(8,128)(2,1)S(1)}, u32[]{:S(2)}, u32[]{:S(2)}) %collective-permute-start.4) | collective-permute-done | bytes 147488 | tf_op jit(solution)/shard_map/ppermute | solution.py:103
  28.0 3.5 %collective-permute-start.5 = (bf16[4,144,128]{2,1,0:T(8,128)(2,1)S(1)}, bf16[4,144,128]{2,1,0:T(8,128)(2,1)S(1)}, u32[]{:S(2)}, u32[]{:S(2)}) collective-permute-start(bf16[4,144,128]{2,1,0:T(8,128)(2,1)S(1)} %get-tuple-element.182), channel_id=1, source_target_pairs={{0,24},{4,28},{8,16},{12,20},{16,8},{20,12},{24,0},{28,4},{1,25},{... | collective-permute-start | bytes 442376 | tf_op jit(solution)/shard_map/ppermute | solution.py:103
  31.4 3.1 %collective-permute-done.5 = bf16[4,144,128]{2,1,0:T(8,128)(2,1)S(1)} collective-permute-done((bf16[4,144,128]{2,1,0:T(8,128)(2,1)S(1)}, bf16[4,144,128]{2,1,0:T(8,128)(2,1)S(1)}, u32[]{:S(2)}, u32[]{:S(2)}) %collective-permute-start.5) | collective-permute-done | bytes 147488 | tf_op jit(solution)/shard_map/ppermute | solution.py:103
  34.6 1.0 collective-permute-done.7
  35.6 1.3 fusion.34
  36.9 1.5 collective-permute-start.9
  38.4 0.6 broadcast_select_fusion.refs_2_
  39.2 0.7 reshape.259.refs_4_
  40.0 2.0 %collective-permute-done.14.refs_2_ = bf16[4,4,144,128]{3,2,1,0:T(8,128)(2,1)S(1)} collective-permute-done((bf16[4,4,144,128]{3,2,1,0:T(8,128)(2,1)S(1)}, bf16[4,4,144,128]{3,2,1,0:T(8,128)(2,1)S(1)}, u32[]{:S(2)}, u32[]{:S(2)}) %collective-permute-start.14) | collective-permute-done | bytes 589856 | tf_op jit(solution)/shard_map/ppermute | solution.py:103
  42.0 5.1 %proj.1 = (bf16[256,576]{1,0:T(8,128)(2,1)S(1)}, f32[256,768]{1,0:T(8,128)S(1)}, bf16[256,576]{1,0:T(8,128)(2,1)S(1)}, bf16[256,384]{1,0:T(8,128)(2,1)S(1)}, bf16[576,1024]{1,0:T(8,128)(2,1)S(1)}) custom-call(s32[4]{0:T(128)S(1)} %copy-done.16, bf16[4,4,144,128]{3,2,1,0:T(8,128)(2,1)S(1)} %pad_maximum_fusion.3.refs_1_, ...), custom_call_target="tpu_custom_call" | custom-call | flops 1 | bytes 1024 | tf_op jit(solution)/shard_map/proj/pallas_call | solution.py:85
  47.2 3.3 %collective-permute-start.17 = (bf16[256,384]{1,0:T(8,128)(2,1)S(1)}, bf16[256,384]{1,0:T(8,128)(2,1)S(1)}, u32[]{:S(2)}, u32[]{:S(2)}) collective-permute-start(bf16[256,384]{1,0:T(8,128)(2,1)S(1)} %get-tuple-element.106.refs_3_), channel_id=1, source_target_pairs={{0,3},{4,7},{8,11},{12,15},{16,19},{20,23},{24,27},{28,31}} | collective-permute-start | bytes 589832 | tf_op jit(solution)/shard_map/ppermute | solution.py:900
  50.5 3.1 %collective-permute-start.16 = (bf16[256,384]{1,0:T(8,128)(2,1)S(1)}, bf16[256,384]{1,0:T(8,128)(2,1)S(1)}, u32[]{:S(2)}, u32[]{:S(2)}) collective-permute-start(bf16[256,384]{1,0:T(8,128)(2,1)S(1)} %get-tuple-element.106.refs_3_), channel_id=1, source_target_pairs={{0,2},{1,3},{4,6},{5,7},{8,10},{9,11},{12,14},{13,15},{16,18},{17,... | collective-permute-start | bytes 589832 | tf_op jit(solution)/shard_map/ppermute | solution.py:900
  53.5 1.5 collective-permute-start.15
  55.1 2.5 %pad_maximum_fusion.refs_5_ = bf16[2,4,752,128]{3,2,1,0:T(8,128)(2,1)} fusion(bf16[1,4,752,128]{3,2,1,0:T(8,128)(2,1)} %bitcast.18, bf16[1,4,752,128]{3,2,1,0:T(8,128)(2,1)S(1)} %copy-done.19), kind=kLoop, calls=%fused_computation.3 | loop fusion | flops 770048 | bytes 3080192 | tf_op jit(solution)/shard_map/stack | solution.py:901
  57.6 1.5 collective-permute-start.10
  59.1 0.9 collective-permute-done.16.refs_5_
  60.0 3.4 %collective-permute-done.15.refs_4_ = bf16[256,384]{1,0:T(8,128)(2,1)S(1)} collective-permute-done((bf16[256,384]{1,0:T(8,128)(2,1)S(1)}, bf16[256,384]{1,0:T(8,128)(2,1)S(1)}, u32[]{:S(2)}, u32[]{:S(2)}) %collective-permute-start.15) | collective-permute-done | bytes 196640 | tf_op jit(solution)/shard_map/ppermute | solution.py:900
  63.4 0.8 copy.28.refs_1_
  64.2 7.4 %attend.1 = (bf16[256,576]{1,0:T(8,128)(2,1)}, f32[256,576]{1,0:T(8,128)}, bf16[9,256,1024]{2,1,0:T(8,128)(2,1)}) custom-call(bf16[256,576]{1,0:T(8,128)(2,1)} %copy-done.3, f32[256,1]{1,0:T(8,128)} %copy.28.refs_1_, f32[1,1024]{1,0:T(1,128)} %broadcast_select_fusion.refs_2_, bf16[256,384]{1,0:T(8,128)(2,1)} %copy-done.5, bf16[256,384]{1,0:T(8,128)(2,1)} %copy-done.11, ...), custom_call_target="tpu_custom_call" | custom-call | flops 1 | bytes 1024 | tf_op jit(solution)/shard_map/attend/pallas_call | solution.py:85
  71.6 6.3 %collective-permute-done.10.refs_6_ = bf16[2,4,752,128]{3,2,1,0:T(8,128)(2,1)} collective-permute-done((bf16[2,4,752,128]{3,2,1,0:T(8,128)(2,1)}, bf16[2,4,752,128]{3,2,1,0:T(8,128)(2,1)}, u32[]{:S(2)}, u32[]{:S(2)}) %collective-permute-start.10) | collective-permute-done | bytes 1540128 | tf_op jit(solution)/shard_map/ppermute | solution.py:118
  77.9 3.6 %collective-permute-done.19.refs_8_ = bf16[2,4,752,128]{3,2,1,0:T(8,128)(2,1)S(1)} collective-permute-done((bf16[2,4,752,128]{3,2,1,0:T(8,128)(2,1)}, bf16[2,4,752,128]{3,2,1,0:T(8,128)(2,1)S(1)}, u32[]{:S(2)}, u32[]{:S(2)}) %collective-permute-start.19) | collective-permute-done | bytes 1540128 | tf_op jit(solution)/shard_map/ppermute | solution.py:103
  81.5 1.1 copy-done.21
  82.7 13.1 %mlp.1 = (bf16[576,256]{1,0:T(8,128)(2,1)}, f32[256,576]{1,0:T(8,128)}, bf16[256,576]{1,0:T(8,128)(2,1)}, f32[1,576]{1,0:T(1,128)}, bf16[2,2,4,752,128]{4,3,2,1,...) custom-call(s32[4]{0:T(128)} %pad_add_fusion.1.refs_0_, bf16[256,576]{1,0:T(8,128)(2,1)} %get-tuple-element.112.refs_1_, ...), custom_call_target="tpu_custom_call" | custom-call | flops 1 | bytes 1024 | tf_op jit(solution)/shard_map/mlp/pallas_call | solution.py:85
  96.0 2.3 %copy-done = bf16[9,256,1024]{2,1,0:T(8,128)(2,1)S(1)} copy-done((bf16[9,256,1024]{2,1,0:T(8,128)(2,1)S(1)}, bf16[9,256,1024]{2,1,0:T(8,128)(2,1)}, u32[]{:S(2)}) %copy-start) | copy-done | bytes 4718616
  98.3 1.0 copy-done.15
  99.3 6.4 %attend_back.1 = (f32[256,576]{1,0:T(8,128)S(1)}, bf16[256,384]{1,0:T(8,128)(2,1)S(1)}, bf16[256,384]{1,0:T(8,128)(2,1)S(1)}, bf16[256,384]{1,0:T(8,128)(2,1)S(1)}, bf16[256,384]{1,0:T(8,128)(2,1)S(1)}) custom-call(bf16[256,576]{1,0:T(8,128)(2,1)S(1)} %copy-done.4, bf16[256,576]{1,0:T(8,128)(2,1)S(1)} %copy-done.15, f32[256,576]{1,0:T(8,128)S(1)} %copy-done.14, ...), custom_call_target="tpu_custom_call" | custom-call | flops 1 | bytes 1024 | tf_op jit(solution)/shard_map/attend_back/pallas_call | solution.py:85
  106.1 1.6 collective-permute-start.21
  107.7 1.3 collective-permute-start.22
  109.0 1.3 collective-permute-start.23
  110.3 1.3 collective-permute-start.24
  111.6 4.2 %query_back.1 = (bf16[576,576]{1,0:T(8,128)(2,1)S(1)}, f32[256,576]{1,0:T(8,128)S(1)}, f32[1,64]{1,0:T(1,128)S(1)}) custom-call(f32[256,576]{1,0:T(8,128)S(1)} %get-tuple-element.132.refs_0_, f32[256,768]{1,0:T(8,128)S(1)} %get-tuple-element.133.refs_1_.refs_4_, bf16[256,576]{1,0:T(8,128)(2,1)S(1)} %get-tuple-element.134.refs_2_.refs_5_, ...), custom_call_target="tpu_custom_call" | custom-call | flops 1 | bytes 1024 | tf_op jit(solution)/shard_map/query_back/pallas_call | solution.py:85
  115.8 0.9 collective-permute-done.22.refs_15_
  116.8 11.4 %collective-permute-done.23.refs_16_ = bf16[256,384]{1,0:T(8,128)(2,1)S(1)} collective-permute-done((bf16[256,384]{1,0:T(8,128)(2,1)S(1)}, bf16[256,384]{1,0:T(8,128)(2,1)S(1)}, u32[]{:S(2)}, u32[]{:S(2)}) %collective-permute-start.23) | collective-permute-done | bytes 196640 | tf_op jit(solution)/shard_map/ppermute | solution.py:917
  128.6 1.5 collective-permute-start.25
  130.1 4.5 %last.1 = (f32[576,256]{1,0:T(8,128)}, bf16[4,4,160,128]{3,2,1,0:T(8,128)(2,1)S(1)}, bf16[4,4,160,128]{3,2,1,0:T(8,128)(2,1)S(1)}) custom-call(s32[4]{0:T(128)S(1)} %copy-done.17, bf16[576,576]{1,0:T(8,128)(2,1)S(1)} %get-tuple-element.139.refs_1_, f32[256,576]{1,0:T(8,128)S(1)} %get-tuple-element.140.refs_2_, f32[1,64]{1,0:T(1,128)S(1)} %get-tuple-element.141.refs_3_, ...), custom_call_target="tpu_custom_call" | custom-call | flops 1 | bytes 1024 | tf_op jit(solution)/shard_map/last/pallas_call | solution.py:85
  134.8 2.1 %collective-permute-done.26 = bf16[4,4,160,128]{3,2,1,0:T(8,128)(2,1)S(1)} collective-permute-done((bf16[4,4,160,128]{3,2,1,0:T(8,128)(2,1)S(1)}, bf16[4,4,160,128]{3,2,1,0:T(8,128)(2,1)S(1)}, u32[]{:S(2)}, u32[]{:S(2)}) %collective-permute-start.26) | collective-permute-done | bytes 655392 | tf_op jit(solution)/shard_map/ppermute | solution.py:103
  136.9 3.6 %collective-permute-done.25 = bf16[4,752,128]{2,1,0:T(8,128)(2,1)S(1)} collective-permute-done((bf16[4,752,128]{2,1,0:T(8,128)(2,1)S(1)}, bf16[4,752,128]{2,1,0:T(8,128)(2,1)S(1)}, u32[]{:S(2)}, u32[]{:S(2)}) %collective-permute-start.25) | collective-permute-done | bytes 770080 | tf_op jit(solution)/shard_map/ppermute | solution.py:118
  140.6 2.1 %collective-permute-start.32 = (bf16[4,160,128]{2,1,0:T(8,128)(2,1)S(1)}, bf16[4,160,128]{2,1,0:T(8,128)(2,1)S(1)}, u32[]{:S(2)}, u32[]{:S(2)}) collective-permute-start(bf16[4,160,128]{2,1,0:T(8,128)(2,1)S(1)} %get-tuple-element.171), channel_id=1, source_target_pairs={{0,24},{4,28},{8,16},{12,20},{16,8},{20,12},{24,0},{28,4},{1,25},{... | collective-permute-start | bytes 491528 | tf_op jit(solution)/shard_map/ppermute | solution.py:103
  142.8 0.9 collective-permute-start.31
  144.6 3.8 %collective-permute-start.29 = (bf16[752,128]{1,0:T(8,128)(2,1)S(1)}, bf16[752,128]{1,0:T(8,128)(2,1)S(1)}, u32[]{:S(2)}, u32[]{:S(2)}) collective-permute-start(bf16[752,128]{1,0:T(8,128)(2,1)S(1)} %get-tuple-element.168), channel_id=1, source_target_pairs={{0,3},{1,0},{2,1},{3,2},{4,7},{5,4},{6,5},{7,6},{8,11},{9,8},{10,9... | collective-permute-start | bytes 577544 | tf_op jit(solution)/shard_map/ppermute | solution.py:108
  148.4 1.5 collective-permute-done.31
  150.0 3.8 %collective-permute-start.35 = (bf16[160,128]{1,0:T(8,128)(2,1)S(1)}, bf16[160,128]{1,0:T(8,128)(2,1)S(1)}, u32[]{:S(2)}, u32[]{:S(2)}) collective-permute-start(bf16[160,128]{1,0:T(8,128)(2,1)S(1)} %get-tuple-element.177), channel_id=1, source_target_pairs={{0,3},{1,0},{2,1},{3,2},{4,7},{5,4},{6,5},{7,6},{8,11},{9,8},{10,9... | collective-permute-start | bytes 122888 | tf_op jit(solution)/shard_map/ppermute | solution.py:108
  154.2 0.7 collective-permute-done.29
  154.9 9.0 %collective-permute-done.28 = bf16[752,128]{1,0:T(8,128)(2,1)S(1)} collective-permute-done((bf16[752,128]{1,0:T(8,128)(2,1)S(1)}, bf16[752,128]{1,0:T(8,128)(2,1)S(1)}, u32[]{:S(2)}, u32[]{:S(2)}) %collective-permute-start.28) | collective-permute-done | bytes 192544 | tf_op jit(solution)/shard_map/ppermute | solution.py:108
  164.1 0.7 collective-permute-done.34
  164.9 1.5 collective-permute-start.37
  166.4 1.7 collective-permute-start.36
  168.4 5.0 %collective-permute-done.37 = bf16[912,128]{1,0:T(8,128)(2,1)S(1)} collective-permute-done((bf16[912,128]{1,0:T(8,128)(2,1)S(1)}, bf16[912,128]{1,0:T(8,128)(2,1)S(1)}, u32[]{:S(2)}, u32[]{:S(2)}) %collective-permute-start.37) | collective-permute-done | bytes 233504 | tf_op jit(solution)/shard_map/ppermute | solution.py:103
  173.4 3.8 %collective-permute-done.36 = bf16[912,128]{1,0:T(8,128)(2,1)S(1)} collective-permute-done((bf16[912,128]{1,0:T(8,128)(2,1)S(1)}, bf16[912,128]{1,0:T(8,128)(2,1)S(1)}, u32[]{:S(2)}, u32[]{:S(2)}) %collective-permute-start.36) | collective-permute-done | bytes 233504 | tf_op jit(solution)/shard_map/ppermute | solution.py:103
  177.4 2.5 %collective-permute-done.39.refs_2_ = bf16[4,912,128]{2,1,0:T(8,128)(2,1)S(1)} collective-permute-done((bf16[4,912,128]{2,1,0:T(8,128)(2,1)S(1)}, bf16[4,912,128]{2,1,0:T(8,128)(2,1)S(1)}, u32[]{:S(2)}, u32[]{:S(2)}) %collective-permute-start.39) | collective-permute-done | bytes 933920 | tf_op jit(solution)/shard_map/ppermute | solution.py:103
  179.9 2.7 %unpack.1 = (f32[144,1536]{1,0:T(8,128)}, f32[144,1536]{1,0:T(8,128)}, f32[576,384]{1,0:T(8,128)}, f32[144,576]{1,0:T(8,128)}, f32[144,576]{1,0:T(8,128)}, /*ind...) custom-call(s32[4]{0:T(128)S(1)} %copy-done.17, ...), custom_call_target="tpu_custom_call" | custom-call | flops 1 | bytes 1024 | tf_op jit(solution)/shard_map/unpack/pallas_call | solution.py:85
  (122 shorter events, 5.0 us)
Async XLA Ops:
  0.6 3.8 %copy-start.27 = (s32[256]{0:T(256)S(1)}, s32[256]{0:T(256)}, u32[]{:S(2)}) copy-start(s32[256]{0:T(256)} %param.15) | copy-start | bytes 3076
  0.7 3.9 %copy-start.25 = (bf16[144]{0:T(256)(128)(2,1)S(1)}, bf16[144]{0:T(256)(128)(2,1)}, u32[]{:S(2)}) copy-start(bf16[144]{0:T(256)(128)(2,1)} %param.24) | copy-start | bytes 868
  0.7 3.9 %copy-start.23 = (bf16[16]{0:T(256)(128)(2,1)S(1)}, bf16[16]{0:T(256)(128)(2,1)}, u32[]{:S(2)}) copy-start(bf16[16]{0:T(256)(128)(2,1)} %param.19) | copy-start | bytes 100
  0.7 3.9 %copy-start.24 = (bf16[16]{0:T(256)(128)(2,1)S(1)}, bf16[16]{0:T(256)(128)(2,1)}, u32[]{:S(2)}) copy-start(bf16[16]{0:T(256)(128)(2,1)} %param.18) | copy-start | bytes 100
  0.7 3.9 %copy-start.26 = (bf16[144]{0:T(256)(128)(2,1)S(1)}, bf16[144]{0:T(256)(128)(2,1)}, u32[]{:S(2)}) copy-start(bf16[144]{0:T(256)(128)(2,1)} %param.17) | copy-start | bytes 868
  4.5 31.1 %copy-start.22 = (bf16[752,128]{1,0:T(8,128)(2,1)S(1)}, bf16[752,128]{1,0:T(8,128)(2,1)}, u32[]{:S(2)}) copy-start(bf16[752,128]{1,0:T(8,128)(2,1)} %get-tuple-element.91) | copy-start | bytes 577540
  4.6 10.3 %collective-permute-start.13 = (bf16[16,128]{1,0:T(8,128)(2,1)S(1)}, bf16[16,128]{1,0:T(8,128)(2,1)S(1)}, u32[]{:S(2)}, u32[]{:S(2)}) collective-permute-start(bf16[16,128]{1,0:T(8,128)(2,1)S(1)} %get-tuple-element.190), channel_id=1, source_target_pairs={{0,3},{1,0},{2,1},{3,2},{4,7},{5,4},{6,5},{7,6},{8,11},{9,8},{10,9... | collective-permute-start | bytes 12296 | tf_op jit(solution)/shard_map/ppermute | solution.py:108
  9.7 5.2 %collective-permute-start.12 = (bf16[16,128]{1,0:T(8,128)(2,1)S(1)}, bf16[16,128]{1,0:T(8,128)(2,1)S(1)}, u32[]{:S(2)}, u32[]{:S(2)}) collective-permute-start(bf16[16,128]{1,0:T(8,128)(2,1)S(1)} %get-tuple-element.190), channel_id=1, source_target_pairs={{0,2},{1,3},{2,0},{3,1},{4,6},{5,7},{6,4},{7,5},{8,10},{9,11},{10,... | collective-permute-start | bytes 12296 | tf_op jit(solution)/shard_map/ppermute | solution.py:108
  9.7 9.0 %collective-permute-start.11 = (bf16[16,128]{1,0:T(8,128)(2,1)S(1)}, bf16[16,128]{1,0:T(8,128)(2,1)S(1)}, u32[]{:S(2)}, u32[]{:S(2)}) collective-permute-start(bf16[16,128]{1,0:T(8,128)(2,1)S(1)} %get-tuple-element.190), channel_id=1, source_target_pairs={{0,1},{1,2},{2,3},{3,0},{4,5},{5,6},{6,7},{7,4},{8,9},{9,10},{10,1... | collective-permute-start | bytes 12296 | tf_op jit(solution)/shard_map/ppermute | solution.py:108
  10.7 9.5 %collective-permute-start.2 = (bf16[144,128]{1,0:T(8,128)(2,1)}, bf16[144,128]{1,0:T(8,128)(2,1)S(1)}, u32[]{:S(2)}, u32[]{:S(2)}) collective-permute-start(bf16[144,128]{1,0:T(8,128)(2,1)} %get-tuple-element.89), channel_id=1, source_target_pairs={{0,3},{1,0},{2,1},{3,2},{4,7},{5,4},{6,5},{7,6},{8,11},{9,8},{10,9... | collective-permute-start | bytes 110600 | tf_op jit(solution)/shard_map/ppermute | solution.py:108
  13.5 7.4 %collective-permute-start.1 = (bf16[144,128]{1,0:T(8,128)(2,1)}, bf16[144,128]{1,0:T(8,128)(2,1)S(1)}, u32[]{:S(2)}, u32[]{:S(2)}) collective-permute-start(bf16[144,128]{1,0:T(8,128)(2,1)} %get-tuple-element.89), channel_id=1, source_target_pairs={{0,2},{1,3},{2,0},{3,1},{4,6},{5,7},{6,4},{7,5},{8,10},{9,11},{10,... | collective-permute-start | bytes 110600 | tf_op jit(solution)/shard_map/ppermute | solution.py:108
  14.8 6.6 %collective-permute-start = (bf16[144,128]{1,0:T(8,128)(2,1)}, bf16[144,128]{1,0:T(8,128)(2,1)S(1)}, u32[]{:S(2)}, u32[]{:S(2)}) collective-permute-start(bf16[144,128]{1,0:T(8,128)(2,1)} %get-tuple-element.89), channel_id=1, source_target_pairs={{0,1},{1,2},{2,3},{3,0},{4,5},{5,6},{6,7},{7,4},{8,9},{9,10},{10,1... | collective-permute-start | bytes 110600 | tf_op jit(solution)/shard_map/ppermute | solution.py:108
  14.9 19.7 %collective-permute-start.8 = (bf16[752,128]{1,0:T(8,128)(2,1)}, bf16[752,128]{1,0:T(8,128)(2,1)S(1)}, u32[]{:S(2)}, u32[]{:S(2)}) collective-permute-start(bf16[752,128]{1,0:T(8,128)(2,1)} %get-tuple-element.91), channel_id=1, source_target_pairs={{0,3},{1,0},{2,1},{3,2},{4,7},{5,4},{6,5},{7,6},{8,11},{9,8},{10,9... | collective-permute-start | bytes 577544 | tf_op jit(solution)/shard_map/ppermute | solution.py:108
  18.7 16.9 %collective-permute-start.7 = (bf16[752,128]{1,0:T(8,128)(2,1)}, bf16[752,128]{1,0:T(8,128)(2,1)S(1)}, u32[]{:S(2)}, u32[]{:S(2)}) collective-permute-start(bf16[752,128]{1,0:T(8,128)(2,1)} %get-tuple-element.91), channel_id=1, source_target_pairs={{0,2},{1,3},{2,0},{3,1},{4,6},{5,7},{6,4},{7,5},{8,10},{9,11},{10,... | collective-permute-start | bytes 577544 | tf_op jit(solution)/shard_map/ppermute | solution.py:108
  20.2 15.4 %collective-permute-start.6 = (bf16[752,128]{1,0:T(8,128)(2,1)}, bf16[752,128]{1,0:T(8,128)(2,1)S(1)}, u32[]{:S(2)}, u32[]{:S(2)}) collective-permute-start(bf16[752,128]{1,0:T(8,128)(2,1)} %get-tuple-element.91), channel_id=1, source_target_pairs={{0,1},{1,2},{2,3},{3,0},{4,5},{5,6},{6,7},{7,4},{8,9},{9,10},{10,1... | collective-permute-start | bytes 577544 | tf_op jit(solution)/shard_map/ppermute | solution.py:108
  22.2 5.7 %collective-permute-start.4 = (bf16[4,144,128]{2,1,0:T(8,128)(2,1)S(1)}, bf16[4,144,128]{2,1,0:T(8,128)(2,1)S(1)}, u32[]{:S(2)}, u32[]{:S(2)}) collective-permute-start(bf16[4,144,128]{2,1,0:T(8,128)(2,1)S(1)} %get-tuple-element.182), channel_id=1, source_target_pairs={{0,8},{4,12},{8,0},{12,4},{16,24},{20,28},{24,16},{28,20},{1,9},{5... | collective-permute-start | bytes 442376 | tf_op jit(solution)/shard_map/ppermute | solution.py:103
  23.8 7.7 %collective-permute-start.3 = (bf16[4,144,128]{2,1,0:T(8,128)(2,1)S(1)}, bf16[4,144,128]{2,1,0:T(8,128)(2,1)S(1)}, u32[]{:S(2)}, u32[]{:S(2)}) collective-permute-start(bf16[4,144,128]{2,1,0:T(8,128)(2,1)S(1)} %get-tuple-element.182), channel_id=1, source_target_pairs={{0,16},{4,20},{8,24},{12,28},{16,0},{20,4},{24,8},{28,12},{1,17},{... | collective-permute-start | bytes 442376 | tf_op jit(solution)/shard_map/ppermute | solution.py:103
  28.0 6.6 %collective-permute-start.5 = (bf16[4,144,128]{2,1,0:T(8,128)(2,1)S(1)}, bf16[4,144,128]{2,1,0:T(8,128)(2,1)S(1)}, u32[]{:S(2)}, u32[]{:S(2)}) collective-permute-start(bf16[4,144,128]{2,1,0:T(8,128)(2,1)S(1)} %get-tuple-element.182), channel_id=1, source_target_pairs={{0,24},{4,28},{8,16},{12,20},{16,8},{20,12},{24,0},{28,4},{1,25},{... | collective-permute-start | bytes 442376 | tf_op jit(solution)/shard_map/ppermute | solution.py:103
  34.6 7.5 %copy-start.1 = (bf16[256,576]{0,1:T(8,128)(2,1)S(1)}, bf16[256,576]{0,1:T(8,128)(2,1)}, u32[]{:S(2)}) copy-start(bf16[256,576]{0,1:T(8,128)(2,1)} %param.14) | copy-start | bytes 884740
  34.6 7.5 %copy-start.16 = (s32[4]{0:T(128)S(1)}, s32[4]{0:T(128)}, u32[]{:S(2)}) copy-start(s32[4]{0:T(128)} %pad_add_fusion.1.refs_0_) | copy-start | bytes 52
  36.9 18.2 %collective-permute-start.9 = (bf16[4,752,128]{2,1,0:T(8,128)(2,1)}, bf16[4,752,128]{2,1,0:T(8,128)(2,1)}, u32[]{:S(2)}, u32[]{:S(2)}) collective-permute-start(bf16[4,752,128]{2,1,0:T(8,128)(2,1)} %get-tuple-element.175), channel_id=1, source_target_pairs={{0,16},{4,12},{8,24},{12,4},{16,0},{20,28},{24,8},{28,20},{1,17},{... | collective-permute-start | bytes 2310152 | tf_op jit(solution)/shard_map/ppermute | solution.py:118
  39.9 15.1 %copy-start.19 = (bf16[1,4,752,128]{3,2,1,0:T(8,128)(2,1)S(1)}, bf16[1,4,752,128]{3,2,1,0:T(8,128)(2,1)}, u32[]{:S(2)}) copy-start(bf16[1,4,752,128]{3,2,1,0:T(8,128)(2,1)} %get-tuple-element.174) | copy-start | bytes 2310148
  40.0 2.1 %collective-permute-start.14 = (bf16[4,4,144,128]{3,2,1,0:T(8,128)(2,1)S(1)}, bf16[4,4,144,128]{3,2,1,0:T(8,128)(2,1)S(1)}, u32[]{:S(2)}, u32[]{:S(2)}) collective-permute-start(bf16[4,4,144,128]{3,2,1,0:T(8,128)(2,1)S(1)} %pad_maximum_fusion.3.refs_1_), channel_id=1, source_target_pairs={{0,4},{4,0},{8,12},{12,8},{16,20},{20,16},{24,28},{28,24},{1,5},{5... | collective-permute-start | bytes 1769480 | tf_op jit(solution)/shard_map/ppermute | solution.py:103
  47.2 10.4 %copy-start.3 = (bf16[256,576]{1,0:T(8,128)(2,1)}, bf16[256,576]{1,0:T(8,128)(2,1)S(1)}, u32[]{:S(2)}) copy-start(bf16[256,576]{1,0:T(8,128)(2,1)S(1)} %get-tuple-element.102.refs_0_) | copy-start | bytes 884740
  47.2 10.4 %copy-start.5 = (bf16[256,384]{1,0:T(8,128)(2,1)}, bf16[256,384]{1,0:T(8,128)(2,1)S(1)}, u32[]{:S(2)}) copy-start(bf16[256,384]{1,0:T(8,128)(2,1)S(1)} %get-tuple-element.106.refs_3_) | copy-start | bytes 589828
  47.2 11.9 %collective-permute-start.17 = (bf16[256,384]{1,0:T(8,128)(2,1)S(1)}, bf16[256,384]{1,0:T(8,128)(2,1)S(1)}, u32[]{:S(2)}, u32[]{:S(2)}) collective-permute-start(bf16[256,384]{1,0:T(8,128)(2,1)S(1)} %get-tuple-element.106.refs_3_), channel_id=1, source_target_pairs={{0,3},{4,7},{8,11},{12,15},{16,19},{20,23},{24,27},{28,31}} | collective-permute-start | bytes 589832 | tf_op jit(solution)/shard_map/ppermute | solution.py:900
  50.5 9.5 %collective-permute-start.16 = (bf16[256,384]{1,0:T(8,128)(2,1)S(1)}, bf16[256,384]{1,0:T(8,128)(2,1)S(1)}, u32[]{:S(2)}, u32[]{:S(2)}) collective-permute-start(bf16[256,384]{1,0:T(8,128)(2,1)S(1)} %get-tuple-element.106.refs_3_), channel_id=1, source_target_pairs={{0,2},{1,3},{4,6},{5,7},{8,10},{9,11},{12,14},{13,15},{16,18},{17,... | collective-permute-start | bytes 589832 | tf_op jit(solution)/shard_map/ppermute | solution.py:900
  53.5 9.8 %collective-permute-start.15 = (bf16[256,384]{1,0:T(8,128)(2,1)S(1)}, bf16[256,384]{1,0:T(8,128)(2,1)S(1)}, u32[]{:S(2)}, u32[]{:S(2)}) collective-permute-start(bf16[256,384]{1,0:T(8,128)(2,1)S(1)} %get-tuple-element.106.refs_3_), channel_id=1, source_target_pairs={{0,1},{1,2},{2,3},{4,5},{5,6},{6,7},{8,9},{9,10},{10,11},{12,13},{... | collective-permute-start | bytes 589832 | tf_op jit(solution)/shard_map/ppermute | solution.py:900
  57.6 20.4 %collective-permute-start.10 = (bf16[2,4,752,128]{3,2,1,0:T(8,128)(2,1)}, bf16[2,4,752,128]{3,2,1,0:T(8,128)(2,1)}, u32[]{:S(2)}, u32[]{:S(2)}) collective-permute-start(bf16[2,4,752,128]{3,2,1,0:T(8,128)(2,1)} %pad_maximum_fusion.refs_5_), channel_id=1, source_target_pairs={{0,8},{4,20},{8,0},{12,28},{16,24},{20,4},{24,16},{28,12},{1,9},{5... | collective-permute-start | bytes 4620296 | tf_op jit(solution)/shard_map/ppermute | solution.py:118
  59.1 5.1 %copy-start.7 = (bf16[256,384]{1,0:T(8,128)(2,1)}, bf16[256,384]{1,0:T(8,128)(2,1)S(1)}, u32[]{:S(2)}) copy-start(bf16[256,384]{1,0:T(8,128)(2,1)S(1)} %collective-permute-done.17.refs_6_) | copy-start | bytes 589828
  60.0 4.2 %copy-start.9 = (bf16[256,384]{1,0:T(8,128)(2,1)}, bf16[256,384]{1,0:T(8,128)(2,1)S(1)}, u32[]{:S(2)}) copy-start(bf16[256,384]{1,0:T(8,128)(2,1)S(1)} %collective-permute-done.16.refs_5_) | copy-start | bytes 589828
  63.4 14.6 %collective-permute-start.18 = (bf16[2,4,752,128]{3,2,1,0:T(8,128)(2,1)}, bf16[2,4,752,128]{3,2,1,0:T(8,128)(2,1)}, u32[]{:S(2)}, u32[]{:S(2)}) collective-permute-start(bf16[2,4,752,128]{3,2,1,0:T(8,128)(2,1)} %pad_maximum_fusion.refs_5_), channel_id=1, source_target_pairs={{0,4},{4,0},{8,12},{12,8},{16,20},{20,16},{24,28},{28,24},{1,5},{5... | collective-permute-start | bytes 4620296 | tf_op jit(solution)/shard_map/ppermute | solution.py:103
  77.9 3.6 %collective-permute-start.19 = (bf16[2,4,752,128]{3,2,1,0:T(8,128)(2,1)}, bf16[2,4,752,128]{3,2,1,0:T(8,128)(2,1)S(1)}, u32[]{:S(2)}, u32[]{:S(2)}) collective-permute-start(bf16[2,4,752,128]{3,2,1,0:T(8,128)(2,1)} %collective-permute-done.10.refs_6_), channel_id=1, source_target_pairs={{0,4},{4,0},{8,12},{12,8},{16,20},{20,16},{24,28},{28,24},{1,5},{5... | collective-permute-start | bytes 4620296 | tf_op jit(solution)/shard_map/ppermute | solution.py:103
  82.7 13.3 %copy-start.4 = (bf16[256,576]{1,0:T(8,128)(2,1)S(1)}, bf16[256,576]{1,0:T(8,128)(2,1)}, u32[]{:S(2)}) copy-start(bf16[256,576]{1,0:T(8,128)(2,1)} %copy-done.3) | copy-start | bytes 884740
  82.7 13.3 %copy-start.6 = (bf16[256,384]{1,0:T(8,128)(2,1)S(1)}, bf16[256,384]{1,0:T(8,128)(2,1)}, u32[]{:S(2)}) copy-start(bf16[256,384]{1,0:T(8,128)(2,1)} %copy-done.5) | copy-start | bytes 589828
  82.7 13.3 %copy-start.8 = (bf16[256,384]{1,0:T(8,128)(2,1)S(1)}, bf16[256,384]{1,0:T(8,128)(2,1)}, u32[]{:S(2)}) copy-start(bf16[256,384]{1,0:T(8,128)(2,1)} %copy-done.7) | copy-start | bytes 589828
  82.7 13.3 %copy-start.10 = (bf16[256,384]{1,0:T(8,128)(2,1)S(1)}, bf16[256,384]{1,0:T(8,128)(2,1)}, u32[]{:S(2)}) copy-start(bf16[256,384]{1,0:T(8,128)(2,1)} %copy-done.9) | copy-start | bytes 589828
  82.7 13.3 %copy-start.12 = (bf16[256,384]{1,0:T(8,128)(2,1)S(1)}, bf16[256,384]{1,0:T(8,128)(2,1)}, u32[]{:S(2)}) copy-start(bf16[256,384]{1,0:T(8,128)(2,1)} %copy-done.11) | copy-start | bytes 589828
  82.7 13.3 %copy-start.14 = (f32[256,576]{1,0:T(8,128)S(1)}, f32[256,576]{1,0:T(8,128)}, u32[]{:S(2)}) copy-start(f32[256,576]{1,0:T(8,128)} %get-tuple-element.120.refs_2_) | copy-start | bytes 1769476
  95.8 9.9 %collective-permute-start.20 = (bf16[2,2,4,752,128]{4,3,2,1,0:T(8,128)(2,1)}, bf16[2,2,4,752,128]{4,3,2,1,0:T(8,128)(2,1)S(1)}, u32[]{:S(2)}, u32[]{:S(2)}) collective-permute-start(bf16[2,2,4,752,128]{4,3,2,1,0:T(8,128)(2,1)} %get-tuple-element.118), channel_id=1, source_target_pairs={{0,4},{4,0},{8,12},{12,8},{16,20},{20,16},{24,28},{28,24},{1,5},{5... | collective-permute-start | bytes 9240584 | tf_op jit(solution)/shard_map/ppermute | solution.py:103
  96.0 2.3 %copy-start = (bf16[9,256,1024]{2,1,0:T(8,128)(2,1)S(1)}, bf16[9,256,1024]{2,1,0:T(8,128)(2,1)}, u32[]{:S(2)}) copy-start(bf16[9,256,1024]{2,1,0:T(8,128)(2,1)} %get-tuple-element.121.refs_7_) | copy-start | bytes 14155780
  99.3 6.4 %copy-start.20 = (bf16[2,2,4,752,128]{4,3,2,1,0:T(8,128)(2,1)S(1)}, bf16[2,2,4,752,128]{4,3,2,1,0:T(8,128)(2,1)}, u32[]{:S(2)}) copy-start(bf16[2,2,4,752,128]{4,3,2,1,0:T(8,128)(2,1)} %get-tuple-element.117) | copy-start | bytes 9240580
  106.1 22.1 %collective-permute-start.21 = (bf16[2,4,752,128]{3,2,1,0:T(8,128)(2,1)S(1)}, bf16[2,4,752,128]{3,2,1,0:T(8,128)(2,1)S(1)}, u32[]{:S(2)}, u32[]{:S(2)}) collective-permute-start(bf16[2,4,752,128]{3,2,1,0:T(8,128)(2,1)S(1)} %fusion), channel_id=1, source_target_pairs={{0,8},{4,20},{8,0},{12,28},{16,24},{20,4},{24,16},{28,12},{1,9},{5... | collective-permute-start | bytes 4620296 | tf_op jit(solution)/shard_map/ppermute | solution.py:118
  107.7 9.1 %collective-permute-start.22 = (bf16[256,384]{1,0:T(8,128)(2,1)S(1)}, bf16[256,384]{1,0:T(8,128)(2,1)S(1)}, u32[]{:S(2)}, u32[]{:S(2)}) collective-permute-start(bf16[256,384]{1,0:T(8,128)(2,1)S(1)} %get-tuple-element.129), channel_id=1, source_target_pairs={{1,0},{2,1},{3,2},{5,4},{6,5},{7,6},{9,8},{10,9},{11,10},{13,12},{... | collective-permute-start | bytes 589832 | tf_op jit(solution)/shard_map/ppermute | solution.py:917
  109.0 19.2 %collective-permute-start.23 = (bf16[256,384]{1,0:T(8,128)(2,1)S(1)}, bf16[256,384]{1,0:T(8,128)(2,1)S(1)}, u32[]{:S(2)}, u32[]{:S(2)}) collective-permute-start(bf16[256,384]{1,0:T(8,128)(2,1)S(1)} %get-tuple-element.130), channel_id=1, source_target_pairs={{2,0},{3,1},{6,4},{7,5},{10,8},{11,9},{14,12},{15,13},{18,16},{19,... | collective-permute-start | bytes 589832 | tf_op jit(solution)/shard_map/ppermute | solution.py:917
  110.3 17.9 %collective-permute-start.24 = (bf16[256,384]{1,0:T(8,128)(2,1)S(1)}, bf16[256,384]{1,0:T(8,128)(2,1)S(1)}, u32[]{:S(2)}, u32[]{:S(2)}) collective-permute-start(bf16[256,384]{1,0:T(8,128)(2,1)S(1)} %get-tuple-element.131), channel_id=1, source_target_pairs={{3,0},{7,4},{11,8},{15,12},{19,16},{23,20},{27,24},{31,28}} | collective-permute-start | bytes 589832 | tf_op jit(solution)/shard_map/ppermute | solution.py:917
  128.2 1.9 %copy-start.2 = (bf16[256,576]{0,1:T(8,128)(2,1)S(1)}, bf16[256,576]{0,1:T(8,128)(2,1)}, u32[]{:S(2)}) copy-start(bf16[256,576]{0,1:T(8,128)(2,1)} %param.14) | copy-start | bytes 884740
  128.2 1.9 %copy-start.13 = (f32[256,576]{1,0:T(8,128)S(1)}, f32[256,576]{1,0:T(8,128)}, u32[]{:S(2)}) copy-start(f32[256,576]{1,0:T(8,128)} %get-tuple-element.142.refs_7_) | copy-start | bytes 1769476
  128.3 1.9 %copy-start.17 = (s32[4]{0:T(128)S(1)}, s32[4]{0:T(128)}, u32[]{:S(2)}) copy-start(s32[4]{0:T(128)} %pad_add_fusion.1.refs_0_) | copy-start | bytes 52
  128.6 11.9 %collective-permute-start.25 = (bf16[4,752,128]{2,1,0:T(8,128)(2,1)S(1)}, bf16[4,752,128]{2,1,0:T(8,128)(2,1)S(1)}, u32[]{:S(2)}, u32[]{:S(2)}) collective-permute-start(bf16[4,752,128]{2,1,0:T(8,128)(2,1)S(1)} %fusion.1), channel_id=1, source_target_pairs={{0,16},{4,12},{8,24},{12,4},{16,0},{20,28},{24,8},{28,20},{1,17},{... | collective-permute-start | bytes 2310152 | tf_op jit(solution)/shard_map/ppermute | solution.py:118
  134.7 2.2 %collective-permute-start.26 = (bf16[4,4,160,128]{3,2,1,0:T(8,128)(2,1)S(1)}, bf16[4,4,160,128]{3,2,1,0:T(8,128)(2,1)S(1)}, u32[]{:S(2)}, u32[]{:S(2)}) collective-permute-start(bf16[4,4,160,128]{3,2,1,0:T(8,128)(2,1)S(1)} %get-tuple-element.150), channel_id=1, source_target_pairs={{0,4},{4,0},{8,12},{12,8},{16,20},{20,16},{24,28},{28,24},{1,5},{5... | collective-permute-start | bytes 1966088 | tf_op jit(solution)/shard_map/ppermute | solution.py:103
  140.6 7.8 %collective-permute-start.32 = (bf16[4,160,128]{2,1,0:T(8,128)(2,1)S(1)}, bf16[4,160,128]{2,1,0:T(8,128)(2,1)S(1)}, u32[]{:S(2)}, u32[]{:S(2)}) collective-permute-start(bf16[4,160,128]{2,1,0:T(8,128)(2,1)S(1)} %get-tuple-element.171), channel_id=1, source_target_pairs={{0,24},{4,28},{8,16},{12,20},{16,8},{20,12},{24,0},{28,4},{1,25},{... | collective-permute-start | bytes 491528 | tf_op jit(solution)/shard_map/ppermute | solution.py:103
  142.8 7.1 %collective-permute-start.31 = (bf16[4,160,128]{2,1,0:T(8,128)(2,1)S(1)}, bf16[4,160,128]{2,1,0:T(8,128)(2,1)S(1)}, u32[]{:S(2)}, u32[]{:S(2)}) collective-permute-start(bf16[4,160,128]{2,1,0:T(8,128)(2,1)S(1)} %get-tuple-element.172), channel_id=1, source_target_pairs={{0,16},{4,20},{8,24},{12,28},{16,0},{20,4},{24,8},{28,12},{1,17},{... | collective-permute-start | bytes 491528 | tf_op jit(solution)/shard_map/ppermute | solution.py:103
  143.7 6.2 %collective-permute-start.30 = (bf16[4,160,128]{2,1,0:T(8,128)(2,1)S(1)}, bf16[4,160,128]{2,1,0:T(8,128)(2,1)S(1)}, u32[]{:S(2)}, u32[]{:S(2)}) collective-permute-start(bf16[4,160,128]{2,1,0:T(8,128)(2,1)S(1)} %get-tuple-element.173), channel_id=1, source_target_pairs={{0,8},{4,12},{8,0},{12,4},{16,24},{20,28},{24,16},{28,20},{1,9},{5... | collective-permute-start | bytes 491528 | tf_op jit(solution)/shard_map/ppermute | solution.py:103
  144.5 9.7 %collective-permute-start.27 = (bf16[752,128]{1,0:T(8,128)(2,1)S(1)}, bf16[752,128]{1,0:T(8,128)(2,1)S(1)}, u32[]{:S(2)}, u32[]{:S(2)}) collective-permute-start(bf16[752,128]{1,0:T(8,128)(2,1)S(1)} %get-tuple-element.167), channel_id=1, source_target_pairs={{0,1},{1,2},{2,3},{3,0},{4,5},{5,6},{6,7},{7,4},{8,9},{9,10},{10,1... | collective-permute-start | bytes 577544 | tf_op jit(solution)/shard_map/ppermute | solution.py:108
  144.6 10.3 %collective-permute-start.29 = (bf16[752,128]{1,0:T(8,128)(2,1)S(1)}, bf16[752,128]{1,0:T(8,128)(2,1)S(1)}, u32[]{:S(2)}, u32[]{:S(2)}) collective-permute-start(bf16[752,128]{1,0:T(8,128)(2,1)S(1)} %get-tuple-element.168), channel_id=1, source_target_pairs={{0,3},{1,0},{2,1},{3,2},{4,7},{5,4},{6,5},{7,6},{8,11},{9,8},{10,9... | collective-permute-start | bytes 577544 | tf_op jit(solution)/shard_map/ppermute | solution.py:108
  148.4 15.5 %collective-permute-start.28 = (bf16[752,128]{1,0:T(8,128)(2,1)S(1)}, bf16[752,128]{1,0:T(8,128)(2,1)S(1)}, u32[]{:S(2)}, u32[]{:S(2)}) collective-permute-start(bf16[752,128]{1,0:T(8,128)(2,1)S(1)} %get-tuple-element.169), channel_id=1, source_target_pairs={{0,2},{1,3},{2,0},{3,1},{4,6},{5,7},{6,4},{7,5},{8,10},{9,11},{10,... | collective-permute-start | bytes 577544 | tf_op jit(solution)/shard_map/ppermute | solution.py:108
  150.0 14.2 %collective-permute-start.33 = (bf16[160,128]{1,0:T(8,128)(2,1)S(1)}, bf16[160,128]{1,0:T(8,128)(2,1)S(1)}, u32[]{:S(2)}, u32[]{:S(2)}) collective-permute-start(bf16[160,128]{1,0:T(8,128)(2,1)S(1)} %get-tuple-element.176), channel_id=1, source_target_pairs={{0,1},{1,2},{2,3},{3,0},{4,5},{5,6},{6,7},{7,4},{8,9},{9,10},{10,1... | collective-permute-start | bytes 122888 | tf_op jit(solution)/shard_map/ppermute | solution.py:108
  150.0 14.1 %collective-permute-start.35 = (bf16[160,128]{1,0:T(8,128)(2,1)S(1)}, bf16[160,128]{1,0:T(8,128)(2,1)S(1)}, u32[]{:S(2)}, u32[]{:S(2)}) collective-permute-start(bf16[160,128]{1,0:T(8,128)(2,1)S(1)} %get-tuple-element.177), channel_id=1, source_target_pairs={{0,3},{1,0},{2,1},{3,2},{4,7},{5,4},{6,5},{7,6},{8,11},{9,8},{10,9... | collective-permute-start | bytes 122888 | tf_op jit(solution)/shard_map/ppermute | solution.py:108
  154.2 10.6 %collective-permute-start.34 = (bf16[160,128]{1,0:T(8,128)(2,1)S(1)}, bf16[160,128]{1,0:T(8,128)(2,1)S(1)}, u32[]{:S(2)}, u32[]{:S(2)}) collective-permute-start(bf16[160,128]{1,0:T(8,128)(2,1)S(1)} %get-tuple-element.178), channel_id=1, source_target_pairs={{0,2},{1,3},{2,0},{3,1},{4,6},{5,7},{6,4},{7,5},{8,10},{9,11},{10,... | collective-permute-start | bytes 122888 | tf_op jit(solution)/shard_map/ppermute | solution.py:108
  164.9 8.5 %collective-permute-start.37 = (bf16[912,128]{1,0:T(8,128)(2,1)S(1)}, bf16[912,128]{1,0:T(8,128)(2,1)S(1)}, u32[]{:S(2)}, u32[]{:S(2)}) collective-permute-start(bf16[912,128]{1,0:T(8,128)(2,1)S(1)} %get-tuple-element.180), channel_id=1, source_target_pairs={{0,8},{4,12},{8,0},{12,4},{16,24},{20,28},{24,16},{28,20},{1,9},{5... | collective-permute-start | bytes 700424 | tf_op jit(solution)/shard_map/ppermute | solution.py:103
  166.4 10.8 %collective-permute-start.36 = (bf16[912,128]{1,0:T(8,128)(2,1)S(1)}, bf16[912,128]{1,0:T(8,128)(2,1)S(1)}, u32[]{:S(2)}, u32[]{:S(2)}) collective-permute-start(bf16[912,128]{1,0:T(8,128)(2,1)S(1)} %get-tuple-element.180), channel_id=1, source_target_pairs={{0,16},{4,20},{8,24},{12,28},{16,0},{20,4},{24,8},{28,12},{1,17},{... | collective-permute-start | bytes 700424 | tf_op jit(solution)/shard_map/ppermute | solution.py:103
  168.1 9.1 %collective-permute-start.38 = (bf16[912,128]{1,0:T(8,128)(2,1)S(1)}, bf16[912,128]{1,0:T(8,128)(2,1)S(1)}, u32[]{:S(2)}, u32[]{:S(2)}) collective-permute-start(bf16[912,128]{1,0:T(8,128)(2,1)S(1)} %get-tuple-element.180), channel_id=1, source_target_pairs={{0,24},{4,28},{8,16},{12,20},{16,8},{20,12},{24,0},{28,4},{1,25},{... | collective-permute-start | bytes 700424 | tf_op jit(solution)/shard_map/ppermute | solution.py:103
  177.3 2.6 %collective-permute-start.39 = (bf16[4,912,128]{2,1,0:T(8,128)(2,1)S(1)}, bf16[4,912,128]{2,1,0:T(8,128)(2,1)S(1)}, u32[]{:S(2)}, u32[]{:S(2)}) collective-permute-start(bf16[4,912,128]{2,1,0:T(8,128)(2,1)S(1)} %pad_maximum_fusion.1.refs_1_), channel_id=1, source_target_pairs={{0,4},{4,0},{8,12},{12,8},{16,20},{20,16},{24,28},{28,24},{1,5},{5... | collective-permute-start | bytes 2801672 | tf_op jit(solution)/shard_map/ppermute | solution.py:103
  (4 other events, 4.8 us)
